TPU v7x, 128 devices: a whole 4x4x4 slice. The times are simulated.
128 devices in a mesh: ka: 16 (over z_lo, x, core), ga: 8 (over y, z_hi).
Axes of the slice: x: 4, y: 4, z: 4 (z_hi: 2, z_lo: 2; z = z_hi * 2 + z_lo), core: 2. Of those that a mesh axis runs over, the one named last changes fastest.
Arguments:
- diag_waves: float32 [16, 8, 2, 4096], P('ka'), may hold values from -6 to 6
- band_waves: float32 [16, 72, 2, 4096], P('ka', 'ga'), may hold values from -6 to 6
- screening: float32 [2, 2, 4096, 4096], P(None, None, 'ga', 'ka'), may hold values from -0.09375 to 0.09375
- partner_map: int32 [2, 16], replicated, may hold values from 0 to 15, as said below
- grid_index: int32 [4096], replicated, may hold values from 0 to 4095, each once
Outputs:
- self_energy: float32 [2, 16, 8], P(None, 'ka')
Inputs may be any that keep to these rules, and one draw needn't show every extreme that they name: For each q-step q there is one shift s_q: partner_map[q, k] lies in the block of 1 consecutive k-points with block number (k - s_q) mod (16), and partner_map[q] is a permutation of the k-points; one q-step has s_q = 1 and the other s_q = 8, in either order. `grid_index`: a permutation of the flattened grid points g1 * 64 + g2.
All inputs are finite; a program needn't handle non-finite values.
Results may differ from a plain program's by a relative error of at most 0.0056.
Values may be sent and summed in bfloat16 or wider, within the bound.
No kernel may reach another device: no remote copies, remote signals or barrier semaphores. Data moves between devices by JAX's collectives and lax.ppermute only.
A program may use at most 256 MiB of HBM per device.

v0:
```python
import math

import jax
import jax.numpy as jnp
from jax import lax
from jax.sharding import PartitionSpec as P

N1 = 64
N2 = 64
NG = 4096
MB = 72
QSTEPS = 2


def dft_tables(length):
    places = jnp.arange(length, dtype=jnp.int32)
    phase = places[:, None] * places[None, :] % length
    angle = phase.astype(jnp.float32) * (2.0 * math.pi / length)
    return (jnp.cos(angle), jnp.sin(angle))


def pair_elements(diag_block, partner_rows, grid_index):
    kcount = diag_block.shape[0]
    bands = diag_block.shape[1]
    points = diag_block.shape[3]
    mcount = partner_rows.shape[1]
    row_total = kcount * bands * mcount
    cos_two, sin_two = dft_tables(N2)
    table_two = jnp.concatenate(
        [jnp.concatenate([cos_two, -sin_two], 1), jnp.concatenate([sin_two, cos_two], 1)], 0
    )
    cos_one, sin_one = dft_tables(N1)
    table_one = jnp.stack([jnp.stack([cos_one, -sin_one]), jnp.stack([sin_one, cos_one])])
    factor = 1.0 / math.sqrt(points)
    diag_re = diag_block[:, :, 0][:, :, None, :]
    diag_im = diag_block[:, :, 1][:, :, None, :]
    band_re = partner_rows[:, :, 0][:, None, :, :]
    band_im = partner_rows[:, :, 1][:, None, :, :]
    rho_re = diag_re * band_re + diag_im * band_im
    rho_im = diag_re * band_im - diag_im * band_re
    field = jnp.concatenate(
        [rho_re.reshape(row_total, N1, N2), rho_im.reshape(row_total, N1, N2)], 2
    )
    half_done = jnp.dot(
        field.reshape(row_total * N1, 2 * N2),
        table_two,
        precision=lax.Precision.HIGHEST,
        preferred_element_type=jnp.float32,
    )
    half_done = half_done.reshape(row_total, N1, 2, N2)
    spectrum = jnp.einsum(
        "prbz,barg->apgz",
        half_done,
        table_one,
        precision=lax.Precision.HIGHEST,
        preferred_element_type=jnp.float32,
    )
    flat_grid = spectrum.reshape(2, row_total, points) * factor
    picked = jnp.take(flat_grid, grid_index, axis=2).astype(jnp.bfloat16)
    return picked.reshape(2, kcount, bands, mcount, grid_index.shape[0])


def body(diag_waves, band_waves, screening, partner_map, grid_index):
    kcount = diag_waves.shape[0]
    bands = diag_waves.shape[1]
    kbase = lax.axis_index("ka") * kcount
    g_local = screening.shape[2]
    g_first = lax.axis_index("ga") * g_local
    dims = (((1,), (1,)), ((), ()))
    partial_value = jnp.zeros((2, kcount, bands), jnp.float32)
    for qstep in range(QSTEPS):
        wanted = lax.dynamic_slice_in_dim(partner_map[qstep], kbase, kcount)
        piece = lax.all_gather(band_waves, "ka", axis=0, tiled=True)
        start = jnp.int32(0)
        inside = (wanted >= start) & (wanted < start + piece.shape[0])
        offset = jnp.clip(wanted, 0, piece.shape[0] - 1)
        chosen = jnp.take(piece, offset, axis=0)
        partner_rows = jnp.where(inside[:, None, None, None], chosen, jnp.zeros_like(band_waves))
        local_pairs = pair_elements(diag_waves, partner_rows, grid_index)
        pairs = lax.all_gather(local_pairs, "ga", axis=3, tiled=True)
        row_count = kcount * bands * pairs.shape[3]
        pair_re = pairs[0].reshape(row_count, pairs.shape[4])
        pair_im = pairs[1].reshape(row_count, pairs.shape[4])
        screen_half = screening[qstep].astype(jnp.bfloat16)
        contract_piece = lax.all_gather(screen_half, "ka", axis=2, tiled=True)
        real_real = lax.dot_general(
            pair_re, contract_piece[0], dims, preferred_element_type=jnp.float32
        )
        imag_imag = lax.dot_general(
            pair_im, contract_piece[1], dims, preferred_element_type=jnp.float32
        )
        real_imag = lax.dot_general(
            pair_re, contract_piece[1], dims, preferred_element_type=jnp.float32
        )
        imag_real = lax.dot_general(
            pair_im, contract_piece[0], dims, preferred_element_type=jnp.float32
        )
        image_re = real_real - imag_imag
        image_im = real_imag + imag_real
        own_re = lax.dynamic_slice_in_dim(pair_re, g_first, g_local, 1).astype(jnp.float32)
        own_im = lax.dynamic_slice_in_dim(pair_im, g_first, g_local, 1).astype(jnp.float32)
        sum_re = jnp.sum((own_re * image_re + own_im * image_im).reshape(kcount, bands, -1), axis=2)
        sum_im = jnp.sum((own_re * image_im - own_im * image_re).reshape(kcount, bands, -1), axis=2)
        partial_value = partial_value + jnp.stack([sum_re, sum_im])
    total = lax.psum(partial_value, "ga")
    return total * (-1.0 / (QSTEPS * MB * math.sqrt(NG)))


def solution(mesh):
    in_specs = (
        P("ka", None, None, None),
        P("ka", "ga", None, None),
        P(None, None, "ga", "ka"),
        P(),
        P(),
    )
    out_specs = P(None, "ka", None)
    return jax.shard_map(body, mesh=mesh, in_specs=in_specs, out_specs=out_specs, check_vma=False)
```

profile of v0, /device:TPU:1, one launch (start us, length us, event | category | flops | bytes accessed | tf_op | source)
XLA Modules:
  0.0 583.7 jit_solution(9293624389670982020)
XLA Ops:
  6.5 0.7 all-gather.8.cloned.1.call-update
  7.3 0.8 fusion.65
  8.1 0.7 fusion.66
  12.6 0.1 fusion.55
  12.8 0.1 fusion.54
  12.9 0.1 fusion.50
  13.1 0.1 fusion.52
  13.4 1.3 compare_and_fusion
  14.7 0.7 fusion.56
  15.4 1.3 fusion.64
  16.7 0.2 copy_bitcast_fusion
  16.9 34.2 %all-gather.8.cloned.1.call-done = f32[16,9,2,4096]{3,2,1,0:T(2,128)} async-done(((f32[1,9,2,4096]{3,2,1,0:T(2,128)}), f32[16,9,2,4096]{3,2,1,0:T(2,128)}) %all-gather.8.cloned.1.call-update) | async-done | bytes 4718608 | tf_op jit(solution)/shard_map/all_gather | solution.py:73
  51.1 1.1 constant_dynamic-slice_fusion
  52.2 0.2 fusion.37
  52.5 0.2 fusion.36
  52.8 3.8 multiply_add_fusion
  56.6 2.2 add.110
  58.8 3.2 sub.35
  62.0 7.7 %fusion.14 = f32[72,64,2,64]{3,1,2,0:T(8,128)} fusion(f32[2,64,128,1]{2,1,0,3:T(8,128)S(1)} %bitcast.143, f32[72,64,64]{2,1,0:T(8,128)} %sub.35, f32[72,64,64]{2,1,0:T(8,128)S(1)} %add.110), kind=kOutput, calls=%fused_computation.23 | convolution fusion | flops 906559488 | bytes 4784128 | tf_op jit(solution)/shard_map/dot_general | solution.py:44
  69.7 7.5 %copy.59 = f32[72,64,2,64]{0,1,2,3:T(8,128)} copy(f32[72,64,2,64]{3,1,2,0:T(8,128)} %fusion.14) | data formatting | bytes 4718592 | tf_op jit(solution)/shard_map/dot_general | solution.py:44
  77.2 6.4 %fusion.3 = bf16[2,72,64,64]{1,2,3,0:T(8,128)(2,1)S(1)} fusion(f32[72,64,2,64]{0,1,2,3:T(8,128)} %copy.59, f32[1,2,64,64]{2,3,0,1:T(8,128)S(1)} %get-tuple-element.43, f32[1,2,64,64]{2,3,0,1:T(8,128)S(1)} %get-tuple-element.42), kind=kOutput, calls=%fused_computation.11 | convolution fusion | flops 907165696 | bytes 3604480 | tf_op jit(solution)/shard_map/prbz,barg->apgz/dot_general | solution.py:51
  83.6 2.2 copy.75
  85.8 26.9 %gather_fusion = bf16[4096,2,72]{2,1,0:T(2,128)(2,1)} fusion(bf16[2,72,4096]{1,0,2:T(2,128)(2,1)S(1)} %bitcast.126, s32[4096]{0:T(1024)S(1)} %fusion.56), kind=kCustom, calls=%fused_computation.clone | custom fusion | bytes 2375680 | tf_op jit(solution)/shard_map/jit(_take)/gather | solution.py:59
  112.7 4.8 copy.62
  117.5 2.2 add.116
  119.7 3.2 sub.39
  122.9 7.7 %fusion.17 = f32[72,64,2,64]{3,1,2,0:T(8,128)} fusion(f32[2,64,128,1]{2,1,0,3:T(8,128)} %bitcast.144, f32[72,64,64]{2,1,0:T(8,128)} %sub.39, f32[72,64,64]{2,1,0:T(8,128)S(1)} %add.116), kind=kOutput, calls=%fused_computation.27 | convolution fusion | flops 906559488 | bytes 4784128 | tf_op jit(solution)/shard_map/dot_general | solution.py:44
  130.6 7.3 %copy.65 = f32[72,64,2,64]{0,1,2,3:T(8,128)} copy(f32[72,64,2,64]{3,1,2,0:T(8,128)} %fusion.17) | data formatting | bytes 4718592 | tf_op jit(solution)/shard_map/dot_general | solution.py:44
  137.8 6.4 %fusion = bf16[2,72,64,64]{1,2,3,0:T(8,128)(2,1)S(1)} fusion(f32[72,64,2,64]{0,1,2,3:T(8,128)} %copy.65, f32[1,2,64,64]{2,3,0,1:T(8,128)S(1)} %copy-done.5, f32[1,2,64,64]{2,3,0,1:T(8,128)S(1)} %copy-done.3), kind=kOutput, calls=%fused_computation.7 | convolution fusion | flops 907165696 | bytes 3604480 | tf_op jit(solution)/shard_map/prbz,barg->apgz/dot_general | solution.py:51
  144.2 2.2 copy.76
  146.4 26.9 %gather_fusion.1 = bf16[4096,2,72]{2,1,0:T(2,128)(2,1)} fusion(bf16[2,72,4096]{1,0,2:T(2,128)(2,1)S(1)} %bitcast.125, s32[4096]{0:T(1024)S(1)} %fusion.56), kind=kCustom, calls=%fused_computation.1.clone | custom fusion | bytes 2375680 | tf_op jit(solution)/shard_map/jit(_take)/gather | solution.py:59
  173.3 4.8 copy.68
  178.1 0.5 bitcast_convert_fusion
  178.6 2.3 copy.69
  180.9 1.7 convert.4
  182.6 1.0 fusion.63
  183.7 2.3 copy.63
  186.1 0.5 all-gather.14.cloned.1.call-update
  186.6 112.3 %all-gather.12.cloned.1.call-done = bf16[2,1,8,72,4096]{4,0,3,2,1:T(2,128)(2,1)} async-done(((bf16[2,1,8,9,4096]{4,0,3,2,1:T(2,128)(2,1)}), bf16[2,1,8,72,4096]{4,0,3,2,1:T(2,128)(2,1)}) %all-gather.12.cloned.1.call-update) | async-done | bytes 9437200 | tf_op jit(solution)/shard_map/all_gather | solution.py:80
  298.9 23.0 %fusion.61 = (bf16[1,1,8,72,4096]{4,0,3,2,1:T(2,128)(2,1)S(1)}, bf16[1,1,8,72,4096]{4,0,3,2,1:T(2,128)(2,1)S(1)}) fusion(bf16[2,1,8,72,4096]{4,0,3,2,1:T(2,128)(2,1)} %all-gather.12.cloned.1.call-done), kind=kLoop, calls=%fused_computation.107 | loop fusion | bytes 18874368 | tf_op jit(solution)/shard_map/slice | solution.py:83
  321.9 7.6 %copy.82 = bf16[1,1,8,72,4096]{4,3,0,2,1:T(8,128)(2,1)} copy(bf16[1,1,8,72,4096]{4,0,3,2,1:T(2,128)(2,1)S(1)} %get-tuple-element.22) | data formatting | bytes 9437184
  329.5 7.5 %copy.81 = bf16[1,1,8,72,4096]{4,3,0,2,1:T(8,128)(2,1)} copy(bf16[1,1,8,72,4096]{4,0,3,2,1:T(2,128)(2,1)S(1)} %get-tuple-element.23) | data formatting | bytes 9437184
  337.0 22.7 %all-gather.16.cloned.1.call-done = bf16[1,2,512,4096]{3,2,1,0:T(8,128)(2,1)} async-done(((bf16[1,2,512,256]{3,2,1,0:T(8,128)(2,1)}), bf16[1,2,512,4096]{3,2,1,0:T(8,128)(2,1)}) %all-gather.16.cloned.1.call-update) | async-done | bytes 8388624 | tf_op jit(solution)/shard_map/all_gather | solution.py:85
  359.7 6.5 %fusion.10 = f32[576,512]{1,0:T(8,128)S(1)} fusion(bf16[576,4096]{1,0:T(8,128)(2,1)} %bitcast.131, bf16[1,2,512,4096]{3,2,1,0:T(8,128)(2,1)} %all-gather.16.cloned.1.call-done), kind=kOutput, calls=%fused_computation.18 | convolution fusion | flops 2415919104 | bytes 10092544 | tf_op jit(solution)/shard_map/dot_general | solution.py:95
  366.2 0.8 copy-done.9
  367.0 2.6 fusion.11
  369.7 2.6 fusion.25
  372.4 3.1 fusion.33
  375.6 0.1 reduce_sum.72
  375.7 0.1 reduce_sum.75
  375.8 103.9 %all-gather.10.cloned.1.call-done = bf16[2,1,8,72,4096]{4,0,3,2,1:T(2,128)(2,1)} async-done(((bf16[2,1,8,9,4096]{4,0,3,2,1:T(2,128)(2,1)}), bf16[2,1,8,72,4096]{4,0,3,2,1:T(2,128)(2,1)}) %all-gather.10.cloned.1.call-update) | async-done | bytes 9437200 | tf_op jit(solution)/shard_map/all_gather | solution.py:80
  479.7 23.0 %fusion.62 = (bf16[1,1,8,72,4096]{4,0,3,2,1:T(2,128)(2,1)S(1)}, bf16[1,1,8,72,4096]{4,0,3,2,1:T(2,128)(2,1)S(1)}) fusion(bf16[2,1,8,72,4096]{4,0,3,2,1:T(2,128)(2,1)} %all-gather.10.cloned.1.call-done), kind=kLoop, calls=%fused_computation.108 | loop fusion | bytes 18874368 | tf_op jit(solution)/shard_map/slice | solution.py:83
  502.7 7.5 %copy.80 = bf16[1,1,8,72,4096]{4,3,0,2,1:T(8,128)(2,1)} copy(bf16[1,1,8,72,4096]{4,0,3,2,1:T(2,128)(2,1)S(1)} %get-tuple-element.24) | data formatting | bytes 9437184
  510.1 7.5 %copy.79 = bf16[1,1,8,72,4096]{4,3,0,2,1:T(8,128)(2,1)} copy(bf16[1,1,8,72,4096]{4,0,3,2,1:T(2,128)(2,1)S(1)} %get-tuple-element.25) | data formatting | bytes 9437184
  517.7 22.6 %all-gather.14.cloned.1.call-done = bf16[1,2,512,4096]{3,2,1,0:T(8,128)(2,1)} async-done(((bf16[1,2,512,256]{3,2,1,0:T(8,128)(2,1)}), bf16[1,2,512,4096]{3,2,1,0:T(8,128)(2,1)}) %all-gather.14.cloned.1.call-update) | async-done | bytes 8388624 | tf_op jit(solution)/shard_map/all_gather | solution.py:85
  540.3 6.3 %fusion.6 = f32[576,512]{1,0:T(8,128)S(1)} fusion(bf16[576,4096]{1,0:T(8,128)(2,1)} %bitcast.127, bf16[1,2,512,4096]{3,2,1,0:T(8,128)(2,1)} %all-gather.14.cloned.1.call-done), kind=kOutput, calls=%fused_computation.14 | convolution fusion | flops 2415919104 | bytes 10092544 | tf_op jit(solution)/shard_map/dot_general | solution.py:95
  546.6 1.1 copy-done.8
  547.6 2.6 fusion.7
  550.3 2.6 fusion.27
  553.0 3.1 fusion.29
  556.1 0.1 reduce_sum.51
  556.3 0.1 reduce_sum.54
  556.5 19.9 %psum.7 = f32[2,1,8]{2,1,0:T(1,128)S(1)} all-reduce(f32[2,1,8]{2,1,0:T(1,128)S(1)} %maximum_add_fusion), channel_id=1, replica_groups=mesh['ka'=16,'ga'=8] {'ga'}, use_global_device_ids=true, to_apply=%region_8.11 | all-reduce | flops 16 | bytes 128 | tf_op jit(solution)/shard_map/psum | solution.py:105
  576.4 0.6 broadcast_multiply_fusion
  (45 shorter events, 0.7 us)
Async XLA Ops:
  6.5 44.6 %all-gather.8.cloned.1.call-start = ((), (), s32[]{:S(2)}) async-start(), calls=%async_computation | async-start | bytes 5013504 | tf_op jit(solution)/shard_map/all_gather | solution.py:73
  7.3 291.7 %all-gather.12.cloned.1.call-start = ((), (), s32[]{:S(2)}) async-start(), calls=%async_computation.2 | async-start | bytes 10616832 | tf_op jit(solution)/shard_map/all_gather | solution.py:80
  13.3 48.7 %copy-start.6 = (f32[128,128]{0,1:T(8,128)}, f32[128,128]{0,1:T(8,128)S(1)}, u32[]{:S(2)}) copy-start(f32[128,128]{0,1:T(8,128)S(1)} %maximum_maximum_fusion) | copy-start | bytes 196612
  13.4 63.9 %copy-start.2 = (f32[1,2,64,64]{2,3,0,1:T(8,128)}, f32[1,2,64,64]{2,3,0,1:T(8,128)S(1)}, u32[]{:S(2)}) copy-start(f32[1,2,64,64]{2,3,0,1:T(8,128)S(1)} %get-tuple-element.42) | copy-start | bytes 98308
  13.4 63.9 %copy-start.4 = (f32[1,2,64,64]{2,3,0,1:T(8,128)}, f32[1,2,64,64]{2,3,0,1:T(8,128)S(1)}, u32[]{:S(2)}) copy-start(f32[1,2,64,64]{2,3,0,1:T(8,128)S(1)} %get-tuple-element.43) | copy-start | bytes 98308
  130.6 7.3 %copy-start.3 = (f32[1,2,64,64]{2,3,0,1:T(8,128)S(1)}, f32[1,2,64,64]{2,3,0,1:T(8,128)}, u32[]{:S(2)}) copy-start(f32[1,2,64,64]{2,3,0,1:T(8,128)} %copy-done.2) | copy-start | bytes 98308
  130.6 7.3 %copy-start.5 = (f32[1,2,64,64]{2,3,0,1:T(8,128)S(1)}, f32[1,2,64,64]{2,3,0,1:T(8,128)}, u32[]{:S(2)}) copy-start(f32[1,2,64,64]{2,3,0,1:T(8,128)} %copy-done.4) | copy-start | bytes 98308
  173.3 4.8 copy-start.7
  180.9 178.8 %all-gather.16.cloned.1.call-start = ((), (), s32[]{:S(2)}) async-start(), calls=%async_computation.4 | async-start | bytes 8912896 | tf_op jit(solution)/shard_map/all_gather | solution.py:85
  183.7 296.0 %all-gather.10.cloned.1.call-start = ((), (), s32[]{:S(2)}) async-start(), calls=%async_computation.1 | async-start | bytes 10616832 | tf_op jit(solution)/shard_map/all_gather | solution.py:80
  186.0 354.2 %all-gather.14.cloned.1.call-start = ((), (), s32[]{:S(2)}) async-start(), calls=%async_computation.3 | async-start | bytes 8912896 | tf_op jit(solution)/shard_map/all_gather | solution.py:85
  359.6 6.5 %copy-start.1 = (bf16[1,1,8,72,4096]{4,3,0,2,1:T(8,128)(2,1)S(1)}, bf16[1,1,8,72,4096]{4,3,0,2,1:T(8,128)(2,1)}, u32[]{:S(2)}) copy-start(bf16[1,1,8,72,4096]{4,3,0,2,1:T(8,128)(2,1)} %copy.81) | copy-start | bytes 14155780
  359.6 7.4 %copy-start.9 = (bf16[1,2,512,4096]{3,2,1,0:T(8,128)(2,1)S(1)}, bf16[1,2,512,4096]{3,2,1,0:T(8,128)(2,1)}, u32[]{:S(2)}) copy-start(bf16[1,2,512,4096]{3,2,1,0:T(8,128)(2,1)} %all-gather.16.cloned.1.call-done) | copy-start | bytes 25165828
  367.0 5.3 slice-start.2
  369.7 2.7 slice-start.3
  540.2 6.3 %copy-start = (bf16[1,1,8,72,4096]{4,3,0,2,1:T(8,128)(2,1)S(1)}, bf16[1,1,8,72,4096]{4,3,0,2,1:T(8,128)(2,1)}, u32[]{:S(2)}) copy-start(bf16[1,1,8,72,4096]{4,3,0,2,1:T(8,128)(2,1)} %copy.79) | copy-start | bytes 14155780
  540.2 7.4 %copy-start.8 = (bf16[1,2,512,4096]{3,2,1,0:T(8,128)(2,1)S(1)}, bf16[1,2,512,4096]{3,2,1,0:T(8,128)(2,1)}, u32[]{:S(2)}) copy-start(bf16[1,2,512,4096]{3,2,1,0:T(8,128)(2,1)} %all-gather.14.cloned.1.call-done) | copy-start | bytes 25165828
  547.6 5.3 slice-start
  550.3 2.7 slice-start.1
Sparse Core Ops, SparseCore 0:
  9.1 42.0 all-gather.7
  181.0 117.8 all-gather.11
  300.5 59.0 all-gather.15
  361.8 117.7 all-gather.9
  481.1 59.0 all-gather.13
where the time goes:
time: 594 us; the launch traced here: 584 us
  waiting for transfers between devices  297 us (50%)
  local copies, waits for them, and re-layouts  181 us (30%)
  matrix products  57.6 us (10%)
  blocking collectives  19.9 us (3%)
  between operations  17.7 us (3%)
  other arithmetic  10.9 us (2%)
    all_gather x2, waiting for transfers between devices, body(): pairs = lax.all_gather(local_pairs, 'ga', axis=3, tiled=True)  216 us
    gather x4, local copies, waits for them, and re-layouts, pair_elements(): picked = jnp.take(flat_grid, grid_index, axis=2).astype(jnp.bfloat16)  63.3 us
    slice x2, local copies, waits for them, and re-layouts, body(): pair_im = pairs[1].reshape(row_count, pairs.shape[4])  46 us
    all_gather x2, waiting for transfers between devices, body(): contract_piece = lax.all_gather(screen_half, 'ka', axis=2, tiled=True)  45.2 us
    all_gather x1, waiting for transfers between devices, body(): piece = lax.all_gather(band_waves, 'ka', axis=0, tiled=True)  34.2 us
    unnamed x32, local copies, waits for them, and re-layouts  32.1 us
    psum x1, blocking collectives, body(): total = lax.psum(partial_value, 'ga')  19.9 us
    dot_general x2, matrix products, pair_elements(): jnp.dot(field.reshape(row_total * N1, 2 * N2), table_two, precision=lax.P...  15.3 us
  transfers between devices with their start and end apart: 5, of which 5 were waited for; matrix products, arithmetic and copies ran while one was open for 17% of the time, Pallas kernels for 0%

commit v1 on v0

v1 whole, which is shorter than its diff:
```python
import math

import jax
import jax.numpy as jnp
import numpy as np
from jax import lax
from jax.experimental import pallas as pl
from jax.experimental.pallas import tpu as pltpu
from jax.sharding import PartitionSpec as P

N1 = 64
NG = 4096
MB = 72
NBD = 8
QSTEPS = 2
KA = 16
GA = 8
F32 = jnp.float32
BF16 = jnp.bfloat16
VMEM_BYTES = 48 * 1024 * 1024
ALL = ("ka", "ga")


def split_table(table):
    high = table.astype(jnp.bfloat16)
    low = (table - high.astype(np.float64)).astype(jnp.bfloat16)
    return high, low


def make_tables():
    places = np.arange(N1)
    angle = (places[:, None] * places[None, :] % N1) * (2.0 * math.pi / N1)
    cos, sin = np.cos(angle), np.sin(angle)
    high, low = split_table(np.concatenate([cos, sin], 0))
    exact_in = np.concatenate([high, low], 1)
    split_in = np.concatenate([high, high, low], 1)
    wide = np.concatenate([cos, sin], 1)
    block = np.zeros((2 * N1, 4 * N1))
    block[:N1, : 2 * N1] = wide
    block[N1:, 2 * N1 :] = wide
    high, low = split_table(block)
    turned = np.concatenate([high, high, low], 0)
    return exact_in, split_in, turned


def lane_sign(rows, first):
    lane = lax.broadcasted_iota(jnp.int32, (rows, 128), 1)
    return jnp.where(lane < 64, first, -first).astype(F32)


def swap_halves(x):
    return pltpu.roll(x, 64, 1)


def split_rows(x):
    high = x.astype(BF16)
    low = (x - high.astype(F32)).astype(BF16)
    return high, low


def dot(a, b):
    return jnp.dot(a, b, preferred_element_type=F32)


def pack_kernel(w_ref, extra_ref, out_ref):
    lane = lax.broadcasted_iota(jnp.int32, (512, 128), 1) // 32
    for dest in range(GA):
        half, place = dest // 4, dest % 4
        total = None
        for slot in range(4):
            part, qstep = slot // 2, slot % 2
            source = w_ref[qstep, part, :, half * 128 : (half + 1) * 128]
            shift = (slot - place) * 32 % 128
            moved = pltpu.roll(source, shift, 1) if shift else source
            total = moved if total is None else jnp.where(lane == slot, moved, total)
        out_ref[dest, 0:512, :] = total.astype(BF16)
        out_ref[dest, 512:592, :] = extra_ref[dest]


def scatter_rows(place_ref, from_ref, to_ref):
    def step(block, carry):
        for inner in range(64):
            row = block * 64 + inner
            to_ref[pl.ds(place_ref[row], 1), :] = from_ref[pl.ds(row, 1), :]
        return carry

    lax.fori_loop(0, NG // 64, step, 0)


def first_axis(exact_ref, grid_ref, half_ref, sign):
    table = exact_ref[...]
    signs = lane_sign(64, sign)

    def step(pair, carry):
        rows = grid_ref[pl.ds(pl.multiple_of(pair * 128, 128), 128), :].astype(BF16)
        left, right = rows[:64], rows[64:]
        stacked = jnp.concatenate(
            [jnp.concatenate([left, left], 0), jnp.concatenate([right, right], 0)], 1
        )
        out = dot(table, stacked)
        for side in range(2):
            piece = out[:, side * 128 : (side + 1) * 128]
            mixed = piece[:64] + signs * swap_halves(piece[64:])
            half_ref[pl.ds(pl.multiple_of(pair * 128 + side * 64, 64), 64), :] = mixed
        return carry

    lax.fori_loop(0, 32, step, 0, unroll=16)


def rows_kernel(place_ref, got_ref, extra_ref, exact_ref, turned_ref, out_ref, waves_ref, flat_ref, grid_ref, half_ref, waves_f32):
    for source in range(GA):
        flat_ref[source * 512 : (source + 1) * 512, :] = got_ref[source, 0:512, :].astype(F32)
        extra = got_ref[source, 512:592, :].astype(F32)
        for part in range(2):
            for group in range(4):
                first = (part * 4 + group) * 9
                waves_f32[part * 72 + source * 9 : part * 72 + source * 9 + 9, group * 128 : (group + 1) * 128] = extra[first : first + 9]
    waves_ref[...] = waves_f32[...].astype(BF16)
    scatter_rows(place_ref, flat_ref, grid_ref)
    first_axis(exact_ref, grid_ref, half_ref, -1.0)
    signs = lane_sign(64, -1.0)
    table = turned_ref[...]

    def step(pair, carry):
        both = jnp.concatenate(
            [half_ref[pl.ds(pair * 2 + side, 64, stride=64), :] for side in range(2)], 0
        )
        high, low = split_rows(both.T)
        out = dot(jnp.concatenate([high, low, high], 1), table)
        for side in range(2):
            piece = out[:, side * 128 : (side + 1) * 128]
            mixed = (piece[:64] + signs * swap_halves(piece[64:])).astype(BF16)
            first = pair * 2 + side
            for qstep in range(2):
                dest = (qstep * 8 + first % 8) * GA + first // 8
                out_ref[dest, 0:32, :] = mixed[qstep * 32 : (qstep + 1) * 32]
        return carry

    lax.fori_loop(0, 32, step, 0, unroll=16)

    def fill(dest, carry):
        out_ref[dest, 32:80, :] = extra_ref[dest // GA]
        return carry

    lax.fori_loop(0, KA * GA, fill, 0, unroll=16)


def columns_kernel(place_ref, got_ref, exact_ref, split_ref, out_ref, waves_ref, diag_ref, flat_ref, grid_ref, half_ref, waves_f32):
    def unpack(point, carry):
        for source in range(GA):
            index = point * GA + source
            flat_ref[pl.ds(pl.multiple_of(index * 32, 32), 32), :] = got_ref[index, 0:32, :].astype(F32)
            extra = got_ref[index, 32:80, :].astype(F32)
            for part in range(2):
                for group in range(2):
                    first = (part * 2 + group) * 9
                    lanes = slice(group * 128, (group + 1) * 128)
                    waves_f32[part * 72 + source * 9 : part * 72 + source * 9 + 9, lanes] = extra[first : first + 9]
                    row = 36 + part * 2 + group
                    diag_ref[point, part * 8 + source : part * 8 + source + 1, lanes] = (
                        extra[row : row + 1] + extra[row + 4 : row + 5]
                    )
        waves_ref[point] = waves_f32[...].astype(BF16)
        return carry

    lax.fori_loop(0, KA, unpack, 0, unroll=2)
    scatter_rows(place_ref, flat_ref, grid_ref)
    first_axis(exact_ref, grid_ref, half_ref, 1.0)
    signs = lane_sign(64, 1.0)
    table = split_ref[...]

    def step(pair, carry):
        columns = []
        for side in range(2):
            high, low = split_rows(half_ref[pl.ds(pair * 2 + side, 64, stride=64), :])
            columns.append(jnp.concatenate([high, low, high], 0))
        out = dot(table, jnp.concatenate(columns, 1))
        for side in range(2):
            piece = out[:, side * 128 : (side + 1) * 128]
            mixed = piece[:64] + signs * swap_halves(piece[64:])
            out_ref[pl.ds(pl.multiple_of(pair * 128 + side * 64, 64), 64), :] = mixed.astype(BF16)
        return carry

    lax.fori_loop(0, 32, step, 0, unroll=16)


def contract_kernel(point_ref, screen_ref, row_ref, waves_ref, diag_ref, out_ref, tile_ref):
    lane = lax.broadcasted_iota(jnp.int32, (256, 128), 1) < 64
    for qstep in range(2):
        for group in range(4):
            even = screen_ref[qstep * 8 + group * 2].astype(F32)
            odd = screen_ref[qstep * 8 + group * 2 + 1].astype(F32)
            lanes = slice(group % 2 * 128, (group % 2 + 1) * 128)
            tile_ref[qstep, 0, group // 2, :, lanes] = jnp.where(lane, even, swap_halves(odd))
            tile_ref[qstep, 1, group // 2, :, lanes] = jnp.where(lane, swap_halves(even), odd)
    out_ref[...] = jnp.zeros_like(out_ref)

    def step(partner, carry):
        near = waves_ref[partner].astype(F32)
        turned = jnp.concatenate([near, jnp.concatenate([near[72:], -near[:72]], 0)], 1).T
        turned = turned.astype(BF16)
        points = [point_ref[qstep, partner] for qstep in range(2)]
        lefts = []
        for point in points:
            diag = diag_ref[point]
            diag_re, diag_im = diag[:8], diag[8:]
            both = jnp.concatenate(
                [jnp.concatenate([diag_re, diag_im], 1), jnp.concatenate([-diag_im, diag_re], 1)], 0
            )
            high, low = split_rows(both)
            lefts.append(jnp.concatenate([high, low], 0))
        for half in range(2):
            lanes = slice(half * 256, (half + 1) * 256)
            product = dot(turned, row_ref[partner, 0:144, lanes])
            real, imag = product[:256], product[256:]
            for qstep in range(2):
                screen_re, screen_im = tile_ref[qstep, 0, half], tile_ref[qstep, 1, half]
                mixed_re = (screen_re * real - screen_im * imag).astype(BF16)
                mixed_im = (screen_re * imag + screen_im * real).astype(BF16)
                total = dot(lefts[qstep], jnp.concatenate([mixed_re, mixed_im], 0))
                total = total[:16] + total[16:]
                far = row_ref[points[qstep], 144:176, lanes].astype(F32)
                far = far[:16] + far[16:]
                far_re, far_im = far[:8], far[8:]
                total_re, total_im = total[:8], total[8:]
                sum_re = far_re * total_re - far_im * total_im
                sum_im = far_re * total_im + far_im * total_re
                both = jnp.concatenate([sum_re, sum_im], 0)
                out_ref[points[qstep]] += both[:, :128] + both[:, 128:]
        return carry

    lax.fori_loop(0, KA, step, 0, unroll=4)


def call(kernel, outs, scratch, smem, *operands):
    smem_spec = [pl.BlockSpec(memory_space=pltpu.SMEM)] * smem
    vmem_spec = [pl.BlockSpec(memory_space=pltpu.VMEM)] * (len(operands) - smem)
    return pl.pallas_call(
        kernel,
        out_shape=[jax.ShapeDtypeStruct(shape, kind) for shape, kind in outs],
        in_specs=smem_spec + vmem_spec,
        out_specs=[pl.BlockSpec(memory_space=pltpu.VMEM)] * len(outs),
        scratch_shapes=scratch,
        compiler_params=pltpu.CompilerParams(vmem_limit_bytes=VMEM_BYTES),
    )(*operands)


def body(diag_waves, band_waves, screening, partner_map, grid_index):
    own = lax.axis_index("ga")
    exact_in, split_in, turned = [jnp.asarray(table) for table in make_tables()]
    place = (grid_index % N1) * N1 + grid_index // N1
    points = jnp.arange(KA, dtype=jnp.int32)
    owners = jnp.sum(
        jnp.where(partner_map[:, :, None] == points[None, None, :], points[None, :, None], 0), axis=1
    )
    band = band_waves[0].astype(BF16)
    band_rows = band.reshape(9, 2, GA, 4, 128).transpose(2, 1, 3, 0, 4).reshape(GA, 72, 128)
    band_rows = jnp.concatenate([band_rows, jnp.zeros((GA, 8, 128), BF16)], 1)
    band_columns = band.reshape(9, 2, KA, 2, 128).transpose(2, 1, 3, 0, 4).reshape(KA, 36, 128)
    diag = diag_waves[0].transpose(1, 0, 2)
    diag_high = lax.reduce_precision(diag, 8, 7)
    diag_low = (diag - diag_high).astype(BF16)
    diag_high = diag_high.astype(BF16)
    diag_both = jnp.stack([diag_high, diag_low])
    diag_columns = lax.dynamic_index_in_dim(diag_both, own, 2, keepdims=False)
    diag_columns = diag_columns.reshape(4, KA, 2, 128).transpose(1, 0, 2, 3).reshape(KA, 8, 128)
    columns = jnp.concatenate([band_columns, diag_columns, jnp.zeros((KA, 4, 128), BF16)], 1)
    diag_rows = lax.dynamic_slice_in_dim(diag_both.reshape(32, NG), own * 512, 512, 1)

    (packed,) = call(pack_kernel, [((GA, 592, 128), BF16)], [], 0, screening, band_rows)
    packed = lax.all_to_all(packed, "ga", 0, 0)
    work = [pltpu.VMEM((NG, 128), F32)] * 3
    spread, band_part = call(
        rows_kernel,
        [((KA * GA, 80, 128), BF16), ((144, 512), BF16)],
        work + [pltpu.VMEM((144, 512), F32)],
        1,
        place, packed, columns, exact_in, turned,
    )
    row_part = lax.all_gather(jnp.concatenate([band_part, diag_rows], 0), "ka", axis=0)
    spread = lax.all_to_all(spread, ALL, 0, 0)
    screen, column_part, diag_part = call(
        columns_kernel,
        [((NG, 128), BF16), ((KA, 144, 256), BF16), ((KA, 16, 256), F32)],
        work + [pltpu.VMEM((144, 256), F32)],
        1,
        place, spread, exact_in, split_in,
    )
    screen = lax.all_to_all(screen.reshape(KA, 256, 128), "ka", 0, 0)
    (partial,) = call(
        contract_kernel,
        [((KA, 16, 128), F32)],
        [pltpu.VMEM((2, 2, 2, 256, 256), F32)],
        1,
        owners, screen, row_part, column_part, diag_part,
    )
    value = jnp.sum(partial, axis=2)
    value = jnp.broadcast_to(value[:, None, :], (KA, GA, 16)).reshape(KA * GA, 16)
    value = jnp.sum(lax.all_to_all(value, ALL, 0, 0, tiled=True), axis=0)
    return value.reshape(2, 1, NBD) * (-1.0 / (QSTEPS * MB * math.sqrt(NG) * NG))


def solution(mesh):
    in_specs = (
        P("ka", None, None, None),
        P("ka", "ga", None, None),
        P(None, None, "ga", "ka"),
        P(),
        P(),
    )
    out_specs = P(None, "ka", None)
    return jax.shard_map(body, mesh=mesh, in_specs=in_specs, out_specs=out_specs, check_vma=False)
```

time: 594 us -> 161 us (0.27); the launches traced: 584 us -> 160 us
  waiting for transfers between devices: 297 us -> 32.2 us
  local copies, waits for them, and re-layouts: 181 us -> 6.3 us
  matrix products: 57.6 us -> 0 us
  blocking collectives: 19.9 us -> 62.7 us
  Pallas kernels: 0 us -> 29.8 us
  starting transfers between devices: 0.17 us -> 12.9 us
  other arithmetic: 10.9 us -> 2.9 us
    all_gather x5 -> x1, waiting for transfers between devices: 296 us -> 0.01 us  [body(): lax.all_gather(jnp.concatenate([band_part, diag_rows], 0), 'ka', axis=0)]
    gather x5 -> x0, local copies, waits for them, and re-layouts: 64.4 us -> none  [the longest x4 63.3 us: pair_elements(): picked = jnp.take(flat_grid, grid_index, axis=2).astype(jnp.bfloat16)]
    all_to_all x0 -> x2, blocking collectives: none -> 62.7 us  [the longest x1 48.2 us: body(): spread = lax.all_to_all(spread, ALL, 0, 0)]
    dot_general x12 -> x0, matrix products: 57.6 us -> none  [the longest x2 15.3 us: pair_elements(): jnp.dot(field.reshape(row_total * N1, 2 * N2), table_two, precision=lax.P...]
    slice x5 -> x0, local copies, waits for them, and re-layouts: 49.1 us -> none  [the longest x2 46 us: body(): pair_im = pairs[1].reshape(row_count, pairs.shape[4])]
    all_to_all x0 -> x2, waiting for transfers between devices: none -> 32.2 us  [the longest x1 16.3 us: body(): packed = lax.all_to_all(packed, 'ga', 0, 0)]
    pallas_call x0 -> x4, Pallas kernels: none -> 29.8 us  [call(): pl.pallas_call(kernel, out_shape=[jax.ShapeDtypeStruct(shape, kind) for s...]
    unnamed x32 -> x18, local copies, waits for them, and re-layouts: 32.1 us -> 4.99 us
  transfers between devices with their start and end apart: 5 -> 3, of which waited for: 5 -> 2; matrix products, arithmetic and copies ran while one was open for 17% -> 1% of each run, Pallas kernels for 0% -> 6%
where the time goes in v1:
time: 161 us; the launch traced here: 160 us
  blocking collectives  62.7 us (39%)
  waiting for transfers between devices  32.2 us (20%)
  Pallas kernels  29.8 us (19%)
  between operations  13.6 us (8%)
  starting transfers between devices  12.9 us (8%)
  local copies, waits for them, and re-layouts  6.3 us (4%)
  other arithmetic  2.9 us (2%)
    all_to_all x1, blocking collectives, body(): spread = lax.all_to_all(spread, ALL, 0, 0)  48.2 us
    pallas_call x4, Pallas kernels, call(): pl.pallas_call(kernel, out_shape=[jax.ShapeDtypeStruct(shape, kind) for s...  29.8 us
    all_to_all x1, waiting for transfers between devices, body(): packed = lax.all_to_all(packed, 'ga', 0, 0)  16.3 us
    all_to_all x1, waiting for transfers between devices, body(): screen = lax.all_to_all(screen.reshape(KA, 256, 128), 'ka', 0, 0)  15.9 us
    all_to_all x1, blocking collectives, body(): value = jnp.sum(lax.all_to_all(value, ALL, 0, 0, tiled=True), axis=0)  14.4 us
    all_to_all x1, starting transfers between devices, body(): packed = lax.all_to_all(packed, 'ga', 0, 0)  8.33 us
    unnamed x18, local copies, waits for them, and re-layouts  4.99 us
    all_to_all x1, starting transfers between devices, body(): screen = lax.all_to_all(screen.reshape(KA, 256, 128), 'ka', 0, 0)  4.48 us
  transfers between devices with their start and end apart: 3, of which 2 were waited for; matrix products, arithmetic and copies ran while one was open for 1% of the time, Pallas kernels for 6%

profile of v1, /device:TPU:1, one launch (start us, length us, event | category | flops | bytes accessed | tf_op | source)
XLA Modules:
  0.0 160.3 jit_solution(11581229855410830490)
XLA Ops:
  6.5 1.1 convert_element_type.17
  7.6 0.1 convert_element_type.18
  7.8 0.0 copy-start.2
  7.8 1.6 copy-done.2
  9.4 0.0 copy-start.6
  9.4 2.0 %shard_map.82 = bf16[8,592,128]{2,1,0:T(8,128)(2,1)} custom-call(f32[2,2,512,256]{3,2,1,0:T(8,128)S(1)} %copy-done.2, bf16[8,80,128]{2,1,0:T(8,128)(2,1)S(1)} %concatenate.9.extra_ref), custom_call_target="tpu_custom_call" | custom-call | tf_op jit(solution)/shard_map/pallas_call | solution.py:238
  11.4 8.3 %all-to-all-start = ((bf16[8,592,128]{2,1,0:T(8,128)(2,1)}), bf16[8,592,128]{2,1,0:T(8,128)(2,1)S(1)}, u32[]{:S(2)}, u32[]{:S(2)}) async-start(bf16[8,592,128]{2,1,0:T(8,128)(2,1)} %shard_map.82), calls=%async_computation | async-start | bytes 2424832 | tf_op jit(solution)/shard_map/all_to_all | solution.py:271
  19.8 0.0 copy-start.7
  19.8 0.0 copy-start.3
  19.8 0.0 copy-start.4
  19.8 0.0 all-gather.3.cloned.1.call-start
  19.9 0.0 copy-done.6
  19.9 0.2 fusion.1
  20.1 0.4 pad_maximum_fusion
  20.5 0.1 convert_element_type.19
  20.7 0.2 copy.37
  20.9 0.1 fusion.3
  21.0 0.1 pad.5.clone
  21.1 0.0 copy-done.7
  21.1 0.1 maximum_maximum_fusion.extra_ref
  21.2 16.3 %all-to-all-done.got_ref = bf16[8,592,128]{2,1,0:T(8,128)(2,1)S(1)} async-done(((bf16[8,592,128]{2,1,0:T(8,128)(2,1)}), bf16[8,592,128]{2,1,0:T(8,128)(2,1)S(1)}, u32[]{:S(2)}, u32[]{:S(2)}) %all-to-all-start) | async-done | bytes 1212448 | tf_op jit(solution)/shard_map/all_to_all | solution.py:271
  37.5 0.0 copy-done.3
  37.5 0.0 copy-done.4
  37.5 8.6 %shard_map.83 = (bf16[128,80,128]{2,1,0:T(8,128)(2,1)S(1)}, bf16[144,512]{1,0:T(8,128)(2,1)S(1)}) custom-call(s32[4096]{0:T(1024)S(1)} %fusion.5.place_ref, bf16[8,592,128]{2,1,0:T(8,128)(2,1)S(1)} %all-to-all-done.got_ref, bf16[16,48,128]{2,1,0:T(8,128)(2,1)S(1)} %maximum_maximum_fusion.extra_ref, bf16[128,128]{1,0:T(8,128)(2,1)S(1)} %copy-done.4, ...), custom_call_target="tpu_custom_call" | custom-call | tf_op jit(solution)/shard_map/pallas_call | solution.py:238
  46.1 0.0 copy-start.1
  46.1 1.6 copy-done.1
  47.7 0.7 pad_maximum_fusion.1
  48.4 0.0 all-gather.3.cloned.1.call-update
  48.4 0.0 copy-start.5
  48.4 48.2 %all_to_all.24.got_ref = bf16[128,80,128]{2,1,0:T(8,128)(2,1)S(1)} all-to-all(bf16[128,80,128]{2,1,0:T(8,128)(2,1)} %copy-done.1), channel_id=1, replica_groups=mesh['ka'=16,'ga'=8] {'ka','ga'}, dimensions={0} | all-to-all | bytes 5242880 | tf_op jit(solution)/shard_map/all_to_all | solution.py:281
  96.6 0.0 copy-done.5
  96.6 0.0 copy-start.8
  96.6 9.0 %shard_map.84 = (bf16[4096,128]{1,0:T(8,128)(2,1)}, bf16[16,144,256]{2,1,0:T(8,128)(2,1)S(1)}, f32[16,16,256]{2,1,0:T(8,128)S(1)}) custom-call(s32[4096]{0:T(1024)S(1)} %fusion.5.place_ref, bf16[128,80,128]{2,1,0:T(8,128)(2,1)S(1)} %all_to_all.24.got_ref, bf16[128,128]{1,0:T(8,128)(2,1)S(1)} %copy-done.4, bf16[128,192]{1,0:T(8,128)(2,1)S(1)} %copy-done.5), custom_call_target="tpu_custom_call" | custom-call | tf_op jit(solution)/shard_map/pallas_call | solution.py:238
  105.7 4.5 %all-to-all-start.2 = ((bf16[16,256,128]{2,1,0:T(8,128)(2,1)}), bf16[16,256,128]{2,1,0:T(8,128)(2,1)S(1)}, u32[]{:S(2)}, u32[]{:S(2)}) async-start(bf16[16,256,128]{2,1,0:T(8,128)(2,1)} %bitcast.11), calls=%async_computation.2 | async-start | bytes 2097152 | tf_op jit(solution)/shard_map/all_to_all | solution.py:289
  110.1 0.0 copy-done.8
  110.1 0.1 select_reduce_fusion.point_ref
  110.2 15.9 %all-to-all-done.2.screen_ref = bf16[16,256,128]{2,1,0:T(8,128)(2,1)S(1)} async-done(((bf16[16,256,128]{2,1,0:T(8,128)(2,1)}), bf16[16,256,128]{2,1,0:T(8,128)(2,1)S(1)}, u32[]{:S(2)}, u32[]{:S(2)}) %all-to-all-start.2) | async-done | bytes 1048608 | tf_op jit(solution)/shard_map/all_to_all | solution.py:289
  126.1 0.0 all-gather.3.cloned.1.call-done
  126.1 0.0 copy-start
  126.1 1.8 %copy-done = bf16[2816,512]{1,0:T(8,128)(2,1)S(1)} copy-done((bf16[2816,512]{1,0:T(8,128)(2,1)S(1)}, bf16[2816,512]{1,0:T(8,128)(2,1)}, u32[]{:S(2)}) %copy-start) | copy-done | bytes 2883608
  127.9 10.2 %shard_map.85 = f32[16,16,128]{2,1,0:T(8,128)S(1)} custom-call(s32[2,16]{1,0:T(2,128)S(1)} %select_reduce_fusion.point_ref, bf16[16,256,128]{2,1,0:T(8,128)(2,1)S(1)} %all-to-all-done.2.screen_ref, bf16[16,176,512]{2,1,0:T(8,128)(2,1)S(1)} %bitcast.26, bf16[16,144,256]{2,1,0:T(8,128)(2,1)S(1)} %get-tuple-element.13.waves_ref, ...), custom_call_target="tpu_custom_call" | custom-call | tf_op jit(solution)/shard_map/pallas_call | solution.py:238
  138.1 0.1 reduce_sum.28
  138.2 14.4 %all_to_all.25 = f32[128,1,16]{2,1,0:T(1,128)S(1)} all-to-all(f32[128,1,16]{2,1,0:T(1,128)S(1)} %bitcast.32), channel_id=1, replica_groups=mesh['ka'=16,'ga'=8] {'ka','ga'}, dimensions={0} | all-to-all | bytes 16384 | tf_op jit(solution)/shard_map/all_to_all | solution.py:299
  152.7 0.2 reduce_sum.29
  152.8 0.6 mul.24
  (12 shorter events, 0.2 us)
Async XLA Ops:
  7.8 1.6 copy-start.2
  9.4 10.4 %copy-start.6 = (f32[1,8,2,4096]{3,2,1,0:T(2,128)S(1)}, f32[1,8,2,4096]{3,2,1,0:T(2,128)}, u32[]{:S(2)}) copy-start(f32[1,8,2,4096]{3,2,1,0:T(2,128)} %param.8) | copy-start | bytes 786436
  11.4 26.1 %all-to-all-start = ((bf16[8,592,128]{2,1,0:T(8,128)(2,1)}), bf16[8,592,128]{2,1,0:T(8,128)(2,1)S(1)}, u32[]{:S(2)}, u32[]{:S(2)}) async-start(bf16[8,592,128]{2,1,0:T(8,128)(2,1)} %shard_map.82), calls=%async_computation | async-start | bytes 2424832 | tf_op jit(solution)/shard_map/all_to_all | solution.py:271
  19.8 1.3 copy-start.7
  19.8 17.7 %copy-start.3 = (bf16[384,256]{1,0:T(8,128)(2,1)S(1)}, bf16[384,256]{1,0:T(8,128)(2,1)}, u32[]{:S(2)}) copy-start(bf16[384,256]{1,0:T(8,128)(2,1)} %constant.58.clone.turned_ref) | copy-start | bytes 589828
  19.8 17.7 %copy-start.4 = (bf16[128,128]{1,0:T(8,128)(2,1)S(1)}, bf16[128,128]{1,0:T(8,128)(2,1)}, u32[]{:S(2)}) copy-start(bf16[128,128]{1,0:T(8,128)(2,1)} %constant.56.clone.exact_ref) | copy-start | bytes 98308
  19.8 106.3 %all-gather.3.cloned.1.call-start = ((), (), s32[]{:S(2)}) async-start(), calls=%async_computation.4 | async-start | bytes 3063808 | tf_op jit(solution)/shard_map/all_gather | solution.py:280
  46.1 1.6 copy-start.1
  48.4 48.2 %copy-start.5 = (bf16[128,192]{1,0:T(8,128)(2,1)S(1)}, bf16[128,192]{1,0:T(8,128)(2,1)}, u32[]{:S(2)}) copy-start(bf16[128,192]{1,0:T(8,128)(2,1)} %constant.57.clone.split_ref) | copy-start | bytes 147460
  96.6 13.5 %copy-start.8 = (s32[2,16]{1,0:T(2,128)S(1)}, s32[2,16]{1,0:T(2,128)}, u32[]{:S(2)}) copy-start(s32[2,16]{1,0:T(2,128)} %param.11) | copy-start | bytes 388
  105.7 20.4 %all-to-all-start.2 = ((bf16[16,256,128]{2,1,0:T(8,128)(2,1)}), bf16[16,256,128]{2,1,0:T(8,128)(2,1)S(1)}, u32[]{:S(2)}, u32[]{:S(2)}) async-start(bf16[16,256,128]{2,1,0:T(8,128)(2,1)} %bitcast.11), calls=%async_computation.2 | async-start | bytes 2097152 | tf_op jit(solution)/shard_map/all_to_all | solution.py:289
  126.1 1.8 %copy-start = (bf16[2816,512]{1,0:T(8,128)(2,1)S(1)}, bf16[2816,512]{1,0:T(8,128)(2,1)}, u32[]{:S(2)}) copy-start(bf16[2816,512]{1,0:T(8,128)(2,1)} %all-gather.3.cloned.1.call-done) | copy-start | bytes 8650756
Sparse Core Ops, SparseCore 0:
  48.5 57.9 all-gather.2

commit v2 on v1

v2 whole, which is shorter than its diff:
```python
import math

import jax
import jax.numpy as jnp
import numpy as np
from jax import lax
from jax.experimental import pallas as pl
from jax.experimental.pallas import tpu as pltpu
from jax.sharding import PartitionSpec as P

N1 = 64
NG = 4096
MB = 72
NBD = 8
QSTEPS = 2
KA = 16
GA = 8
F32 = jnp.float32
BF16 = jnp.bfloat16
VMEM_BYTES = 24 * 1024 * 1024
WHOLE_VMEM = 63 * 1024 * 1024
ALL = ("ka", "ga")


def split_table(table):
    high = table.astype(jnp.bfloat16)
    low = (table - high.astype(np.float64)).astype(jnp.bfloat16)
    return high, low


def make_tables():
    places = np.arange(N1)
    angle = (places[:, None] * places[None, :] % N1) * (2.0 * math.pi / N1)
    cos, sin = np.cos(angle), np.sin(angle)
    high, low = split_table(np.concatenate([cos, sin], 0))
    exact_in = np.concatenate([high, low], 1)
    split_in = np.concatenate([high, high, low], 1)
    wide = np.concatenate([cos, sin], 1)
    block = np.zeros((2 * N1, 4 * N1))
    block[:N1, : 2 * N1] = wide
    block[N1:, 2 * N1 :] = wide
    high, low = split_table(block)
    turned = np.concatenate([high, high, low], 0)
    return exact_in, split_in, turned


def lane_sign(rows, first):
    lane = lax.broadcasted_iota(jnp.int32, (rows, 128), 1)
    return jnp.where(lane < 64, first, -first).astype(F32)


def swap_halves(x):
    return pltpu.roll(x, 64, 1)


def split_rows(x):
    high = x.astype(BF16)
    low = (x - high.astype(F32)).astype(BF16)
    return high, low


def dot(a, b):
    return jnp.dot(a, b, preferred_element_type=F32)


def pack_kernel(own_ref, w_hbm, band_hbm, diag_hbm, out_ref, columns_ref, rows_ref, w_ref, band_ref, diag_ref, sems):
    own = own_ref[0]
    band_copy = pltpu.make_async_copy(band_hbm, band_ref, sems.at[0])
    diag_copy = pltpu.make_async_copy(diag_hbm.at[own], diag_ref, sems.at[1])
    band_copy.start()
    diag_copy.start()
    w_copies = []
    for block in range(4):
        lines = pl.ds(block * 128, 128)
        copy = pltpu.make_async_copy(w_hbm.at[:, :, lines], w_ref.at[:, :, lines], sems.at[2 + block])
        copy.start()
        w_copies.append(copy)
    band_copy.wait()
    diag_copy.wait()
    rows_ref[16:24, :] = jnp.zeros((8, NG), F32)
    for band in range(8):
        rows_ref[band : band + 1, :] = band_ref[band, 0:1, :]
        rows_ref[8 + band : 9 + band, :] = band_ref[band, 1:2, :]
    rows_ref[16:18, :] = band_ref[8]
    diag = diag_ref[...]
    high = diag.astype(BF16).astype(F32)
    rows_ref[18:20, :] = high
    rows_ref[20:22, :] = diag - high
    for pair in range(16):
        lanes = [slice((pair * 2 + side) * 128, (pair * 2 + side + 1) * 128) for side in range(2)]
        block = jnp.concatenate([rows_ref[:, lane] for lane in lanes], 0).astype(BF16)
        columns_ref[2 * pair] = block
        columns_ref[2 * pair + 1] = block
        first = 512 + pair % 2 * 48
        out_ref[pair // 2, first : first + 48, :] = block
    lane = lax.broadcasted_iota(jnp.int32, (128, 128), 1) // 32
    for block in range(4):
        w_copies[block].wait()
        lines = slice(block * 128, (block + 1) * 128)
        for dest in range(GA):
            half, place = dest // 4, dest % 4
            total = None
            for slot in range(4):
                part, qstep = slot // 2, slot % 2
                source = w_ref[qstep, part, lines, half * 128 : (half + 1) * 128]
                shift = (slot - place) * 32 % 128
                moved = pltpu.roll(source, shift, 1) if shift else source
                total = moved if total is None else jnp.where(lane == slot, moved, total)
            out_ref[dest, lines, :] = total.astype(BF16)


def scatter_rows(place_ref, from_ref, to_ref):
    def step(block, carry):
        for inner in range(64):
            row = block * 64 + inner
            to_ref[pl.ds(place_ref[row], 1), :] = from_ref[pl.ds(row, 1), :]
        return carry

    lax.fori_loop(0, NG // 64, step, 0)


def first_axis(exact_ref, grid_ref, half_ref, sign):
    table = exact_ref[...]
    signs = lane_sign(64, sign)

    def step(pair, carry):
        rows = grid_ref[pl.ds(pl.multiple_of(pair * 128, 128), 128), :].astype(BF16)
        left, right = rows[:64], rows[64:]
        stacked = jnp.concatenate(
            [jnp.concatenate([left, left], 0), jnp.concatenate([right, right], 0)], 1
        )
        out = dot(table, stacked)
        for side in range(2):
            piece = out[:, side * 128 : (side + 1) * 128]
            mixed = piece[:64] + signs * swap_halves(piece[64:])
            half_ref[pl.ds(pl.multiple_of(pair * 128 + side * 64, 64), 64), :] = mixed
        return carry

    lax.fori_loop(0, 32, step, 0, unroll=16)


def rows_kernel(place_ref, got_ref, exact_ref, turned_ref, out_ref, flat_ref, grid_ref, half_ref):
    for source in range(GA):
        flat_ref[source * 512 : (source + 1) * 512, :] = got_ref[source, 0:512, :].astype(F32)
    scatter_rows(place_ref, flat_ref, grid_ref)
    first_axis(exact_ref, grid_ref, half_ref, -1.0)
    signs = lane_sign(64, -1.0)
    table = turned_ref[...]

    def step(pair, carry):
        both = jnp.concatenate(
            [half_ref[pl.ds(pair * 2 + side, 64, stride=64), :] for side in range(2)], 0
        )
        high, low = split_rows(both.T)
        out = dot(jnp.concatenate([high, low, high], 1), table)
        for side in range(2):
            piece = out[:, side * 128 : (side + 1) * 128]
            mixed = (piece[:64] + signs * swap_halves(piece[64:])).astype(BF16)
            first = pair * 2 + side
            for qstep in range(2):
                dest = (qstep * 8 + first % 8) * GA + first // 8
                out_ref[dest, 0:32, :] = mixed[qstep * 32 : (qstep + 1) * 32]
        return carry

    lax.fori_loop(0, 32, step, 0, unroll=16)


def columns_kernel(place_ref, got_ref, exact_ref, split_ref, out_ref, flat_ref, grid_ref, half_ref):
    def unpack(index, carry):
        flat_ref[pl.ds(pl.multiple_of(index * 32, 32), 32), :] = got_ref[index, 0:32, :].astype(F32)
        return carry

    lax.fori_loop(0, KA * GA, unpack, 0, unroll=16)
    scatter_rows(place_ref, flat_ref, grid_ref)
    first_axis(exact_ref, grid_ref, half_ref, 1.0)
    signs = lane_sign(64, 1.0)
    table = split_ref[...]

    def step(pair, carry):
        columns = []
        for side in range(2):
            high, low = split_rows(half_ref[pl.ds(pair * 2 + side, 64, stride=64), :])
            columns.append(jnp.concatenate([high, low, high], 0))
        out = dot(table, jnp.concatenate(columns, 1))
        for side in range(2):
            piece = out[:, side * 128 : (side + 1) * 128]
            mixed = piece[:64] + signs * swap_halves(piece[64:])
            out_ref[pl.ds(pl.multiple_of(pair * 128 + side * 64, 64), 64), :] = mixed.astype(BF16)
        return carry

    lax.fori_loop(0, 32, step, 0, unroll=16)


def pick_diag(rows):
    line = lax.broadcasted_iota(jnp.int32, (16, 192), 0)
    place = lax.broadcasted_iota(jnp.int32, (16, 192), 1)
    first = line % 8 * 24 + 18 + line // 8
    pick = jnp.where((place == first) | (place == first + 2), 1.0, 0.0).astype(BF16)
    return dot(pick, rows)


def row_side_kernel(own_ref, *refs):
    *part_refs, rows_ref, diag_ref = refs
    own = own_ref[0]
    z_own, x_own, c_own = own // 8, own // 2 % 4, own % 2
    for flip in range(2):
        for shift in range(4):
            from_ref = part_refs[flip * 4 + shift]
            for turn in range(2):
                point = (z_own + turn) % 2 * 8 + (x_own + 4 - shift) % 4 * 2 + (c_own + flip) % 2
                for pair in range(4):
                    blocks = []
                    for source in (2 * pair, 2 * pair + 1):
                        block = from_ref[turn, source].astype(F32)
                        blocks.append(
                            jnp.concatenate([block[24 * group : 24 * group + 24] for group in range(4)], 1)
                        )
                    rows_ref[point, 48 * pair : 48 * pair + 48, :] = jnp.concatenate(blocks, 0).astype(BF16)

    def step(point, carry):
        diag_ref[point] = pick_diag(rows_ref[point])
        return carry

    lax.fori_loop(0, KA, step, 0, unroll=4)


def column_side_kernel(own_ref, *refs):
    *part_refs, turned_ref, left_ref, whole_ref = refs
    y_own = own_ref[0] // 2
    for shift in range(4):
        whole_ref[(y_own + 4 - shift) % 4] = part_refs[shift][...]
    line = lax.broadcasted_iota(jnp.int32, (8, 256), 0)

    def step(point, carry):
        plain, straight, crossed = [], [], []
        for source in range(GA):
            block = whole_ref[source // 2, 2 * point + source % 2].astype(F32)
            block = jnp.concatenate([block[:24], block[24:]], 1)
            plain.append(block)
            real, imag, rest = block[:8], block[8:16], block[16:]
            straight += [real, imag, jnp.where(line < 2, rest, 0.0)]
            swapped = jnp.where(line == 0, pltpu.roll(rest, 7, 0), -pltpu.roll(rest, 1, 0))
            crossed += [imag, -real, jnp.where(line < 2, swapped, 0.0)]
        diag = pick_diag(jnp.concatenate(plain, 0).astype(BF16))
        diag_re, diag_im = diag[:8], diag[8:]
        both = jnp.concatenate(
            [jnp.concatenate([diag_re, diag_im], 1), jnp.concatenate([-diag_im, diag_re], 1)], 0
        )
        high, low = split_rows(both)
        left_ref[point] = jnp.concatenate([high, low], 0)
        turned_ref[point, 0:256, :] = jnp.concatenate(straight, 0).T.astype(BF16)
        turned_ref[point, 256:512, :] = jnp.concatenate(crossed, 0).T.astype(BF16)
        return carry

    lax.fori_loop(0, KA, step, 0, unroll=2)


def fill_tiles(screen_ref, tile_ref):
    lane = lax.broadcasted_iota(jnp.int32, (256, 128), 1) < 64
    for qstep in range(2):
        for group in range(4):
            even = screen_ref[qstep * 8 + group * 2].astype(F32)
            odd = screen_ref[qstep * 8 + group * 2 + 1].astype(F32)
            lanes = slice(group % 2 * 128, (group % 2 + 1) * 128)
            tile_ref[qstep, 0, group // 2, :, lanes] = jnp.where(lane, even, swap_halves(odd))
            tile_ref[qstep, 1, group // 2, :, lanes] = jnp.where(lane, swap_halves(even), odd)


def contract_kernel(point_ref, screen_ref, row_ref, far_ref, turned_ref, left_ref, out_ref, sum_ref, tile_ref):
    first = pl.program_id(0) * 4

    @pl.when(first == 0)
    def _():
        sum_ref[...] = jnp.zeros_like(sum_ref)
        fill_tiles(screen_ref, tile_ref)

    for inner in range(4):
        turned = turned_ref[inner]
        for half in range(2):
            lanes = slice(half * 256, (half + 1) * 256)
            product = dot(turned, row_ref[inner, :, lanes])
            real, imag = product[:256], product[256:]
            for qstep in range(2):
                point = point_ref[qstep, first + inner]
                screen_re, screen_im = tile_ref[qstep, 0, half], tile_ref[qstep, 1, half]
                mixed_re = (screen_re * real - screen_im * imag).astype(BF16)
                mixed_im = (screen_re * imag + screen_im * real).astype(BF16)
                total = dot(left_ref[point], jnp.concatenate([mixed_re, mixed_im], 0))
                total = total[:16] + total[16:]
                far = far_ref[point, :, lanes]
                far_re, far_im = far[:8], far[8:]
                total_re, total_im = total[:8], total[8:]
                sum_re = far_re * total_re - far_im * total_im
                sum_im = far_re * total_im + far_im * total_re
                both = jnp.concatenate([sum_re, sum_im], 0)
                sum_ref[point] += both[:, :128] + both[:, 128:]

    @pl.when(first == KA - 4)
    def _():
        value = jnp.sum(sum_ref[...], axis=2)
        out_ref[...] = jnp.broadcast_to(value[:, None, :], (KA, GA, 16))


def call(kernel, outs, scratch, smem, *operands, space=pltpu.VMEM, limit=VMEM_BYTES):
    smem_spec = [pl.BlockSpec(memory_space=pltpu.SMEM)] * smem
    vmem_spec = [pl.BlockSpec(memory_space=space)] * (len(operands) - smem)
    return pl.pallas_call(
        kernel,
        out_shape=[jax.ShapeDtypeStruct(shape, kind) for shape, kind in outs],
        in_specs=smem_spec + vmem_spec,
        out_specs=[pl.BlockSpec(memory_space=pltpu.VMEM)] * len(outs),
        scratch_shapes=scratch,
        compiler_params=pltpu.CompilerParams(vmem_limit_bytes=limit),
    )(*operands)


def flip_z(part):
    return lax.ppermute(part, "ka", [(index, index ^ 8) for index in range(KA)])


def along_x(part):
    parts = []
    for shift in range(1, 4):
        along = [(index, index // 8 * 8 + (index + 2 * shift) % 8) for index in range(KA)]
        parts.append(lax.ppermute(part, "ka", along))
    return parts


def along_y(part):
    parts = [part]
    for shift in range(1, 4):
        along = [(index, (index + 2 * shift) % GA) for index in range(GA)]
        parts.append(lax.ppermute(part, "ga", along))
    return parts


def flip_core(part):
    return lax.ppermute(part, "ka", [(index, index ^ 1) for index in range(KA)])


def body(diag_waves, band_waves, screening, partner_map, grid_index):
    own_k = lax.axis_index("ka").astype(jnp.int32).reshape(1)
    own_g = lax.axis_index("ga").astype(jnp.int32).reshape(1)
    exact_in, split_in, turned = [jnp.asarray(table) for table in make_tables()]
    place = (grid_index % N1) * N1 + grid_index // N1
    points = jnp.arange(KA, dtype=jnp.int32)
    owners = jnp.sum(
        jnp.where(partner_map[:, :, None] == points[None, None, :], points[None, :, None], 0), axis=1
    )
    work = [pltpu.VMEM((NG, 128), F32)] * 3
    packed, columns = call(
        pack_kernel,
        [((GA, 608, 128), BF16), ((2 * KA, 48, 128), BF16)],
        [
            pltpu.VMEM((24, NG), F32),
            pltpu.VMEM((2, 2, 512, 256), F32),
            pltpu.VMEM((9, 2, NG), F32),
            pltpu.VMEM((2, NG), F32),
            pltpu.SemaphoreType.DMA((6,)),
        ],
        1,
        own_g, screening, band_waves[0], diag_waves[0],
        space=pltpu.HBM,
        limit=WHOLE_VMEM,
    )
    packed = lax.all_to_all(packed, "ga", 0, 0)
    packed, columns = lax.optimization_barrier((packed, columns))
    planes = [[ka * GA + 2 * y + z for ka in range(KA) for z in range(2)] for y in range(4)]
    columns = lax.all_to_all(columns, ALL, 0, 0, axis_index_groups=planes)
    own_part = packed[:, 512:608]
    flipped_part = flip_z(own_part)
    (spread,) = call(
        rows_kernel, [((KA * GA, 32, 128), BF16)], work, 1, place, packed, exact_in, turned
    )
    spread, flipped_part, columns = lax.optimization_barrier((spread, flipped_part, columns))
    own_part = jnp.stack([own_part, flipped_part])
    parts = along_x(own_part)
    column_parts = along_y(columns)
    spread = lax.all_to_all(spread, ALL, 0, 0)
    (screen,) = call(
        columns_kernel, [((NG, 128), BF16)], work, 1, place, spread, exact_in, split_in
    )
    parts, column_parts, screen = lax.optimization_barrier((parts, column_parts, screen))
    screen = lax.all_to_all(screen.reshape(KA, 256, 128), "ka", 0, 0)
    parts = [own_part, *parts]
    parts += [flip_core(part) for part in parts]
    rows, far = call(
        row_side_kernel, [((KA, 192, 512), BF16), ((KA, 16, 512), F32)], [], 1, own_k, *parts
    )
    near, left = call(
        column_side_kernel, [((KA, 512, 192), BF16), ((KA, 32, 512), BF16)],
        [pltpu.VMEM((4, 2 * KA, 48, 128), BF16)],
        1,
        own_g, *column_parts,
    )
    partial = pl.pallas_call(
        contract_kernel,
        out_shape=jax.ShapeDtypeStruct((KA, GA, 16), F32),
        grid=(4,),
        in_specs=[
            pl.BlockSpec(memory_space=pltpu.SMEM),
            pl.BlockSpec((KA, 256, 128), lambda step: (0, 0, 0)),
            pl.BlockSpec((4, 192, 512), lambda step: (step, 0, 0)),
            pl.BlockSpec((KA, 16, 512), lambda step: (0, 0, 0)),
            pl.BlockSpec((4, 512, 192), lambda step: (step, 0, 0)),
            pl.BlockSpec((KA, 32, 512), lambda step: (0, 0, 0)),
        ],
        out_specs=pl.BlockSpec((KA, GA, 16), lambda step: (0, 0, 0)),
        scratch_shapes=[pltpu.VMEM((KA, 16, 128), F32), pltpu.VMEM((2, 2, 2, 256, 256), F32)],
        compiler_params=pltpu.CompilerParams(vmem_limit_bytes=WHOLE_VMEM),
    )(owners, screen, rows, far, near, left)
    value = partial.reshape(KA * GA, 16)
    value = jnp.sum(lax.all_to_all(value, ALL, 0, 0, tiled=True), axis=0)
    return value.reshape(2, 1, NBD) * (-1.0 / (QSTEPS * MB * math.sqrt(NG) * NG))


def solution(mesh):
    in_specs = (
        P("ka", None, None, None),
        P("ka", "ga", None, None),
        P(None, None, "ga", "ka"),
        P(),
        P(),
    )
    out_specs = P(None, "ka", None)
    return jax.shard_map(body, mesh=mesh, in_specs=in_specs, out_specs=out_specs, check_vma=False)
```

time: 161 us -> 140 us (0.87)
  blocking collectives: 62.7 us -> 41.6 us
  starting transfers between devices: 12.9 us -> 32.9 us
  between operations: 13.6 us -> 0.17 us
  waiting for transfers between devices: 32.2 us -> 20.1 us
  Pallas kernels: 29.8 us -> 36.7 us
  other arithmetic: 2.9 us -> 0.87 us
    all_to_all x1, blocking collectives: 48.2 us -> 26 us  [body(): packed = lax.all_to_all(packed, 'ga', 0, 0)]
    all_to_all x1 -> x2, waiting for transfers between devices: 16.3 us -> 0.01 us  [the longest x1 0.01 us: body(): columns = lax.all_to_all(columns, ALL, 0, 0, axis_index_groups=planes)]
    ppermute x0 -> x11, waiting for transfers between devices: none -> 15.4 us  [the longest x3 14.4 us: along_x(): parts.append(lax.ppermute(part, 'ka', along))]
    pallas_call x0 -> x1, Pallas kernels: none -> 11.6 us  [body(): pl.pallas_call(contract_kernel, out_shape=jax.ShapeDtypeStruct((KA, GA, 1...]
    all_to_all x1, waiting for transfers between devices: 15.9 us -> 4.74 us  [body(): screen = lax.all_to_all(screen.reshape(KA, 256, 128), 'ka', 0, 0)]
    ppermute x0 -> x11, starting transfers between devices: none -> 10.5 us  [the longest x3 4.16 us: along_y(): parts.append(lax.ppermute(part, 'ga', along))]
    all_to_all x1 -> x2, starting transfers between devices: 8.33 us -> 15.2 us  [the longest x1 7.76 us: body(): columns = lax.all_to_all(columns, ALL, 0, 0, axis_index_groups=planes)]
    pallas_call x4 -> x5, Pallas kernels: 29.8 us -> 25.1 us  [call(): pl.pallas_call(kernel, out_shape=[jax.ShapeDtypeStruct(shape, kind) for s...]
  transfers between devices with their start and end apart: 3 -> 14, of which waited for: 2 -> 4; matrix products, arithmetic and copies ran while one was open for 1% -> 1% of each run, Pallas kernels for 6% -> 16%
where the time goes in v2:
time: 140 us; the launch traced here: 139 us
  blocking collectives  41.6 us (30%)
  Pallas kernels  36.7 us (26%)
  starting transfers between devices  32.9 us (24%)
  waiting for transfers between devices  20.1 us (14%)
  local copies, waits for them, and re-layouts  6.73 us (5%)
    all_to_all x1, blocking collectives, body(): packed = lax.all_to_all(packed, 'ga', 0, 0)  26 us
    pallas_call x5, Pallas kernels, call(): pl.pallas_call(kernel, out_shape=[jax.ShapeDtypeStruct(shape, kind) for s...  25.1 us
    all_to_all x1, blocking collectives, body(): value = jnp.sum(lax.all_to_all(value, ALL, 0, 0, tiled=True), axis=0)  15.5 us
    ppermute x3, waiting for transfers between devices, along_x(): parts.append(lax.ppermute(part, 'ka', along))  14.4 us
    pallas_call x1, Pallas kernels, body(): pl.pallas_call(contract_kernel, out_shape=jax.ShapeDtypeStruct((KA, GA, 1...  11.6 us
    all_to_all x1, starting transfers between devices, body(): columns = lax.all_to_all(columns, ALL, 0, 0, axis_index_groups=planes)  7.76 us
    all_to_all x1, starting transfers between devices, body(): spread = lax.all_to_all(spread, ALL, 0, 0)  7.49 us
    all_to_all x1, starting transfers between devices, body(): screen = lax.all_to_all(screen.reshape(KA, 256, 128), 'ka', 0, 0)  7.19 us
  transfers between devices with their start and end apart: 14, of which 4 were waited for; matrix products, arithmetic and copies ran while one was open for 1% of the time, Pallas kernels for 16%

profile of v2, /device:TPU:1, one launch (start us, length us, event | category | flops | bytes accessed | tf_op | source)
XLA Modules:
  0.0 139.1 jit_solution(17895179956983905536)
XLA Ops:
  0.0 3.4 %shard_map.82 = (bf16[8,608,128]{2,1,0:T(8,128)(2,1)}, bf16[32,48,128]{2,1,0:T(8,128)(2,1)}) custom-call(s32[1]{0:T(128)} %bitcast.own_ref, f32[2,2,512,256]{3,2,1,0:T(8,128)} %w_hbm.1, f32[9,2,4096]{2,1,0:T(2,128)} %bitcast.12, f32[8,2,4096]{2,1,0:T(2,128)} %bitcast.14), custom_call_target="tpu_custom_call" | custom-call | tf_op jit(solution)/shard_map/pallas_call | solution.py:307
  3.4 0.0 copy-start.9
  3.4 0.0 copy-start.6
  3.4 0.0 copy-start.7
  3.4 26.0 %all_to_all.29.got_ref = bf16[8,608,128]{2,1,0:T(8,128)(2,1)S(1)} all-to-all(bf16[8,608,128]{2,1,0:T(8,128)(2,1)} %get-tuple-element.24), channel_id=1, replica_groups=mesh['ka'=16,'ga'=8] {'ga'}, dimensions={0} | all-to-all | bytes 2490368 | tf_op jit(solution)/shard_map/all_to_all | solution.py:366
  29.4 7.8 %all-to-all-start.1 = ((bf16[32,48,128]{2,1,0:T(8,128)(2,1)}), bf16[32,48,128]{2,1,0:T(8,128)(2,1)S(1)}, u32[]{:S(2)}, u32[]{:S(2)}) async-start(bf16[32,48,128]{2,1,0:T(8,128)(2,1)} %get-tuple-element.27), calls=%async_computation.1 | async-start | bytes 786432 | tf_op jit(solution)/shard_map/all_to_all | solution.py:369
  37.2 0.1 slice_bitcast_fusion
  37.3 1.5 %collective-permute-start = (bf16[8,96,128]{2,1,0:T(8,128)(2,1)S(1)}, bf16[8,96,128]{2,1,0:T(8,128)(2,1)S(1)}, u32[]{:S(2)}, u32[]{:S(2)}) collective-permute-start(bf16[8,96,128]{2,1,0:T(8,128)(2,1)S(1)} %get-tuple-element.44), channel_id=1, source_target_pairs={{0,64},{8,72},{16,80},{24,88},{32,96},{40,104},{48,112},{56,120},{... | collective-permute-start | bytes 589832 | tf_op jit(solution)/shard_map/ppermute | solution.py:318
  38.7 0.0 copy-done.9
  38.8 0.0 copy-done.6
  38.8 0.0 copy-done.7
  38.8 0.0 copy-start.8
  38.8 8.8 %shard_map.83 = bf16[128,32,128]{2,1,0:T(8,128)(2,1)} custom-call(s32[4096]{0:T(1024)S(1)} %fusion.1.place_ref, bf16[8,608,128]{2,1,0:T(8,128)(2,1)S(1)} %all_to_all.29.got_ref, bf16[128,128]{1,0:T(8,128)(2,1)S(1)} %copy-done.7, bf16[384,256]{1,0:T(8,128)(2,1)S(1)} %copy-done.6), custom_call_target="tpu_custom_call" | custom-call | tf_op jit(solution)/shard_map/pallas_call | solution.py:307
  47.6 0.2 collective-permute-done
  47.9 0.0 all-to-all-done.1.refs_0_
  47.9 7.5 %all-to-all-start.2 = ((bf16[128,32,128]{2,1,0:T(8,128)(2,1)}), bf16[128,32,128]{2,1,0:T(8,128)(2,1)S(1)}, u32[]{:S(2)}, u32[]{:S(2)}) async-start(bf16[128,32,128]{2,1,0:T(8,128)(2,1)} %shard_map.83), calls=%async_computation.2 | async-start | bytes 2097152 | tf_op jit(solution)/shard_map/all_to_all | solution.py:379
  55.4 0.0 copy-start.10
  55.4 2.7 %collective-permute-start.3 = (bf16[2,8,96,128]{3,2,1,0:T(8,128)(2,1)S(1)}, bf16[2,8,96,128]{3,2,1,0:T(8,128)(2,1)S(1)}, u32[]{:S(2)}, u32[]{:S(2)}) collective-permute-start(bf16[2,8,96,128]{3,2,1,0:T(8,128)(2,1)S(1)} %pad_maximum_fusion.refs_0_), channel_id=1, source_target_pairs={{0,48},{8,56},{16,0},{24,8},{32,16},{40,24},{48,32},{56,40},{64,11... | collective-permute-start | bytes 1179656 | tf_op jit(solution)/shard_map/ppermute | solution.py:325
  58.1 0.6 collective-permute-start.2
  58.7 0.6 collective-permute-start.1
  59.3 2.5 %collective-permute-start.6 = (bf16[32,48,128]{2,1,0:T(8,128)(2,1)S(1)}, bf16[32,48,128]{2,1,0:T(8,128)(2,1)S(1)}, u32[]{:S(2)}, u32[]{:S(2)}) collective-permute-start(bf16[32,48,128]{2,1,0:T(8,128)(2,1)S(1)} %all-to-all-done.1.refs_0_), channel_id=1, source_target_pairs={{0,6},{1,7},{2,0},{3,1},{4,2},{5,3},{6,4},{7,5},{8,14},{9,15},{10,... | collective-permute-start | bytes 1179656 | tf_op jit(solution)/shard_map/ppermute | solution.py:333
  61.7 0.5 collective-permute-start.5
  62.2 14.4 %collective-permute-done.3.refs_3_ = bf16[2,8,96,128]{3,2,1,0:T(8,128)(2,1)S(1)} collective-permute-done((bf16[2,8,96,128]{3,2,1,0:T(8,128)(2,1)S(1)}, bf16[2,8,96,128]{3,2,1,0:T(8,128)(2,1)S(1)}, u32[]{:S(2)}, u32[]{:S(2)}) %collective-permute-start.3) | collective-permute-done | bytes 393248 | tf_op jit(solution)/shard_map/ppermute | solution.py:325
  76.6 0.0 copy-start.4
  76.6 0.8 copy-done.4
  77.4 1.2 collective-permute-start.4
  78.6 0.0 all-to-all-done.2.got_ref
  78.6 0.0 copy-done.8
  78.6 8.6 %shard_map.84 = bf16[4096,128]{1,0:T(8,128)(2,1)} custom-call(s32[4096]{0:T(1024)S(1)} %fusion.1.place_ref, bf16[128,32,128]{2,1,0:T(8,128)(2,1)S(1)} %all-to-all-done.2.got_ref, bf16[128,128]{1,0:T(8,128)(2,1)S(1)} %copy-done.7, bf16[128,192]{1,0:T(8,128)(2,1)S(1)} %copy-done.8), custom_call_target="tpu_custom_call" | custom-call | tf_op jit(solution)/shard_map/pallas_call | solution.py:307
  87.2 0.0 copy-start.5
  87.2 0.0 collective-permute-done.2.refs_2_
  87.2 0.0 collective-permute-done.1.refs_1_
  87.2 0.0 collective-permute-done.6.refs_3_
  87.2 0.0 collective-permute-done.5.refs_2_
  87.3 0.7 collective-permute-done.4.refs_1_
  88.0 7.2 %all-to-all-start.3 = ((bf16[16,256,128]{2,1,0:T(8,128)(2,1)}), bf16[16,256,128]{2,1,0:T(8,128)(2,1)}, u32[]{:S(2)}, u32[]{:S(2)}) async-start(bf16[16,256,128]{2,1,0:T(8,128)(2,1)} %bitcast.5), calls=%async_computation.3 | async-start | bytes 2097152 | tf_op jit(solution)/shard_map/all_to_all | solution.py:384
  95.2 0.2 collective-permute-start.7
  95.4 0.3 collective-permute-start.8
  95.7 0.2 collective-permute-start.9
  95.9 0.0 copy-done.5
  95.9 0.3 collective-permute-start.10
  96.2 0.0 copy-done.10
  96.2 0.6 select_reduce_fusion.point_ref
  96.8 1.8 %shard_map.86 = (bf16[16,512,192]{2,1,0:T(8,128)(2,1)S(1)}, bf16[16,32,512]{2,1,0:T(8,128)(2,1)S(1)}) custom-call(s32[1]{0:T(128)} %bitcast.own_ref, bf16[32,48,128]{2,1,0:T(8,128)(2,1)S(1)} %all-to-all-done.1.refs_0_, bf16[32,48,128]{2,1,0:T(8,128)(2,1)S(1)} %collective-permute-done.4.refs_1_, bf16[32,48,128]{2,1,0:T(8,128)(2,1)S(1)} %collective-permute-done.5.refs_2_, ...), custom_call_target="tpu_custom_call" | custom-call | tf_op jit(solution)/shard_map/pallas_call | solution.py:307
  98.7 0.0 copy-start
  98.7 1.9 %copy-done = bf16[16,512,192]{2,1,0:T(8,128)(2,1)} copy-done((bf16[16,512,192]{2,1,0:T(8,128)(2,1)}, bf16[16,512,192]{2,1,0:T(8,128)(2,1)S(1)}, u32[]{:S(2)}) %copy-start) | copy-done | bytes 3145752
  100.6 0.0 copy-start.2
  100.6 0.8 copy-done.2
  101.4 0.0 collective-permute-done.7.refs_4_
  101.4 0.0 collective-permute-done.8.refs_5_
  101.4 0.0 collective-permute-done.9.refs_6_
  101.4 0.0 collective-permute-done.10.refs_7_
  101.4 2.4 %shard_map.85 = (bf16[16,192,512]{2,1,0:T(8,128)(2,1)S(1)}, f32[16,16,512]{2,1,0:T(8,128)S(1)}) custom-call(s32[1]{0:T(128)} %bitcast.6.own_ref, bf16[2,8,96,128]{3,2,1,0:T(8,128)(2,1)S(1)} %pad_maximum_fusion.refs_0_, bf16[2,8,96,128]{3,2,1,0:T(8,128)(2,1)} %collective-permute-done.1.refs_1_, bf16[2,8,96,128]{3,2,1,0:T(8,128)(2,1)} %collective-permute-done.2.refs_2_, ...), custom_call_target="tpu_custom_call" | custom-call | tf_op jit(solution)/shard_map/pallas_call | solution.py:307
  103.9 0.0 copy-start.1
  103.9 1.7 %copy-done.1 = bf16[16,192,512]{2,1,0:T(8,128)(2,1)} copy-done((bf16[16,192,512]{2,1,0:T(8,128)(2,1)}, bf16[16,192,512]{2,1,0:T(8,128)(2,1)S(1)}, u32[]{:S(2)}) %copy-start.1) | copy-done | bytes 3145752
  105.5 0.0 copy-start.3
  105.5 0.8 copy-done.3
  106.4 4.7 %all-to-all-done.3.screen_ref = bf16[16,256,128]{2,1,0:T(8,128)(2,1)} async-done(((bf16[16,256,128]{2,1,0:T(8,128)(2,1)}), bf16[16,256,128]{2,1,0:T(8,128)(2,1)}, u32[]{:S(2)}, u32[]{:S(2)}) %all-to-all-start.3) | async-done | bytes 1048608 | tf_op jit(solution)/shard_map/all_to_all | solution.py:384
  111.1 11.6 %shard_map.87 = f32[16,8,16]{2,1,0:T(8,128)} custom-call(s32[2,16]{1,0:T(2,128)} %select_reduce_fusion.point_ref, bf16[16,256,128]{2,1,0:T(8,128)(2,1)} %all-to-all-done.3.screen_ref, bf16[16,192,512]{2,1,0:T(8,128)(2,1)} %copy-done.1, f32[16,16,512]{2,1,0:T(8,128)} %copy-done.3, bf16[16,512,192]{2,1,0:T(8,128)(2,1)} %copy-done, bf16[16,32,512]{2,1,0:T(8,128)(2,1)} %copy-done.2), custom_call_target="tpu_custom_call" | custom-call | tf_op jit(solution)/shard_map/pallas_call | solution.py:396
  122.8 15.5 %all_to_all.30 = f32[128,1,16]{2,1,0:T(1,128)S(1)} all-to-all(f32[128,1,16]{2,1,0:T(1,128)} %bitcast.13), channel_id=1, replica_groups=mesh['ka'=16,'ga'=8] {'ka','ga'}, dimensions={0} | all-to-all | bytes 16384 | tf_op jit(solution)/shard_map/all_to_all | solution.py:413
  138.3 0.2 reduce_sum.19
  138.5 0.6 mul.20
  (3 shorter events, 0.1 us)
Async XLA Ops:
  3.4 35.4 %copy-start.9 = (s32[4096]{0:T(1024)S(1)}, s32[4096]{0:T(1024)}, u32[]{:S(2)}) copy-start(s32[4096]{0:T(1024)} %param.12) | copy-start | bytes 49156
  3.4 35.4 %copy-start.6 = (bf16[384,256]{1,0:T(8,128)(2,1)S(1)}, bf16[384,256]{1,0:T(8,128)(2,1)}, u32[]{:S(2)}) copy-start(bf16[384,256]{1,0:T(8,128)(2,1)} %constant.51.clone.turned_ref) | copy-start | bytes 589828
  3.4 35.4 %copy-start.7 = (bf16[128,128]{1,0:T(8,128)(2,1)S(1)}, bf16[128,128]{1,0:T(8,128)(2,1)}, u32[]{:S(2)}) copy-start(bf16[128,128]{1,0:T(8,128)(2,1)} %constant.49.clone.exact_ref) | copy-start | bytes 98308
  29.4 18.5 %all-to-all-start.1 = ((bf16[32,48,128]{2,1,0:T(8,128)(2,1)}), bf16[32,48,128]{2,1,0:T(8,128)(2,1)S(1)}, u32[]{:S(2)}, u32[]{:S(2)}) async-start(bf16[32,48,128]{2,1,0:T(8,128)(2,1)} %get-tuple-element.27), calls=%async_computation.1 | async-start | bytes 786432 | tf_op jit(solution)/shard_map/all_to_all | solution.py:369
  37.3 10.6 %collective-permute-start = (bf16[8,96,128]{2,1,0:T(8,128)(2,1)S(1)}, bf16[8,96,128]{2,1,0:T(8,128)(2,1)S(1)}, u32[]{:S(2)}, u32[]{:S(2)}) collective-permute-start(bf16[8,96,128]{2,1,0:T(8,128)(2,1)S(1)} %get-tuple-element.44), channel_id=1, source_target_pairs={{0,64},{8,72},{16,80},{24,88},{32,96},{40,104},{48,112},{56,120},{... | collective-permute-start | bytes 589832 | tf_op jit(solution)/shard_map/ppermute | solution.py:318
  38.8 39.8 %copy-start.8 = (bf16[128,192]{1,0:T(8,128)(2,1)S(1)}, bf16[128,192]{1,0:T(8,128)(2,1)}, u32[]{:S(2)}) copy-start(bf16[128,192]{1,0:T(8,128)(2,1)} %constant.50.clone.split_ref) | copy-start | bytes 147460
  47.9 30.7 %all-to-all-start.2 = ((bf16[128,32,128]{2,1,0:T(8,128)(2,1)}), bf16[128,32,128]{2,1,0:T(8,128)(2,1)S(1)}, u32[]{:S(2)}, u32[]{:S(2)}) async-start(bf16[128,32,128]{2,1,0:T(8,128)(2,1)} %shard_map.83), calls=%async_computation.2 | async-start | bytes 2097152 | tf_op jit(solution)/shard_map/all_to_all | solution.py:379
  55.4 40.8 %copy-start.10 = (s32[2,16]{1,0:T(2,128)S(1)}, s32[2,16]{1,0:T(2,128)}, u32[]{:S(2)}) copy-start(s32[2,16]{1,0:T(2,128)} %param.11) | copy-start | bytes 388
  55.4 21.2 %collective-permute-start.3 = (bf16[2,8,96,128]{3,2,1,0:T(8,128)(2,1)S(1)}, bf16[2,8,96,128]{3,2,1,0:T(8,128)(2,1)S(1)}, u32[]{:S(2)}, u32[]{:S(2)}) collective-permute-start(bf16[2,8,96,128]{3,2,1,0:T(8,128)(2,1)S(1)} %pad_maximum_fusion.refs_0_), channel_id=1, source_target_pairs={{0,48},{8,56},{16,0},{24,8},{32,16},{40,24},{48,32},{56,40},{64,11... | collective-permute-start | bytes 1179656 | tf_op jit(solution)/shard_map/ppermute | solution.py:325
  58.1 29.1 %collective-permute-start.2 = (bf16[2,8,96,128]{3,2,1,0:T(8,128)(2,1)S(1)}, bf16[2,8,96,128]{3,2,1,0:T(8,128)(2,1)}, u32[]{:S(2)}, u32[]{:S(2)}) collective-permute-start(bf16[2,8,96,128]{3,2,1,0:T(8,128)(2,1)S(1)} %pad_maximum_fusion.refs_0_), channel_id=1, source_target_pairs={{0,32},{8,40},{16,48},{24,56},{32,0},{40,8},{48,16},{56,24},{64,96... | collective-permute-start | bytes 1179656 | tf_op jit(solution)/shard_map/ppermute | solution.py:325
  58.7 28.6 %collective-permute-start.1 = (bf16[2,8,96,128]{3,2,1,0:T(8,128)(2,1)S(1)}, bf16[2,8,96,128]{3,2,1,0:T(8,128)(2,1)}, u32[]{:S(2)}, u32[]{:S(2)}) collective-permute-start(bf16[2,8,96,128]{3,2,1,0:T(8,128)(2,1)S(1)} %pad_maximum_fusion.refs_0_), channel_id=1, source_target_pairs={{0,16},{8,24},{16,32},{24,40},{32,48},{40,56},{48,0},{56,8},{64,80... | collective-permute-start | bytes 1179656 | tf_op jit(solution)/shard_map/ppermute | solution.py:325
  59.3 28.0 %collective-permute-start.6 = (bf16[32,48,128]{2,1,0:T(8,128)(2,1)S(1)}, bf16[32,48,128]{2,1,0:T(8,128)(2,1)S(1)}, u32[]{:S(2)}, u32[]{:S(2)}) collective-permute-start(bf16[32,48,128]{2,1,0:T(8,128)(2,1)S(1)} %all-to-all-done.1.refs_0_), channel_id=1, source_target_pairs={{0,6},{1,7},{2,0},{3,1},{4,2},{5,3},{6,4},{7,5},{8,14},{9,15},{10,... | collective-permute-start | bytes 1179656 | tf_op jit(solution)/shard_map/ppermute | solution.py:333
  61.7 25.5 %collective-permute-start.5 = (bf16[32,48,128]{2,1,0:T(8,128)(2,1)S(1)}, bf16[32,48,128]{2,1,0:T(8,128)(2,1)S(1)}, u32[]{:S(2)}, u32[]{:S(2)}) collective-permute-start(bf16[32,48,128]{2,1,0:T(8,128)(2,1)S(1)} %all-to-all-done.1.refs_0_), channel_id=1, source_target_pairs={{0,4},{1,5},{2,6},{3,7},{4,0},{5,1},{6,2},{7,3},{8,12},{9,13},{10,... | collective-permute-start | bytes 1179656 | tf_op jit(solution)/shard_map/ppermute | solution.py:333
  76.6 0.8 copy-start.4
  77.4 10.6 %collective-permute-start.4 = (bf16[32,48,128]{2,1,0:T(8,128)(2,1)S(1)}, bf16[32,48,128]{2,1,0:T(8,128)(2,1)S(1)}, u32[]{:S(2)}, u32[]{:S(2)}) collective-permute-start(bf16[32,48,128]{2,1,0:T(8,128)(2,1)S(1)} %all-to-all-done.1.refs_0_), channel_id=1, source_target_pairs={{0,2},{1,3},{2,4},{3,5},{4,6},{5,7},{6,0},{7,1},{8,10},{9,11},{10,... | collective-permute-start | bytes 1179656 | tf_op jit(solution)/shard_map/ppermute | solution.py:333
  87.2 8.7 %copy-start.5 = (bf16[2,8,96,128]{3,2,1,0:T(8,128)(2,1)S(1)}, bf16[2,8,96,128]{3,2,1,0:T(8,128)(2,1)}, u32[]{:S(2)}) copy-start(bf16[2,8,96,128]{3,2,1,0:T(8,128)(2,1)} %copy-done.4) | copy-start | bytes 1179652
  88.0 23.2 %all-to-all-start.3 = ((bf16[16,256,128]{2,1,0:T(8,128)(2,1)}), bf16[16,256,128]{2,1,0:T(8,128)(2,1)}, u32[]{:S(2)}, u32[]{:S(2)}) async-start(bf16[16,256,128]{2,1,0:T(8,128)(2,1)} %bitcast.5), calls=%async_computation.3 | async-start | bytes 2097152 | tf_op jit(solution)/shard_map/all_to_all | solution.py:384
  95.2 6.2 %collective-permute-start.7 = (bf16[2,8,96,128]{3,2,1,0:T(8,128)(2,1)S(1)}, bf16[2,8,96,128]{3,2,1,0:T(8,128)(2,1)S(1)}, u32[]{:S(2)}, u32[]{:S(2)}) collective-permute-start(bf16[2,8,96,128]{3,2,1,0:T(8,128)(2,1)S(1)} %pad_maximum_fusion.refs_0_), channel_id=1, source_target_pairs={{0,8},{8,0},{16,24},{24,16},{32,40},{40,32},{48,56},{56,48},{64,72... | collective-permute-start | bytes 1179656 | tf_op jit(solution)/shard_map/ppermute | solution.py:338
  95.4 6.0 %collective-permute-start.8 = (bf16[2,8,96,128]{3,2,1,0:T(8,128)(2,1)}, bf16[2,8,96,128]{3,2,1,0:T(8,128)(2,1)S(1)}, u32[]{:S(2)}, u32[]{:S(2)}) collective-permute-start(bf16[2,8,96,128]{3,2,1,0:T(8,128)(2,1)} %collective-permute-done.1.refs_1_), channel_id=1, source_target_pairs={{0,8},{8,0},{16,24},{24,16},{32,40},{40,32},{48,56},{56,48},{64,72... | collective-permute-start | bytes 1179656 | tf_op jit(solution)/shard_map/ppermute | solution.py:338
  95.7 5.7 %collective-permute-start.9 = (bf16[2,8,96,128]{3,2,1,0:T(8,128)(2,1)}, bf16[2,8,96,128]{3,2,1,0:T(8,128)(2,1)}, u32[]{:S(2)}, u32[]{:S(2)}) collective-permute-start(bf16[2,8,96,128]{3,2,1,0:T(8,128)(2,1)} %collective-permute-done.2.refs_2_), channel_id=1, source_target_pairs={{0,8},{8,0},{16,24},{24,16},{32,40},{40,32},{48,56},{56,48},{64,72... | collective-permute-start | bytes 1179656 | tf_op jit(solution)/shard_map/ppermute | solution.py:338
  95.9 5.5 %collective-permute-start.10 = (bf16[2,8,96,128]{3,2,1,0:T(8,128)(2,1)S(1)}, bf16[2,8,96,128]{3,2,1,0:T(8,128)(2,1)}, u32[]{:S(2)}, u32[]{:S(2)}) collective-permute-start(bf16[2,8,96,128]{3,2,1,0:T(8,128)(2,1)S(1)} %copy-done.5), channel_id=1, source_target_pairs={{0,8},{8,0},{16,24},{24,16},{32,40},{40,32},{48,56},{56,48},{64,72... | collective-permute-start | bytes 1179656 | tf_op jit(solution)/shard_map/ppermute | solution.py:338
  98.7 1.9 %copy-start = (bf16[16,512,192]{2,1,0:T(8,128)(2,1)}, bf16[16,512,192]{2,1,0:T(8,128)(2,1)S(1)}, u32[]{:S(2)}) copy-start(bf16[16,512,192]{2,1,0:T(8,128)(2,1)S(1)} %get-tuple-element.41.turned_ref) | copy-start | bytes 9437188
  100.6 0.8 copy-start.2
  103.9 1.7 %copy-start.1 = (bf16[16,192,512]{2,1,0:T(8,128)(2,1)}, bf16[16,192,512]{2,1,0:T(8,128)(2,1)S(1)}, u32[]{:S(2)}) copy-start(bf16[16,192,512]{2,1,0:T(8,128)(2,1)S(1)} %get-tuple-element.35.row_ref) | copy-start | bytes 9437188
  105.5 0.8 copy-start.3

commit v3 on v2

--- a/solution.py
+++ b/solution.py
@@ -111,12 +111,12 @@
 
 def scatter_rows(place_ref, from_ref, to_ref):
     def step(block, carry):
-        for inner in range(64):
-            row = block * 64 + inner
+        for inner in range(256):
+            row = block * 256 + inner
             to_ref[pl.ds(place_ref[row], 1), :] = from_ref[pl.ds(row, 1), :]
         return carry
 
-    lax.fori_loop(0, NG // 64, step, 0)
+    lax.fori_loop(0, NG // 256, step, 0)
 
 
 def first_axis(exact_ref, grid_ref, half_ref, sign):
@@ -136,36 +136,42 @@
             half_ref[pl.ds(pl.multiple_of(pair * 128 + side * 64, 64), 64), :] = mixed
         return carry
 
-    lax.fori_loop(0, 32, step, 0, unroll=16)
-
-
-def rows_kernel(place_ref, got_ref, exact_ref, turned_ref, out_ref, flat_ref, grid_ref, half_ref):
+    lax.fori_loop(0, 32, step, 0, unroll=32)
+
+
+def rows_kernel(place_ref, got_ref, exact_ref, turned_ref, out_hbm, out_ref, flat_ref, grid_ref, half_ref, sems):
     for source in range(GA):
         flat_ref[source * 512 : (source + 1) * 512, :] = got_ref[source, 0:512, :].astype(F32)
     scatter_rows(place_ref, flat_ref, grid_ref)
     first_axis(exact_ref, grid_ref, half_ref, -1.0)
     signs = lane_sign(64, -1.0)
     table = turned_ref[...]
-
-    def step(pair, carry):
-        both = jnp.concatenate(
-            [half_ref[pl.ds(pair * 2 + side, 64, stride=64), :] for side in range(2)], 0
-        )
-        high, low = split_rows(both.T)
-        out = dot(jnp.concatenate([high, low, high], 1), table)
-        for side in range(2):
-            piece = out[:, side * 128 : (side + 1) * 128]
-            mixed = (piece[:64] + signs * swap_halves(piece[64:])).astype(BF16)
-            first = pair * 2 + side
-            for qstep in range(2):
-                dest = (qstep * 8 + first % 8) * GA + first // 8
-                out_ref[dest, 0:32, :] = mixed[qstep * 32 : (qstep + 1) * 32]
-        return carry
-
-    lax.fori_loop(0, 32, step, 0, unroll=16)
-
-
-def columns_kernel(place_ref, got_ref, exact_ref, split_ref, out_ref, flat_ref, grid_ref, half_ref):
+    sent = []
+    for owner in range(GA):
+        for duo in range(2):
+            first = owner * 8 + duo * 4
+            lefts = []
+            for pair in range(2):
+                both = jnp.concatenate(
+                    [half_ref[pl.ds(first + pair * 2 + side, 64, stride=64), :] for side in range(2)], 0
+                )
+                high, low = split_rows(both.T)
+                lefts.append(jnp.concatenate([high, low, high], 1))
+            out = dot(jnp.concatenate(lefts, 0), table)
+            for place in range(4):
+                pair, side = place // 2, place % 2
+                piece = out[pair * 128 : (pair + 1) * 128, side * 128 : (side + 1) * 128]
+                mixed = (piece[:64] + signs * swap_halves(piece[64:])).astype(BF16)
+                for qstep in range(2):
+                    out_ref[owner, qstep * 8 + duo * 4 + place] = mixed[qstep * 32 : (qstep + 1) * 32]
+        copy = pltpu.make_async_copy(out_ref.at[owner], out_hbm.at[:, owner], sems.at[owner])
+        copy.start()
+        sent.append(copy)
+    for copy in sent:
+        copy.wait()
+
+
+def columns_kernel(place_ref, got_ref, exact_ref, split_ref, out_hbm, out_ref, flat_ref, grid_ref, half_ref, sems):
     def unpack(index, carry):
         flat_ref[pl.ds(pl.multiple_of(index * 32, 32), 32), :] = got_ref[index, 0:32, :].astype(F32)
         return carry
@@ -176,7 +182,8 @@
     signs = lane_sign(64, 1.0)
     table = split_ref[...]
 
-    def step(pair, carry):
+    sent = []
+    for pair in range(32):
         columns = []
         for side in range(2):
             high, low = split_rows(half_ref[pl.ds(pair * 2 + side, 64, stride=64), :])
@@ -185,10 +192,14 @@
         for side in range(2):
             piece = out[:, side * 128 : (side + 1) * 128]
             mixed = piece[:64] + signs * swap_halves(piece[64:])
-            out_ref[pl.ds(pl.multiple_of(pair * 128 + side * 64, 64), 64), :] = mixed.astype(BF16)
-        return carry
-
-    lax.fori_loop(0, 32, step, 0, unroll=16)
+            out_ref[pair * 128 + side * 64 : pair * 128 + side * 64 + 64, :] = mixed.astype(BF16)
+        if pair % 8 == 7:
+            lines = pl.ds((pair - 7) * 128, 1024)
+            copy = pltpu.make_async_copy(out_ref.at[lines], out_hbm.at[lines], sems.at[pair // 8])
+            copy.start()
+            sent.append(copy)
+    for copy in sent:
+        copy.wait()
 
 
 def pick_diag(rows):
@@ -205,13 +216,14 @@
     z_own, x_own, c_own = own // 8, own // 2 % 4, own % 2
     for flip in range(2):
         for shift in range(4):
-            from_ref = part_refs[flip * 4 + shift]
             for turn in range(2):
+                own_pair, up, down, *far = part_refs[flip * 5 : flip * 5 + 5]
+                from_ref = (own_pair, up, far[turn], down)[shift]
                 point = (z_own + turn) % 2 * 8 + (x_own + 4 - shift) % 4 * 2 + (c_own + flip) % 2
                 for pair in range(4):
                     blocks = []
                     for source in (2 * pair, 2 * pair + 1):
-                        block = from_ref[turn, source].astype(F32)
+                        block = (from_ref[source] if shift == 2 else from_ref[turn, source]).astype(F32)
                         blocks.append(
                             jnp.concatenate([block[24 * group : 24 * group + 24] for group in range(4)], 1)
                         )
@@ -301,14 +313,16 @@
         out_ref[...] = jnp.broadcast_to(value[:, None, :], (KA, GA, 16))
 
 
-def call(kernel, outs, scratch, smem, *operands, space=pltpu.VMEM, limit=VMEM_BYTES):
+def call(kernel, outs, scratch, smem, *operands, space=pltpu.VMEM, limit=VMEM_BYTES, far_outs=0):
     smem_spec = [pl.BlockSpec(memory_space=pltpu.SMEM)] * smem
     vmem_spec = [pl.BlockSpec(memory_space=space)] * (len(operands) - smem)
     return pl.pallas_call(
         kernel,
         out_shape=[jax.ShapeDtypeStruct(shape, kind) for shape, kind in outs],
         in_specs=smem_spec + vmem_spec,
-        out_specs=[pl.BlockSpec(memory_space=pltpu.VMEM)] * len(outs),
+        out_specs=[
+            pl.BlockSpec(memory_space=pl.ANY if index < far_outs else pltpu.VMEM) for index in range(len(outs))
+        ],
         scratch_shapes=scratch,
         compiler_params=pltpu.CompilerParams(vmem_limit_bytes=limit),
     )(*operands)
@@ -318,12 +332,8 @@
     return lax.ppermute(part, "ka", [(index, index ^ 8) for index in range(KA)])
 
 
-def along_x(part):
-    parts = []
-    for shift in range(1, 4):
-        along = [(index, index // 8 * 8 + (index + 2 * shift) % 8) for index in range(KA)]
-        parts.append(lax.ppermute(part, "ka", along))
-    return parts
+def along_x(part, shift):
+    return lax.ppermute(part, "ka", [(index, index // 8 * 8 + (index + 2 * shift) % 8) for index in range(KA)])
 
 
 def along_y(part):
@@ -369,20 +379,34 @@
     columns = lax.all_to_all(columns, ALL, 0, 0, axis_index_groups=planes)
     own_part = packed[:, 512:608]
     flipped_part = flip_z(own_part)
+    far_part = along_x(own_part, 2)
     (spread,) = call(
-        rows_kernel, [((KA * GA, 32, 128), BF16)], work, 1, place, packed, exact_in, turned
-    )
-    spread, flipped_part, columns = lax.optimization_barrier((spread, flipped_part, columns))
+        rows_kernel,
+        [((KA, GA, 32, 128), BF16)],
+        [pltpu.VMEM((GA, KA, 32, 128), BF16), *work, pltpu.SemaphoreType.DMA((GA,))],
+        1,
+        place, packed, exact_in, turned,
+        far_outs=1,
+    )
+    spread = spread.reshape(KA * GA, 32, 128)
+    spread, flipped_part, far_part, columns = lax.optimization_barrier((spread, flipped_part, far_part, columns))
     own_part = jnp.stack([own_part, flipped_part])
-    parts = along_x(own_part)
+    parts = [along_x(own_part, 1), along_x(own_part, 3)]
     column_parts = along_y(columns)
     spread = lax.all_to_all(spread, ALL, 0, 0)
+    spread, far_part = lax.optimization_barrier((spread, far_part))
+    far_parts = [far_part, flip_z(far_part)]
     (screen,) = call(
-        columns_kernel, [((NG, 128), BF16)], work, 1, place, spread, exact_in, split_in
-    )
-    parts, column_parts, screen = lax.optimization_barrier((parts, column_parts, screen))
+        columns_kernel,
+        [((NG, 128), BF16)],
+        [pltpu.VMEM((NG, 128), BF16), *work, pltpu.SemaphoreType.DMA((4,))],
+        1,
+        place, spread, exact_in, split_in,
+        far_outs=1,
+    )
+    parts, column_parts, far_parts, screen = lax.optimization_barrier((parts, column_parts, far_parts, screen))
     screen = lax.all_to_all(screen.reshape(KA, 256, 128), "ka", 0, 0)
-    parts = [own_part, *parts]
+    parts = [own_part, *parts, *far_parts]
     parts += [flip_core(part) for part in parts]
     rows, far = call(
         row_side_kernel, [((KA, 192, 512), BF16), ((KA, 16, 512), F32)], [], 1, own_k, *parts

time: 140 us -> 137 us (0.979)
  Pallas kernels: 36.7 us -> 34.5 us
    ppermute x3, waiting for transfers between devices: 14.4 us -> 3.32 us  [along_x(): lax.ppermute(part, 'ka', [(index, index // 8 * 8 + (index + 2 * shift) %...]
    all_to_all x1, waiting for transfers between devices: 0.01 us -> 10.7 us  [body(): spread = lax.all_to_all(spread, ALL, 0, 0)]
    pallas_call x5, Pallas kernels: 25.1 us -> 22.9 us  [call(): pl.pallas_call(kernel, out_shape=[jax.ShapeDtypeStruct(shape, kind) for s...]
    ppermute x3, starting transfers between devices: 3.82 us -> 5.39 us  [along_x(): lax.ppermute(part, 'ka', [(index, index // 8 * 8 + (index + 2 * shift) %...]
    all_to_all x1, starting transfers between devices: 7.49 us -> 6.08 us  [body(): spread = lax.all_to_all(spread, ALL, 0, 0)]
    unnamed x22 -> x18, local copies, waits for them, and re-layouts: 6.04 us -> 5.28 us
  transfers between devices with their start and end apart: 14 -> 16, of which waited for: 4 -> 4; matrix products, arithmetic and copies ran while one was open for 1% -> 1% of each run, Pallas kernels for 16% -> 14%
where the time goes in v3:
time: 137 us; the launch traced here: 136 us
  blocking collectives  41 us (30%)
  Pallas kernels  34.5 us (25%)
  starting transfers between devices  33 us (24%)
  waiting for transfers between devices  19.7 us (14%)
  local copies, waits for them, and re-layouts  5.98 us (4%)
  other arithmetic  1.79 us (1%)
    all_to_all x1, blocking collectives, body(): packed = lax.all_to_all(packed, 'ga', 0, 0)  26 us
    pallas_call x5, Pallas kernels, call(): pl.pallas_call(kernel, out_shape=[jax.ShapeDtypeStruct(shape, kind) for s...  22.9 us
    all_to_all x1, blocking collectives, body(): value = jnp.sum(lax.all_to_all(value, ALL, 0, 0, tiled=True), axis=0)  14.9 us
    pallas_call x1, Pallas kernels, body(): pl.pallas_call(contract_kernel, out_shape=jax.ShapeDtypeStruct((KA, GA, 1...  11.6 us
    all_to_all x1, waiting for transfers between devices, body(): spread = lax.all_to_all(spread, ALL, 0, 0)  10.7 us
    all_to_all x1, starting transfers between devices, body(): columns = lax.all_to_all(columns, ALL, 0, 0, axis_index_groups=planes)  7.76 us
    all_to_all x1, starting transfers between devices, body(): screen = lax.all_to_all(screen.reshape(KA, 256, 128), 'ka', 0, 0)  6.08 us
    all_to_all x1, starting transfers between devices, body(): spread = lax.all_to_all(spread, ALL, 0, 0)  6.08 us
  transfers between devices with their start and end apart: 16, of which 4 were waited for; matrix products, arithmetic and copies ran while one was open for 1% of the time, Pallas kernels for 14%

profile of v3, /device:TPU:1, one launch (start us, length us, event | category | flops | bytes accessed | tf_op | source)
XLA Modules:
  0.0 136.1 jit_solution(6213901547569058955)
XLA Ops:
  0.0 3.4 %shard_map.82 = (bf16[8,608,128]{2,1,0:T(8,128)(2,1)}, bf16[32,48,128]{2,1,0:T(8,128)(2,1)}) custom-call(s32[1]{0:T(128)} %bitcast.own_ref, f32[2,2,512,256]{3,2,1,0:T(8,128)} %w_hbm.1, f32[9,2,4096]{2,1,0:T(2,128)} %bitcast.13, f32[8,2,4096]{2,1,0:T(2,128)} %bitcast.15), custom_call_target="tpu_custom_call" | custom-call | tf_op jit(solution)/shard_map/pallas_call | solution.py:319
  3.4 0.0 copy-start.7
  3.4 0.0 copy-start.4
  3.4 0.0 copy-start.5
  3.4 26.0 %all_to_all.29.got_ref = bf16[8,608,128]{2,1,0:T(8,128)(2,1)S(1)} all-to-all(bf16[8,608,128]{2,1,0:T(8,128)(2,1)} %get-tuple-element.28), channel_id=1, replica_groups=mesh['ka'=16,'ga'=8] {'ga'}, dimensions={0} | all-to-all | bytes 2490368 | tf_op jit(solution)/shard_map/all_to_all | solution.py:376
  29.4 7.8 %all-to-all-start.1 = ((bf16[32,48,128]{2,1,0:T(8,128)(2,1)}), bf16[32,48,128]{2,1,0:T(8,128)(2,1)S(1)}, u32[]{:S(2)}, u32[]{:S(2)}) async-start(bf16[32,48,128]{2,1,0:T(8,128)(2,1)} %get-tuple-element.31), calls=%async_computation.1 | async-start | bytes 786432 | tf_op jit(solution)/shard_map/all_to_all | solution.py:379
  37.2 0.1 slice_bitcast_fusion
  37.3 1.5 %collective-permute-start = (bf16[8,96,128]{2,1,0:T(8,128)(2,1)S(1)}, bf16[8,96,128]{2,1,0:T(8,128)(2,1)}, u32[]{:S(2)}, u32[]{:S(2)}) collective-permute-start(bf16[8,96,128]{2,1,0:T(8,128)(2,1)S(1)} %get-tuple-element.52), channel_id=1, source_target_pairs={{0,64},{8,72},{16,80},{24,88},{32,96},{40,104},{48,112},{56,120},{... | collective-permute-start | bytes 589832 | tf_op jit(solution)/shard_map/ppermute | solution.py:332
  38.7 2.7 %collective-permute-start.1 = (bf16[8,96,128]{2,1,0:T(8,128)(2,1)S(1)}, bf16[8,96,128]{2,1,0:T(8,128)(2,1)S(1)}, u32[]{:S(2)}, u32[]{:S(2)}) collective-permute-start(bf16[8,96,128]{2,1,0:T(8,128)(2,1)S(1)} %get-tuple-element.52), channel_id=1, source_target_pairs={{0,32},{8,40},{16,48},{24,56},{32,0},{40,8},{48,16},{56,24},{64,96... | collective-permute-start | bytes 589832 | tf_op jit(solution)/shard_map/ppermute | solution.py:336
  41.5 0.0 copy-done.7
  41.5 0.0 copy-done.4
  41.5 0.0 copy-done.5
  41.5 0.0 copy-start.6
  41.5 7.9 %shard_map.83 = bf16[16,8,32,128]{3,2,1,0:T(8,128)(2,1)} custom-call(s32[4096]{0:T(1024)S(1)} %fusion.1.place_ref, bf16[8,608,128]{2,1,0:T(8,128)(2,1)S(1)} %all_to_all.29.got_ref, bf16[128,128]{1,0:T(8,128)(2,1)S(1)} %copy-done.5, bf16[384,256]{1,0:T(8,128)(2,1)S(1)} %copy-done.4), custom_call_target="tpu_custom_call" | custom-call | tf_op jit(solution)/shard_map/pallas_call | solution.py:319
  49.4 0.0 collective-permute-done
  49.4 0.0 collective-permute-done.1.refs_3_
  49.4 0.0 all-to-all-done.1.refs_0_
  49.4 6.1 %all-to-all-start.2 = ((bf16[128,32,128]{2,1,0:T(8,128)(2,1)}), bf16[128,32,128]{2,1,0:T(8,128)(2,1)S(1)}, u32[]{:S(2)}, u32[]{:S(2)}) async-start(bf16[128,32,128]{2,1,0:T(8,128)(2,1)} %bitcast.4), calls=%async_computation.2 | async-start | bytes 2097152 | tf_op jit(solution)/shard_map/all_to_all | solution.py:396
  55.5 1.0 pad_maximum_fusion.refs_0_
  56.5 0.0 copy-start.8
  56.5 2.7 %collective-permute-start.3 = (bf16[2,8,96,128]{3,2,1,0:T(8,128)(2,1)S(1)}, bf16[2,8,96,128]{3,2,1,0:T(8,128)(2,1)}, u32[]{:S(2)}, u32[]{:S(2)}) collective-permute-start(bf16[2,8,96,128]{3,2,1,0:T(8,128)(2,1)S(1)} %pad_maximum_fusion.refs_0_), channel_id=1, source_target_pairs={{0,48},{8,56},{16,0},{24,8},{32,16},{40,24},{48,32},{56,40},{64,11... | collective-permute-start | bytes 1179656 | tf_op jit(solution)/shard_map/ppermute | solution.py:336
  59.1 0.0 collective-permute-start.2
  59.1 2.5 %collective-permute-start.6 = (bf16[32,48,128]{2,1,0:T(8,128)(2,1)S(1)}, bf16[32,48,128]{2,1,0:T(8,128)(2,1)S(1)}, u32[]{:S(2)}, u32[]{:S(2)}) collective-permute-start(bf16[32,48,128]{2,1,0:T(8,128)(2,1)S(1)} %all-to-all-done.1.refs_0_), channel_id=1, source_target_pairs={{0,6},{1,7},{2,0},{3,1},{4,2},{5,3},{6,4},{7,5},{8,14},{9,15},{10,... | collective-permute-start | bytes 1179656 | tf_op jit(solution)/shard_map/ppermute | solution.py:343
  61.6 0.5 collective-permute-start.5
  62.1 0.6 collective-permute-start.4
  62.7 10.7 %all-to-all-done.2.got_ref = bf16[128,32,128]{2,1,0:T(8,128)(2,1)S(1)} async-done(((bf16[128,32,128]{2,1,0:T(8,128)(2,1)}), bf16[128,32,128]{2,1,0:T(8,128)(2,1)S(1)}, u32[]{:S(2)}, u32[]{:S(2)}) %all-to-all-start.2) | async-done | bytes 1048608 | tf_op jit(solution)/shard_map/all_to_all | solution.py:396
  73.4 3.3 %collective-permute-done.3.refs_2_ = bf16[2,8,96,128]{3,2,1,0:T(8,128)(2,1)} collective-permute-done((bf16[2,8,96,128]{3,2,1,0:T(8,128)(2,1)S(1)}, bf16[2,8,96,128]{3,2,1,0:T(8,128)(2,1)}, u32[]{:S(2)}, u32[]{:S(2)}) %collective-permute-start.3) | collective-permute-done | bytes 393248 | tf_op jit(solution)/shard_map/ppermute | solution.py:336
  76.7 1.3 collective-permute-start.7
  78.1 0.0 copy-done.6
  78.1 7.5 %shard_map.84 = bf16[4096,128]{1,0:T(8,128)(2,1)} custom-call(s32[4096]{0:T(1024)S(1)} %fusion.1.place_ref, bf16[128,32,128]{2,1,0:T(8,128)(2,1)S(1)} %all-to-all-done.2.got_ref, bf16[128,128]{1,0:T(8,128)(2,1)S(1)} %copy-done.5, bf16[128,192]{1,0:T(8,128)(2,1)S(1)} %copy-done.6), custom_call_target="tpu_custom_call" | custom-call | tf_op jit(solution)/shard_map/pallas_call | solution.py:319
  85.6 0.0 collective-permute-done.2.refs_1_
  85.6 0.0 collective-permute-done.6.refs_3_
  85.6 0.0 collective-permute-done.5.refs_2_
  85.6 1.0 collective-permute-done.4.refs_1_
  86.7 0.0 collective-permute-done.7.refs_4_
  86.7 6.1 %all-to-all-start.3 = ((bf16[16,256,128]{2,1,0:T(8,128)(2,1)}), bf16[16,256,128]{2,1,0:T(8,128)(2,1)}, u32[]{:S(2)}, u32[]{:S(2)}) async-start(bf16[16,256,128]{2,1,0:T(8,128)(2,1)} %bitcast.6), calls=%async_computation.3 | async-start | bytes 2097152 | tf_op jit(solution)/shard_map/all_to_all | solution.py:408
  92.8 0.2 collective-permute-start.8
  93.0 0.3 collective-permute-start.9
  93.3 0.3 collective-permute-start.10
  93.6 0.2 collective-permute-start.11
  93.8 0.3 collective-permute-start.12
  94.1 0.0 copy-done.8
  94.1 0.6 select_reduce_fusion.point_ref
  94.7 1.8 %shard_map.86 = (bf16[16,512,192]{2,1,0:T(8,128)(2,1)S(1)}, bf16[16,32,512]{2,1,0:T(8,128)(2,1)S(1)}) custom-call(s32[1]{0:T(128)} %bitcast.own_ref, bf16[32,48,128]{2,1,0:T(8,128)(2,1)S(1)} %all-to-all-done.1.refs_0_, bf16[32,48,128]{2,1,0:T(8,128)(2,1)S(1)} %collective-permute-done.4.refs_1_, bf16[32,48,128]{2,1,0:T(8,128)(2,1)S(1)} %collective-permute-done.5.refs_2_, ...), custom_call_target="tpu_custom_call" | custom-call | tf_op jit(solution)/shard_map/pallas_call | solution.py:319
  96.5 0.0 copy-start
  96.5 1.9 %copy-done = bf16[16,512,192]{2,1,0:T(8,128)(2,1)} copy-done((bf16[16,512,192]{2,1,0:T(8,128)(2,1)}, bf16[16,512,192]{2,1,0:T(8,128)(2,1)S(1)}, u32[]{:S(2)}) %copy-start) | copy-done | bytes 3145752
  98.5 0.0 copy-start.2
  98.5 0.8 copy-done.2
  99.3 0.0 collective-permute-done.8.refs_5_
  99.3 0.0 collective-permute-done.11.refs_8_
  99.3 0.0 collective-permute-done.12.refs_9_
  99.3 0.0 collective-permute-done.9.refs_6_
  99.3 0.0 collective-permute-done.10.refs_7_
  99.3 2.3 %shard_map.85 = (bf16[16,192,512]{2,1,0:T(8,128)(2,1)S(1)}, f32[16,16,512]{2,1,0:T(8,128)S(1)}) custom-call(s32[1]{0:T(128)} %bitcast.7.own_ref, bf16[2,8,96,128]{3,2,1,0:T(8,128)(2,1)S(1)} %pad_maximum_fusion.refs_0_, bf16[2,8,96,128]{3,2,1,0:T(8,128)(2,1)} %collective-permute-done.2.refs_1_, bf16[2,8,96,128]{3,2,1,0:T(8,128)(2,1)} %collective-permute-done.3.refs_2_, ...), custom_call_target="tpu_custom_call" | custom-call | tf_op jit(solution)/shard_map/pallas_call | solution.py:319
  101.6 0.0 copy-start.1
  101.6 1.7 %copy-done.1 = bf16[16,192,512]{2,1,0:T(8,128)(2,1)} copy-done((bf16[16,192,512]{2,1,0:T(8,128)(2,1)}, bf16[16,192,512]{2,1,0:T(8,128)(2,1)S(1)}, u32[]{:S(2)}) %copy-start.1) | copy-done | bytes 3145752
  103.3 0.0 copy-start.3
  103.3 0.8 copy-done.3
  104.1 4.6 %all-to-all-done.3.screen_ref = bf16[16,256,128]{2,1,0:T(8,128)(2,1)} async-done(((bf16[16,256,128]{2,1,0:T(8,128)(2,1)}), bf16[16,256,128]{2,1,0:T(8,128)(2,1)}, u32[]{:S(2)}, u32[]{:S(2)}) %all-to-all-start.3) | async-done | bytes 1048608 | tf_op jit(solution)/shard_map/all_to_all | solution.py:408
  108.7 11.6 %shard_map.87 = f32[16,8,16]{2,1,0:T(8,128)} custom-call(s32[2,16]{1,0:T(2,128)} %select_reduce_fusion.point_ref, bf16[16,256,128]{2,1,0:T(8,128)(2,1)} %all-to-all-done.3.screen_ref, bf16[16,192,512]{2,1,0:T(8,128)(2,1)} %copy-done.1, f32[16,16,512]{2,1,0:T(8,128)} %copy-done.3, bf16[16,512,192]{2,1,0:T(8,128)(2,1)} %copy-done, bf16[16,32,512]{2,1,0:T(8,128)(2,1)} %copy-done.2), custom_call_target="tpu_custom_call" | custom-call | tf_op jit(solution)/shard_map/pallas_call | solution.py:420
  120.4 14.9 %all_to_all.30 = f32[128,1,16]{2,1,0:T(1,128)S(1)} all-to-all(f32[128,1,16]{2,1,0:T(1,128)} %bitcast.14), channel_id=1, replica_groups=mesh['ka'=16,'ga'=8] {'ka','ga'}, dimensions={0} | all-to-all | bytes 16384 | tf_op jit(solution)/shard_map/all_to_all | solution.py:437
  135.3 0.2 reduce_sum.19
  135.5 0.6 mul.20
  (2 shorter events, 0.0 us)
Async XLA Ops:
  3.4 38.1 %copy-start.7 = (s32[4096]{0:T(1024)S(1)}, s32[4096]{0:T(1024)}, u32[]{:S(2)}) copy-start(s32[4096]{0:T(1024)} %param.12) | copy-start | bytes 49156
  3.4 38.1 %copy-start.4 = (bf16[384,256]{1,0:T(8,128)(2,1)S(1)}, bf16[384,256]{1,0:T(8,128)(2,1)}, u32[]{:S(2)}) copy-start(bf16[384,256]{1,0:T(8,128)(2,1)} %constant.51.clone.turned_ref) | copy-start | bytes 589828
  3.4 38.1 %copy-start.5 = (bf16[128,128]{1,0:T(8,128)(2,1)S(1)}, bf16[128,128]{1,0:T(8,128)(2,1)}, u32[]{:S(2)}) copy-start(bf16[128,128]{1,0:T(8,128)(2,1)} %constant.49.clone.exact_ref) | copy-start | bytes 98308
  29.4 20.0 %all-to-all-start.1 = ((bf16[32,48,128]{2,1,0:T(8,128)(2,1)}), bf16[32,48,128]{2,1,0:T(8,128)(2,1)S(1)}, u32[]{:S(2)}, u32[]{:S(2)}) async-start(bf16[32,48,128]{2,1,0:T(8,128)(2,1)} %get-tuple-element.31), calls=%async_computation.1 | async-start | bytes 786432 | tf_op jit(solution)/shard_map/all_to_all | solution.py:379
  37.3 12.1 %collective-permute-start = (bf16[8,96,128]{2,1,0:T(8,128)(2,1)S(1)}, bf16[8,96,128]{2,1,0:T(8,128)(2,1)}, u32[]{:S(2)}, u32[]{:S(2)}) collective-permute-start(bf16[8,96,128]{2,1,0:T(8,128)(2,1)S(1)} %get-tuple-element.52), channel_id=1, source_target_pairs={{0,64},{8,72},{16,80},{24,88},{32,96},{40,104},{48,112},{56,120},{... | collective-permute-start | bytes 589832 | tf_op jit(solution)/shard_map/ppermute | solution.py:332
  38.7 10.7 %collective-permute-start.1 = (bf16[8,96,128]{2,1,0:T(8,128)(2,1)S(1)}, bf16[8,96,128]{2,1,0:T(8,128)(2,1)S(1)}, u32[]{:S(2)}, u32[]{:S(2)}) collective-permute-start(bf16[8,96,128]{2,1,0:T(8,128)(2,1)S(1)} %get-tuple-element.52), channel_id=1, source_target_pairs={{0,32},{8,40},{16,48},{24,56},{32,0},{40,8},{48,16},{56,24},{64,96... | collective-permute-start | bytes 589832 | tf_op jit(solution)/shard_map/ppermute | solution.py:336
  41.5 36.6 %copy-start.6 = (bf16[128,192]{1,0:T(8,128)(2,1)S(1)}, bf16[128,192]{1,0:T(8,128)(2,1)}, u32[]{:S(2)}) copy-start(bf16[128,192]{1,0:T(8,128)(2,1)} %constant.50.clone.split_ref) | copy-start | bytes 147460
  49.4 24.0 %all-to-all-start.2 = ((bf16[128,32,128]{2,1,0:T(8,128)(2,1)}), bf16[128,32,128]{2,1,0:T(8,128)(2,1)S(1)}, u32[]{:S(2)}, u32[]{:S(2)}) async-start(bf16[128,32,128]{2,1,0:T(8,128)(2,1)} %bitcast.4), calls=%async_computation.2 | async-start | bytes 2097152 | tf_op jit(solution)/shard_map/all_to_all | solution.py:396
  56.5 37.6 %copy-start.8 = (s32[2,16]{1,0:T(2,128)S(1)}, s32[2,16]{1,0:T(2,128)}, u32[]{:S(2)}) copy-start(s32[2,16]{1,0:T(2,128)} %param.11) | copy-start | bytes 388
  56.5 20.3 %collective-permute-start.3 = (bf16[2,8,96,128]{3,2,1,0:T(8,128)(2,1)S(1)}, bf16[2,8,96,128]{3,2,1,0:T(8,128)(2,1)}, u32[]{:S(2)}, u32[]{:S(2)}) collective-permute-start(bf16[2,8,96,128]{3,2,1,0:T(8,128)(2,1)S(1)} %pad_maximum_fusion.refs_0_), channel_id=1, source_target_pairs={{0,48},{8,56},{16,0},{24,8},{32,16},{40,24},{48,32},{56,40},{64,11... | collective-permute-start | bytes 1179656 | tf_op jit(solution)/shard_map/ppermute | solution.py:336
  59.1 26.5 %collective-permute-start.2 = (bf16[2,8,96,128]{3,2,1,0:T(8,128)(2,1)S(1)}, bf16[2,8,96,128]{3,2,1,0:T(8,128)(2,1)}, u32[]{:S(2)}, u32[]{:S(2)}) collective-permute-start(bf16[2,8,96,128]{3,2,1,0:T(8,128)(2,1)S(1)} %pad_maximum_fusion.refs_0_), channel_id=1, source_target_pairs={{0,16},{8,24},{16,32},{24,40},{32,48},{40,56},{48,0},{56,8},{64,80... | collective-permute-start | bytes 1179656 | tf_op jit(solution)/shard_map/ppermute | solution.py:336
  59.1 26.5 %collective-permute-start.6 = (bf16[32,48,128]{2,1,0:T(8,128)(2,1)S(1)}, bf16[32,48,128]{2,1,0:T(8,128)(2,1)S(1)}, u32[]{:S(2)}, u32[]{:S(2)}) collective-permute-start(bf16[32,48,128]{2,1,0:T(8,128)(2,1)S(1)} %all-to-all-done.1.refs_0_), channel_id=1, source_target_pairs={{0,6},{1,7},{2,0},{3,1},{4,2},{5,3},{6,4},{7,5},{8,14},{9,15},{10,... | collective-permute-start | bytes 1179656 | tf_op jit(solution)/shard_map/ppermute | solution.py:343
  61.6 24.0 %collective-permute-start.5 = (bf16[32,48,128]{2,1,0:T(8,128)(2,1)S(1)}, bf16[32,48,128]{2,1,0:T(8,128)(2,1)S(1)}, u32[]{:S(2)}, u32[]{:S(2)}) collective-permute-start(bf16[32,48,128]{2,1,0:T(8,128)(2,1)S(1)} %all-to-all-done.1.refs_0_), channel_id=1, source_target_pairs={{0,4},{1,5},{2,6},{3,7},{4,0},{5,1},{6,2},{7,3},{8,12},{9,13},{10,... | collective-permute-start | bytes 1179656 | tf_op jit(solution)/shard_map/ppermute | solution.py:343
  62.1 24.6 %collective-permute-start.4 = (bf16[32,48,128]{2,1,0:T(8,128)(2,1)S(1)}, bf16[32,48,128]{2,1,0:T(8,128)(2,1)S(1)}, u32[]{:S(2)}, u32[]{:S(2)}) collective-permute-start(bf16[32,48,128]{2,1,0:T(8,128)(2,1)S(1)} %all-to-all-done.1.refs_0_), channel_id=1, source_target_pairs={{0,2},{1,3},{2,4},{3,5},{4,6},{5,7},{6,0},{7,1},{8,10},{9,11},{10,... | collective-permute-start | bytes 1179656 | tf_op jit(solution)/shard_map/ppermute | solution.py:343
  76.7 10.0 %collective-permute-start.7 = (bf16[8,96,128]{2,1,0:T(8,128)(2,1)S(1)}, bf16[8,96,128]{2,1,0:T(8,128)(2,1)S(1)}, u32[]{:S(2)}, u32[]{:S(2)}) collective-permute-start(bf16[8,96,128]{2,1,0:T(8,128)(2,1)S(1)} %collective-permute-done.1.refs_3_), channel_id=1, source_target_pairs={{0,64},{8,72},{16,80},{24,88},{32,96},{40,104},{48,112},{56,120},{... | collective-permute-start | bytes 589832 | tf_op jit(solution)/shard_map/ppermute | solution.py:332
  86.7 22.0 %all-to-all-start.3 = ((bf16[16,256,128]{2,1,0:T(8,128)(2,1)}), bf16[16,256,128]{2,1,0:T(8,128)(2,1)}, u32[]{:S(2)}, u32[]{:S(2)}) async-start(bf16[16,256,128]{2,1,0:T(8,128)(2,1)} %bitcast.6), calls=%async_computation.3 | async-start | bytes 2097152 | tf_op jit(solution)/shard_map/all_to_all | solution.py:408
  92.8 6.5 %collective-permute-start.8 = (bf16[2,8,96,128]{3,2,1,0:T(8,128)(2,1)S(1)}, bf16[2,8,96,128]{3,2,1,0:T(8,128)(2,1)S(1)}, u32[]{:S(2)}, u32[]{:S(2)}) collective-permute-start(bf16[2,8,96,128]{3,2,1,0:T(8,128)(2,1)S(1)} %pad_maximum_fusion.refs_0_), channel_id=1, source_target_pairs={{0,8},{8,0},{16,24},{24,16},{32,40},{40,32},{48,56},{56,48},{64,72... | collective-permute-start | bytes 1179656 | tf_op jit(solution)/shard_map/ppermute | solution.py:348
  93.0 6.3 %collective-permute-start.9 = (bf16[2,8,96,128]{3,2,1,0:T(8,128)(2,1)}, bf16[2,8,96,128]{3,2,1,0:T(8,128)(2,1)S(1)}, u32[]{:S(2)}, u32[]{:S(2)}) collective-permute-start(bf16[2,8,96,128]{3,2,1,0:T(8,128)(2,1)} %collective-permute-done.2.refs_1_), channel_id=1, source_target_pairs={{0,8},{8,0},{16,24},{24,16},{32,40},{40,32},{48,56},{56,48},{64,72... | collective-permute-start | bytes 1179656 | tf_op jit(solution)/shard_map/ppermute | solution.py:348
  93.3 6.0 %collective-permute-start.10 = (bf16[2,8,96,128]{3,2,1,0:T(8,128)(2,1)}, bf16[2,8,96,128]{3,2,1,0:T(8,128)(2,1)S(1)}, u32[]{:S(2)}, u32[]{:S(2)}) collective-permute-start(bf16[2,8,96,128]{3,2,1,0:T(8,128)(2,1)} %collective-permute-done.3.refs_2_), channel_id=1, source_target_pairs={{0,8},{8,0},{16,24},{24,16},{32,40},{40,32},{48,56},{56,48},{64,72... | collective-permute-start | bytes 1179656 | tf_op jit(solution)/shard_map/ppermute | solution.py:348
  93.6 5.7 %collective-permute-start.11 = (bf16[8,96,128]{2,1,0:T(8,128)(2,1)S(1)}, bf16[8,96,128]{2,1,0:T(8,128)(2,1)}, u32[]{:S(2)}, u32[]{:S(2)}) collective-permute-start(bf16[8,96,128]{2,1,0:T(8,128)(2,1)S(1)} %collective-permute-done.1.refs_3_), channel_id=1, source_target_pairs={{0,8},{8,0},{16,24},{24,16},{32,40},{40,32},{48,56},{56,48},{64,72... | collective-permute-start | bytes 589832 | tf_op jit(solution)/shard_map/ppermute | solution.py:348
  93.8 5.5 %collective-permute-start.12 = (bf16[8,96,128]{2,1,0:T(8,128)(2,1)S(1)}, bf16[8,96,128]{2,1,0:T(8,128)(2,1)}, u32[]{:S(2)}, u32[]{:S(2)}) collective-permute-start(bf16[8,96,128]{2,1,0:T(8,128)(2,1)S(1)} %collective-permute-done.7.refs_4_), channel_id=1, source_target_pairs={{0,8},{8,0},{16,24},{24,16},{32,40},{40,32},{48,56},{56,48},{64,72... | collective-permute-start | bytes 589832 | tf_op jit(solution)/shard_map/ppermute | solution.py:348
  96.5 1.9 %copy-start = (bf16[16,512,192]{2,1,0:T(8,128)(2,1)}, bf16[16,512,192]{2,1,0:T(8,128)(2,1)S(1)}, u32[]{:S(2)}) copy-start(bf16[16,512,192]{2,1,0:T(8,128)(2,1)S(1)} %get-tuple-element.49.turned_ref) | copy-start | bytes 9437188
  98.5 0.8 copy-start.2
  101.6 1.7 %copy-start.1 = (bf16[16,192,512]{2,1,0:T(8,128)(2,1)}, bf16[16,192,512]{2,1,0:T(8,128)(2,1)S(1)}, u32[]{:S(2)}) copy-start(bf16[16,192,512]{2,1,0:T(8,128)(2,1)S(1)} %get-tuple-element.43.row_ref) | copy-start | bytes 9437188
  103.3 0.8 copy-start.3

commit v4 on v3

--- a/solution.py
+++ b/solution.py
@@ -217,13 +217,12 @@
     for flip in range(2):
         for shift in range(4):
             for turn in range(2):
-                own_pair, up, down, *far = part_refs[flip * 5 : flip * 5 + 5]
-                from_ref = (own_pair, up, far[turn], down)[shift]
+                from_ref = part_refs[flip * 4 + shift]
                 point = (z_own + turn) % 2 * 8 + (x_own + 4 - shift) % 4 * 2 + (c_own + flip) % 2
                 for pair in range(4):
                     blocks = []
                     for source in (2 * pair, 2 * pair + 1):
-                        block = (from_ref[source] if shift == 2 else from_ref[turn, source]).astype(F32)
+                        block = from_ref[turn, source].astype(F32)
                         blocks.append(
                             jnp.concatenate([block[24 * group : 24 * group + 24] for group in range(4)], 1)
                         )
@@ -379,7 +378,6 @@
     columns = lax.all_to_all(columns, ALL, 0, 0, axis_index_groups=planes)
     own_part = packed[:, 512:608]
     flipped_part = flip_z(own_part)
-    far_part = along_x(own_part, 2)
     (spread,) = call(
         rows_kernel,
         [((KA, GA, 32, 128), BF16)],
@@ -389,13 +387,13 @@
         far_outs=1,
     )
     spread = spread.reshape(KA * GA, 32, 128)
-    spread, flipped_part, far_part, columns = lax.optimization_barrier((spread, flipped_part, far_part, columns))
+    spread, flipped_part, columns = lax.optimization_barrier((spread, flipped_part, columns))
     own_part = jnp.stack([own_part, flipped_part])
     parts = [along_x(own_part, 1), along_x(own_part, 3)]
     column_parts = along_y(columns)
     spread = lax.all_to_all(spread, ALL, 0, 0)
-    spread, far_part = lax.optimization_barrier((spread, far_part))
-    far_parts = [far_part, flip_z(far_part)]
+    spread, far_part = lax.optimization_barrier((spread, own_part))
+    far_part = along_x(far_part, 2)
     (screen,) = call(
         columns_kernel,
         [((NG, 128), BF16)],
@@ -404,9 +402,9 @@
         place, spread, exact_in, split_in,
         far_outs=1,
     )
-    parts, column_parts, far_parts, screen = lax.optimization_barrier((parts, column_parts, far_parts, screen))
+    parts, column_parts, far_part, screen = lax.optimization_barrier((parts, column_parts, far_part, screen))
     screen = lax.all_to_all(screen.reshape(KA, 256, 128), "ka", 0, 0)
-    parts = [own_part, *parts, *far_parts]
+    parts = [own_part, parts[0], far_part, parts[1]]
     parts += [flip_core(part) for part in parts]
     rows, far = call(
         row_side_kernel, [((KA, 192, 512), BF16), ((KA, 16, 512), F32)], [], 1, own_k, *parts

time: 137 us -> 141 us (1.029)
  waiting for transfers between devices: 19.7 us -> 22.2 us
  blocking collectives: 41 us -> 42.8 us
    all_to_all x1, blocking collectives: 14.9 us -> 16.7 us  [body(): value = jnp.sum(lax.all_to_all(value, ALL, 0, 0, tiled=True), axis=0)]
    all_to_all x1, starting transfers between devices: 6.08 us -> 7.49 us  [body(): spread = lax.all_to_all(spread, ALL, 0, 0)]
    unnamed x18 -> x22, local copies, waits for them, and re-layouts: 5.28 us -> 6.07 us
  transfers between devices with their start and end apart: 16 -> 14, of which waited for: 4 -> 6; matrix products, arithmetic and copies ran while one was open for 1% -> 1% of each run, Pallas kernels for 14% -> 14%
where the time goes in v4:
time: 141 us
  blocking collectives  42.8 us (30%)
  Pallas kernels  34.6 us (25%)
  starting transfers between devices  33.3 us (24%)
  waiting for transfers between devices  22.2 us (16%)
  local copies, waits for them, and re-layouts  6.77 us (5%)
    all_to_all x1, blocking collectives, body(): packed = lax.all_to_all(packed, 'ga', 0, 0)  26 us
    pallas_call x5, Pallas kernels, call(): pl.pallas_call(kernel, out_shape=[jax.ShapeDtypeStruct(shape, kind) for s...  23 us
    all_to_all x1, blocking collectives, body(): value = jnp.sum(lax.all_to_all(value, ALL, 0, 0, tiled=True), axis=0)  16.7 us
    pallas_call x1, Pallas kernels, body(): pl.pallas_call(contract_kernel, out_shape=jax.ShapeDtypeStruct((KA, GA, 1...  11.6 us
    all_to_all x1, waiting for transfers between devices, body(): spread = lax.all_to_all(spread, ALL, 0, 0)  11.6 us
    all_to_all x1, starting transfers between devices, body(): columns = lax.all_to_all(columns, ALL, 0, 0, axis_index_groups=planes)  7.76 us
    all_to_all x1, starting transfers between devices, body(): spread = lax.all_to_all(spread, ALL, 0, 0)  7.49 us
    all_to_all x1, starting transfers between devices, body(): screen = lax.all_to_all(screen.reshape(KA, 256, 128), 'ka', 0, 0)  6.94 us
  transfers between devices with their start and end apart: 14, of which 6 were waited for; matrix products, arithmetic and copies ran while one was open for 1% of the time, Pallas kernels for 14%

profile of v4, /device:TPU:1, one launch (start us, length us, event | category | flops | bytes accessed | tf_op | source)
XLA Modules:
  0.0 140.8 jit_solution(13473148791680488615)
XLA Ops:
  0.0 3.4 %shard_map.82 = (bf16[8,608,128]{2,1,0:T(8,128)(2,1)}, bf16[32,48,128]{2,1,0:T(8,128)(2,1)}) custom-call(s32[1]{0:T(128)} %bitcast.own_ref, f32[2,2,512,256]{3,2,1,0:T(8,128)} %w_hbm.1, f32[9,2,4096]{2,1,0:T(2,128)} %bitcast.13, f32[8,2,4096]{2,1,0:T(2,128)} %bitcast.15), custom_call_target="tpu_custom_call" | custom-call | tf_op jit(solution)/shard_map/pallas_call | solution.py:318
  3.4 0.0 copy-start.9
  3.4 0.0 copy-start.6
  3.4 0.0 copy-start.7
  3.4 26.0 %all_to_all.29.got_ref = bf16[8,608,128]{2,1,0:T(8,128)(2,1)S(1)} all-to-all(bf16[8,608,128]{2,1,0:T(8,128)(2,1)} %get-tuple-element.26), channel_id=1, replica_groups=mesh['ka'=16,'ga'=8] {'ga'}, dimensions={0} | all-to-all | bytes 2490368 | tf_op jit(solution)/shard_map/all_to_all | solution.py:375
  29.4 7.8 %all-to-all-start.1 = ((bf16[32,48,128]{2,1,0:T(8,128)(2,1)}), bf16[32,48,128]{2,1,0:T(8,128)(2,1)S(1)}, u32[]{:S(2)}, u32[]{:S(2)}) async-start(bf16[32,48,128]{2,1,0:T(8,128)(2,1)} %get-tuple-element.29), calls=%async_computation.1 | async-start | bytes 786432 | tf_op jit(solution)/shard_map/all_to_all | solution.py:378
  37.2 0.1 slice_bitcast_fusion
  37.3 1.5 %collective-permute-start = (bf16[8,96,128]{2,1,0:T(8,128)(2,1)S(1)}, bf16[8,96,128]{2,1,0:T(8,128)(2,1)S(1)}, u32[]{:S(2)}, u32[]{:S(2)}) collective-permute-start(bf16[8,96,128]{2,1,0:T(8,128)(2,1)S(1)} %get-tuple-element.48), channel_id=1, source_target_pairs={{0,64},{8,72},{16,80},{24,88},{32,96},{40,104},{48,112},{56,120},{... | collective-permute-start | bytes 589832 | tf_op jit(solution)/shard_map/ppermute | solution.py:331
  38.7 0.0 copy-done.9
  38.8 0.0 copy-done.6
  38.8 0.0 copy-done.7
  38.8 0.0 copy-start.8
  38.8 7.8 %shard_map.83 = bf16[16,8,32,128]{3,2,1,0:T(8,128)(2,1)} custom-call(s32[4096]{0:T(1024)S(1)} %fusion.1.place_ref, bf16[8,608,128]{2,1,0:T(8,128)(2,1)S(1)} %all_to_all.29.got_ref, bf16[128,128]{1,0:T(8,128)(2,1)S(1)} %copy-done.7, bf16[384,256]{1,0:T(8,128)(2,1)S(1)} %copy-done.6), custom_call_target="tpu_custom_call" | custom-call | tf_op jit(solution)/shard_map/pallas_call | solution.py:318
  46.6 1.2 collective-permute-done
  47.9 0.0 all-to-all-done.1.refs_0_
  47.9 7.5 %all-to-all-start.2 = ((bf16[128,32,128]{2,1,0:T(8,128)(2,1)}), bf16[128,32,128]{2,1,0:T(8,128)(2,1)S(1)}, u32[]{:S(2)}, u32[]{:S(2)}) async-start(bf16[128,32,128]{2,1,0:T(8,128)(2,1)} %bitcast.4), calls=%async_computation.2 | async-start | bytes 2097152 | tf_op jit(solution)/shard_map/all_to_all | solution.py:394
  55.4 0.0 copy-start.10
  55.4 2.7 %collective-permute-start.2 = (bf16[2,8,96,128]{3,2,1,0:T(8,128)(2,1)S(1)}, bf16[2,8,96,128]{3,2,1,0:T(8,128)(2,1)}, u32[]{:S(2)}, u32[]{:S(2)}) collective-permute-start(bf16[2,8,96,128]{3,2,1,0:T(8,128)(2,1)S(1)} %pad_maximum_fusion.refs_0_), channel_id=1, source_target_pairs={{0,48},{8,56},{16,0},{24,8},{32,16},{40,24},{48,32},{56,40},{64,11... | collective-permute-start | bytes 1179656 | tf_op jit(solution)/shard_map/ppermute | solution.py:335
  58.1 0.0 collective-permute-start.1
  58.1 2.5 %collective-permute-start.5 = (bf16[32,48,128]{2,1,0:T(8,128)(2,1)S(1)}, bf16[32,48,128]{2,1,0:T(8,128)(2,1)S(1)}, u32[]{:S(2)}, u32[]{:S(2)}) collective-permute-start(bf16[32,48,128]{2,1,0:T(8,128)(2,1)S(1)} %all-to-all-done.1.refs_0_), channel_id=1, source_target_pairs={{0,6},{1,7},{2,0},{3,1},{4,2},{5,3},{6,4},{7,5},{8,14},{9,15},{10,... | collective-permute-start | bytes 1179656 | tf_op jit(solution)/shard_map/ppermute | solution.py:342
  60.6 0.5 collective-permute-start.4
  61.1 0.6 collective-permute-start.3
  61.7 11.6 %all-to-all-done.2.got_ref = bf16[128,32,128]{2,1,0:T(8,128)(2,1)S(1)} async-done(((bf16[128,32,128]{2,1,0:T(8,128)(2,1)}), bf16[128,32,128]{2,1,0:T(8,128)(2,1)S(1)}, u32[]{:S(2)}, u32[]{:S(2)}) %all-to-all-start.2) | async-done | bytes 1048608 | tf_op jit(solution)/shard_map/all_to_all | solution.py:394
  73.3 3.3 %collective-permute-done.2.refs_3_ = bf16[2,8,96,128]{3,2,1,0:T(8,128)(2,1)} collective-permute-done((bf16[2,8,96,128]{3,2,1,0:T(8,128)(2,1)S(1)}, bf16[2,8,96,128]{3,2,1,0:T(8,128)(2,1)}, u32[]{:S(2)}, u32[]{:S(2)}) %collective-permute-start.2) | collective-permute-done | bytes 393248 | tf_op jit(solution)/shard_map/ppermute | solution.py:335
  76.6 2.4 %collective-permute-start.6 = (bf16[2,8,96,128]{3,2,1,0:T(8,128)(2,1)S(1)}, bf16[2,8,96,128]{3,2,1,0:T(8,128)(2,1)S(1)}, u32[]{:S(2)}, u32[]{:S(2)}) collective-permute-start(bf16[2,8,96,128]{3,2,1,0:T(8,128)(2,1)S(1)} %pad_maximum_fusion.refs_0_), channel_id=1, source_target_pairs={{0,32},{8,40},{16,48},{24,56},{32,0},{40,8},{48,16},{56,24},{64,96... | collective-permute-start | bytes 1179656 | tf_op jit(solution)/shard_map/ppermute | solution.py:335
  79.0 0.0 copy-done.8
  79.0 7.5 %shard_map.84 = bf16[4096,128]{1,0:T(8,128)(2,1)} custom-call(s32[4096]{0:T(1024)S(1)} %fusion.1.place_ref, bf16[128,32,128]{2,1,0:T(8,128)(2,1)S(1)} %all-to-all-done.2.got_ref, bf16[128,128]{1,0:T(8,128)(2,1)S(1)} %copy-done.7, bf16[128,192]{1,0:T(8,128)(2,1)S(1)} %copy-done.8), custom_call_target="tpu_custom_call" | custom-call | tf_op jit(solution)/shard_map/pallas_call | solution.py:318
  86.6 0.0 collective-permute-done.1.refs_1_
  86.6 0.0 collective-permute-done.5.refs_3_
  86.6 0.0 collective-permute-done.4.refs_2_
  86.6 0.4 collective-permute-done.3.refs_1_
  87.0 0.9 collective-permute-done.6.refs_2_
  87.9 0.0 copy-start.4
  87.9 0.8 copy-done.4
  88.7 0.0 copy-start.5
  88.7 6.9 %all-to-all-start.3 = ((bf16[16,256,128]{2,1,0:T(8,128)(2,1)}), bf16[16,256,128]{2,1,0:T(8,128)(2,1)}, u32[]{:S(2)}, u32[]{:S(2)}) async-start(bf16[16,256,128]{2,1,0:T(8,128)(2,1)} %bitcast.6), calls=%async_computation.3 | async-start | bytes 2097152 | tf_op jit(solution)/shard_map/all_to_all | solution.py:406
  95.6 0.2 collective-permute-start.7
  95.9 0.3 collective-permute-start.8
  96.1 0.0 copy-done.5
  96.1 0.2 collective-permute-start.9
  96.4 0.3 collective-permute-start.10
  96.6 0.0 copy-done.10
  96.7 0.6 select_reduce_fusion.point_ref
  97.3 1.8 %shard_map.86 = (bf16[16,512,192]{2,1,0:T(8,128)(2,1)S(1)}, bf16[16,32,512]{2,1,0:T(8,128)(2,1)S(1)}) custom-call(s32[1]{0:T(128)} %bitcast.own_ref, bf16[32,48,128]{2,1,0:T(8,128)(2,1)S(1)} %all-to-all-done.1.refs_0_, bf16[32,48,128]{2,1,0:T(8,128)(2,1)S(1)} %collective-permute-done.3.refs_1_, bf16[32,48,128]{2,1,0:T(8,128)(2,1)S(1)} %collective-permute-done.4.refs_2_, ...), custom_call_target="tpu_custom_call" | custom-call | tf_op jit(solution)/shard_map/pallas_call | solution.py:318
  99.1 0.0 copy-start
  99.1 1.9 %copy-done = bf16[16,512,192]{2,1,0:T(8,128)(2,1)} copy-done((bf16[16,512,192]{2,1,0:T(8,128)(2,1)}, bf16[16,512,192]{2,1,0:T(8,128)(2,1)S(1)}, u32[]{:S(2)}) %copy-start) | copy-done | bytes 3145752
  101.1 0.0 copy-start.2
  101.1 0.8 copy-done.2
  101.9 0.0 collective-permute-done.7.refs_4_
  101.9 0.0 collective-permute-done.8.refs_5_
  101.9 0.0 collective-permute-done.9.refs_6_
  101.9 0.0 collective-permute-done.10.refs_7_
  101.9 2.4 %shard_map.85 = (bf16[16,192,512]{2,1,0:T(8,128)(2,1)S(1)}, f32[16,16,512]{2,1,0:T(8,128)S(1)}) custom-call(s32[1]{0:T(128)} %bitcast.7.own_ref, bf16[2,8,96,128]{3,2,1,0:T(8,128)(2,1)S(1)} %pad_maximum_fusion.refs_0_, bf16[2,8,96,128]{3,2,1,0:T(8,128)(2,1)} %collective-permute-done.1.refs_1_, bf16[2,8,96,128]{3,2,1,0:T(8,128)(2,1)S(1)} %copy-done.5, ...), custom_call_target="tpu_custom_call" | custom-call | tf_op jit(solution)/shard_map/pallas_call | solution.py:318
  104.3 0.0 copy-start.1
  104.3 1.7 %copy-done.1 = bf16[16,192,512]{2,1,0:T(8,128)(2,1)} copy-done((bf16[16,192,512]{2,1,0:T(8,128)(2,1)}, bf16[16,192,512]{2,1,0:T(8,128)(2,1)S(1)}, u32[]{:S(2)}) %copy-start.1) | copy-done | bytes 3145752
  106.0 0.0 copy-start.3
  106.0 0.8 copy-done.3
  106.8 4.7 %all-to-all-done.3.screen_ref = bf16[16,256,128]{2,1,0:T(8,128)(2,1)} async-done(((bf16[16,256,128]{2,1,0:T(8,128)(2,1)}), bf16[16,256,128]{2,1,0:T(8,128)(2,1)}, u32[]{:S(2)}, u32[]{:S(2)}) %all-to-all-start.3) | async-done | bytes 1048608 | tf_op jit(solution)/shard_map/all_to_all | solution.py:406
  111.6 11.6 %shard_map.87 = f32[16,8,16]{2,1,0:T(8,128)} custom-call(s32[2,16]{1,0:T(2,128)} %select_reduce_fusion.point_ref, bf16[16,256,128]{2,1,0:T(8,128)(2,1)} %all-to-all-done.3.screen_ref, bf16[16,192,512]{2,1,0:T(8,128)(2,1)} %copy-done.1, f32[16,16,512]{2,1,0:T(8,128)} %copy-done.3, bf16[16,512,192]{2,1,0:T(8,128)(2,1)} %copy-done, bf16[16,32,512]{2,1,0:T(8,128)(2,1)} %copy-done.2), custom_call_target="tpu_custom_call" | custom-call | tf_op jit(solution)/shard_map/pallas_call | solution.py:418
  123.2 16.7 %all_to_all.30 = f32[128,1,16]{2,1,0:T(1,128)S(1)} all-to-all(f32[128,1,16]{2,1,0:T(1,128)} %bitcast.14), channel_id=1, replica_groups=mesh['ka'=16,'ga'=8] {'ka','ga'}, dimensions={0} | all-to-all | bytes 16384 | tf_op jit(solution)/shard_map/all_to_all | solution.py:435
  140.0 0.2 reduce_sum.19
  140.1 0.6 mul.20
  (3 shorter events, 0.1 us)
Async XLA Ops:
  3.4 35.4 %copy-start.9 = (s32[4096]{0:T(1024)S(1)}, s32[4096]{0:T(1024)}, u32[]{:S(2)}) copy-start(s32[4096]{0:T(1024)} %param.12) | copy-start | bytes 49156
  3.4 35.4 %copy-start.6 = (bf16[384,256]{1,0:T(8,128)(2,1)S(1)}, bf16[384,256]{1,0:T(8,128)(2,1)}, u32[]{:S(2)}) copy-start(bf16[384,256]{1,0:T(8,128)(2,1)} %constant.51.clone.turned_ref) | copy-start | bytes 589828
  3.4 35.4 %copy-start.7 = (bf16[128,128]{1,0:T(8,128)(2,1)S(1)}, bf16[128,128]{1,0:T(8,128)(2,1)}, u32[]{:S(2)}) copy-start(bf16[128,128]{1,0:T(8,128)(2,1)} %constant.49.clone.exact_ref) | copy-start | bytes 98308
  29.4 18.5 %all-to-all-start.1 = ((bf16[32,48,128]{2,1,0:T(8,128)(2,1)}), bf16[32,48,128]{2,1,0:T(8,128)(2,1)S(1)}, u32[]{:S(2)}, u32[]{:S(2)}) async-start(bf16[32,48,128]{2,1,0:T(8,128)(2,1)} %get-tuple-element.29), calls=%async_computation.1 | async-start | bytes 786432 | tf_op jit(solution)/shard_map/all_to_all | solution.py:378
  37.3 10.6 %collective-permute-start = (bf16[8,96,128]{2,1,0:T(8,128)(2,1)S(1)}, bf16[8,96,128]{2,1,0:T(8,128)(2,1)S(1)}, u32[]{:S(2)}, u32[]{:S(2)}) collective-permute-start(bf16[8,96,128]{2,1,0:T(8,128)(2,1)S(1)} %get-tuple-element.48), channel_id=1, source_target_pairs={{0,64},{8,72},{16,80},{24,88},{32,96},{40,104},{48,112},{56,120},{... | collective-permute-start | bytes 589832 | tf_op jit(solution)/shard_map/ppermute | solution.py:331
  38.8 40.3 %copy-start.8 = (bf16[128,192]{1,0:T(8,128)(2,1)S(1)}, bf16[128,192]{1,0:T(8,128)(2,1)}, u32[]{:S(2)}) copy-start(bf16[128,192]{1,0:T(8,128)(2,1)} %constant.50.clone.split_ref) | copy-start | bytes 147460
  47.9 25.4 %all-to-all-start.2 = ((bf16[128,32,128]{2,1,0:T(8,128)(2,1)}), bf16[128,32,128]{2,1,0:T(8,128)(2,1)S(1)}, u32[]{:S(2)}, u32[]{:S(2)}) async-start(bf16[128,32,128]{2,1,0:T(8,128)(2,1)} %bitcast.4), calls=%async_computation.2 | async-start | bytes 2097152 | tf_op jit(solution)/shard_map/all_to_all | solution.py:394
  55.4 41.2 %copy-start.10 = (s32[2,16]{1,0:T(2,128)S(1)}, s32[2,16]{1,0:T(2,128)}, u32[]{:S(2)}) copy-start(s32[2,16]{1,0:T(2,128)} %param.11) | copy-start | bytes 388
  55.4 21.2 %collective-permute-start.2 = (bf16[2,8,96,128]{3,2,1,0:T(8,128)(2,1)S(1)}, bf16[2,8,96,128]{3,2,1,0:T(8,128)(2,1)}, u32[]{:S(2)}, u32[]{:S(2)}) collective-permute-start(bf16[2,8,96,128]{3,2,1,0:T(8,128)(2,1)S(1)} %pad_maximum_fusion.refs_0_), channel_id=1, source_target_pairs={{0,48},{8,56},{16,0},{24,8},{32,16},{40,24},{48,32},{56,40},{64,11... | collective-permute-start | bytes 1179656 | tf_op jit(solution)/shard_map/ppermute | solution.py:335
  58.1 28.5 %collective-permute-start.1 = (bf16[2,8,96,128]{3,2,1,0:T(8,128)(2,1)S(1)}, bf16[2,8,96,128]{3,2,1,0:T(8,128)(2,1)}, u32[]{:S(2)}, u32[]{:S(2)}) collective-permute-start(bf16[2,8,96,128]{3,2,1,0:T(8,128)(2,1)S(1)} %pad_maximum_fusion.refs_0_), channel_id=1, source_target_pairs={{0,16},{8,24},{16,32},{24,40},{32,48},{40,56},{48,0},{56,8},{64,80... | collective-permute-start | bytes 1179656 | tf_op jit(solution)/shard_map/ppermute | solution.py:335
  58.1 28.5 %collective-permute-start.5 = (bf16[32,48,128]{2,1,0:T(8,128)(2,1)S(1)}, bf16[32,48,128]{2,1,0:T(8,128)(2,1)S(1)}, u32[]{:S(2)}, u32[]{:S(2)}) collective-permute-start(bf16[32,48,128]{2,1,0:T(8,128)(2,1)S(1)} %all-to-all-done.1.refs_0_), channel_id=1, source_target_pairs={{0,6},{1,7},{2,0},{3,1},{4,2},{5,3},{6,4},{7,5},{8,14},{9,15},{10,... | collective-permute-start | bytes 1179656 | tf_op jit(solution)/shard_map/ppermute | solution.py:342
  60.6 26.0 %collective-permute-start.4 = (bf16[32,48,128]{2,1,0:T(8,128)(2,1)S(1)}, bf16[32,48,128]{2,1,0:T(8,128)(2,1)S(1)}, u32[]{:S(2)}, u32[]{:S(2)}) collective-permute-start(bf16[32,48,128]{2,1,0:T(8,128)(2,1)S(1)} %all-to-all-done.1.refs_0_), channel_id=1, source_target_pairs={{0,4},{1,5},{2,6},{3,7},{4,0},{5,1},{6,2},{7,3},{8,12},{9,13},{10,... | collective-permute-start | bytes 1179656 | tf_op jit(solution)/shard_map/ppermute | solution.py:342
  61.1 25.9 %collective-permute-start.3 = (bf16[32,48,128]{2,1,0:T(8,128)(2,1)S(1)}, bf16[32,48,128]{2,1,0:T(8,128)(2,1)S(1)}, u32[]{:S(2)}, u32[]{:S(2)}) collective-permute-start(bf16[32,48,128]{2,1,0:T(8,128)(2,1)S(1)} %all-to-all-done.1.refs_0_), channel_id=1, source_target_pairs={{0,2},{1,3},{2,4},{3,5},{4,6},{5,7},{6,0},{7,1},{8,10},{9,11},{10,... | collective-permute-start | bytes 1179656 | tf_op jit(solution)/shard_map/ppermute | solution.py:342
  76.6 11.3 %collective-permute-start.6 = (bf16[2,8,96,128]{3,2,1,0:T(8,128)(2,1)S(1)}, bf16[2,8,96,128]{3,2,1,0:T(8,128)(2,1)S(1)}, u32[]{:S(2)}, u32[]{:S(2)}) collective-permute-start(bf16[2,8,96,128]{3,2,1,0:T(8,128)(2,1)S(1)} %pad_maximum_fusion.refs_0_), channel_id=1, source_target_pairs={{0,32},{8,40},{16,48},{24,56},{32,0},{40,8},{48,16},{56,24},{64,96... | collective-permute-start | bytes 1179656 | tf_op jit(solution)/shard_map/ppermute | solution.py:335
  87.9 0.8 copy-start.4
  88.7 7.5 %copy-start.5 = (bf16[2,8,96,128]{3,2,1,0:T(8,128)(2,1)S(1)}, bf16[2,8,96,128]{3,2,1,0:T(8,128)(2,1)}, u32[]{:S(2)}) copy-start(bf16[2,8,96,128]{3,2,1,0:T(8,128)(2,1)} %copy-done.4) | copy-start | bytes 1179652
  88.7 22.9 %all-to-all-start.3 = ((bf16[16,256,128]{2,1,0:T(8,128)(2,1)}), bf16[16,256,128]{2,1,0:T(8,128)(2,1)}, u32[]{:S(2)}, u32[]{:S(2)}) async-start(bf16[16,256,128]{2,1,0:T(8,128)(2,1)} %bitcast.6), calls=%async_computation.3 | async-start | bytes 2097152 | tf_op jit(solution)/shard_map/all_to_all | solution.py:406
  95.6 6.2 %collective-permute-start.7 = (bf16[2,8,96,128]{3,2,1,0:T(8,128)(2,1)S(1)}, bf16[2,8,96,128]{3,2,1,0:T(8,128)(2,1)S(1)}, u32[]{:S(2)}, u32[]{:S(2)}) collective-permute-start(bf16[2,8,96,128]{3,2,1,0:T(8,128)(2,1)S(1)} %pad_maximum_fusion.refs_0_), channel_id=1, source_target_pairs={{0,8},{8,0},{16,24},{24,16},{32,40},{40,32},{48,56},{56,48},{64,72... | collective-permute-start | bytes 1179656 | tf_op jit(solution)/shard_map/ppermute | solution.py:347
  95.9 6.0 %collective-permute-start.8 = (bf16[2,8,96,128]{3,2,1,0:T(8,128)(2,1)}, bf16[2,8,96,128]{3,2,1,0:T(8,128)(2,1)S(1)}, u32[]{:S(2)}, u32[]{:S(2)}) collective-permute-start(bf16[2,8,96,128]{3,2,1,0:T(8,128)(2,1)} %collective-permute-done.1.refs_1_), channel_id=1, source_target_pairs={{0,8},{8,0},{16,24},{24,16},{32,40},{40,32},{48,56},{56,48},{64,72... | collective-permute-start | bytes 1179656 | tf_op jit(solution)/shard_map/ppermute | solution.py:347
  96.1 5.7 %collective-permute-start.9 = (bf16[2,8,96,128]{3,2,1,0:T(8,128)(2,1)S(1)}, bf16[2,8,96,128]{3,2,1,0:T(8,128)(2,1)}, u32[]{:S(2)}, u32[]{:S(2)}) collective-permute-start(bf16[2,8,96,128]{3,2,1,0:T(8,128)(2,1)S(1)} %copy-done.5), channel_id=1, source_target_pairs={{0,8},{8,0},{16,24},{24,16},{32,40},{40,32},{48,56},{56,48},{64,72... | collective-permute-start | bytes 1179656 | tf_op jit(solution)/shard_map/ppermute | solution.py:347
  96.4 5.5 %collective-permute-start.10 = (bf16[2,8,96,128]{3,2,1,0:T(8,128)(2,1)}, bf16[2,8,96,128]{3,2,1,0:T(8,128)(2,1)}, u32[]{:S(2)}, u32[]{:S(2)}) collective-permute-start(bf16[2,8,96,128]{3,2,1,0:T(8,128)(2,1)} %collective-permute-done.2.refs_3_), channel_id=1, source_target_pairs={{0,8},{8,0},{16,24},{24,16},{32,40},{40,32},{48,56},{56,48},{64,72... | collective-permute-start | bytes 1179656 | tf_op jit(solution)/shard_map/ppermute | solution.py:347
  99.1 1.9 %copy-start = (bf16[16,512,192]{2,1,0:T(8,128)(2,1)}, bf16[16,512,192]{2,1,0:T(8,128)(2,1)S(1)}, u32[]{:S(2)}) copy-start(bf16[16,512,192]{2,1,0:T(8,128)(2,1)S(1)} %get-tuple-element.45.turned_ref) | copy-start | bytes 9437188
  101.1 0.8 copy-start.2
  104.3 1.7 %copy-start.1 = (bf16[16,192,512]{2,1,0:T(8,128)(2,1)}, bf16[16,192,512]{2,1,0:T(8,128)(2,1)S(1)}, u32[]{:S(2)}) copy-start(bf16[16,192,512]{2,1,0:T(8,128)(2,1)S(1)} %get-tuple-element.39.row_ref) | copy-start | bytes 9437188
  106.0 0.8 copy-start.3

commit v5 on v3

--- a/solution.py
+++ b/solution.py
@@ -310,6 +310,7 @@
     @pl.when(first == KA - 4)
     def _():
         value = jnp.sum(sum_ref[...], axis=2)
+        value = value * (-1.0 / (QSTEPS * MB * math.sqrt(NG) * NG))
         out_ref[...] = jnp.broadcast_to(value[:, None, :], (KA, GA, 16))
 
 
@@ -394,8 +395,9 @@
     parts = [along_x(own_part, 1), along_x(own_part, 3)]
     column_parts = along_y(columns)
     spread = lax.all_to_all(spread, ALL, 0, 0)
-    spread, far_part = lax.optimization_barrier((spread, far_part))
     far_parts = [far_part, flip_z(far_part)]
+    spread, columns = lax.optimization_barrier((spread, columns))
+    column_parts[2] = along_y(columns)[2]
     (screen,) = call(
         columns_kernel,
         [((NG, 128), BF16)],
@@ -434,8 +436,8 @@
         compiler_params=pltpu.CompilerParams(vmem_limit_bytes=WHOLE_VMEM),
     )(owners, screen, rows, far, near, left)
     value = partial.reshape(KA * GA, 16)
-    value = jnp.sum(lax.all_to_all(value, ALL, 0, 0, tiled=True), axis=0)
-    return value.reshape(2, 1, NBD) * (-1.0 / (QSTEPS * MB * math.sqrt(NG) * NG))
+    value = lax.all_to_all(value, ALL, 0, 0, tiled=True).reshape(KA * GA, 2, 1, NBD)
+    return jnp.sum(value, axis=0)
 
 
 def solution(mesh):

time: 137 us -> 137 us (level)
    ppermute x3, waiting for transfers between devices: 3.32 us -> 0.01 us  [along_x(): lax.ppermute(part, 'ka', [(index, index // 8 * 8 + (index + 2 * shift) %...]
    ppermute x3, waiting for transfers between devices: 1.05 us -> 4.01 us  [along_y(): parts.append(lax.ppermute(part, 'ga', along))]
    ppermute x3, starting transfers between devices: 3.58 us -> 4.98 us  [along_y(): parts.append(lax.ppermute(part, 'ga', along))]
    unnamed x18 -> x20, local copies, waits for them, and re-layouts: 5.28 us -> 5.27 us
  transfers between devices with their start and end apart: 16 -> 16, of which waited for: 4 -> 3; matrix products, arithmetic and copies ran while one was open for 1% -> 2% of each run, Pallas kernels for 14% -> 14%
where the time goes in v5:
time: 137 us; the launch traced here: 136 us
  blocking collectives  40.7 us (30%)
  Pallas kernels  34.5 us (25%)
  starting transfers between devices  33.6 us (25%)
  waiting for transfers between devices  18.8 us (14%)
  local copies, waits for them, and re-layouts  6.63 us (5%)
  other arithmetic  1.78 us (1%)
    all_to_all x1, blocking collectives, body(): packed = lax.all_to_all(packed, 'ga', 0, 0)  26 us
    pallas_call x5, Pallas kernels, call(): pl.pallas_call(kernel, out_shape=[jax.ShapeDtypeStruct(shape, kind) for s...  22.9 us
    all_to_all x1, blocking collectives, body(): lax.all_to_all(value, ALL, 0, 0, tiled=True).reshape(KA * GA, 2, 1, NBD)  14.7 us
    pallas_call x1, Pallas kernels, body(): pl.pallas_call(contract_kernel, out_shape=jax.ShapeDtypeStruct((KA, GA, 1...  11.6 us
    all_to_all x1, waiting for transfers between devices, body(): spread = lax.all_to_all(spread, ALL, 0, 0)  10.1 us
    all_to_all x1, starting transfers between devices, body(): columns = lax.all_to_all(columns, ALL, 0, 0, axis_index_groups=planes)  7.76 us
    all_to_all x1, starting transfers between devices, body(): spread = lax.all_to_all(spread, ALL, 0, 0)  5.72 us
    all_to_all x1, starting transfers between devices, body(): screen = lax.all_to_all(screen.reshape(KA, 256, 128), 'ka', 0, 0)  5.62 us
  transfers between devices with their start and end apart: 16, of which 3 were waited for; matrix products, arithmetic and copies ran while one was open for 2% of the time, Pallas kernels for 14%

profile of v5, /device:TPU:1, one launch (start us, length us, event | category | flops | bytes accessed | tf_op | source)
XLA Modules:
  0.0 136.2 jit_solution(761011533903170160)
XLA Ops:
  0.0 3.4 %shard_map.82 = (bf16[8,608,128]{2,1,0:T(8,128)(2,1)}, bf16[32,48,128]{2,1,0:T(8,128)(2,1)}) custom-call(s32[1]{0:T(128)} %bitcast.own_ref, f32[2,2,512,256]{3,2,1,0:T(8,128)} %w_hbm.1, f32[9,2,4096]{2,1,0:T(2,128)} %bitcast.13, f32[8,2,4096]{2,1,0:T(2,128)} %bitcast.15), custom_call_target="tpu_custom_call" | custom-call | tf_op jit(solution)/shard_map/pallas_call | solution.py:320
  3.4 0.0 copy-start.8
  3.4 0.0 copy-start.4
  3.4 0.0 copy-start.5
  3.4 26.0 %all_to_all.29.got_ref = bf16[8,608,128]{2,1,0:T(8,128)(2,1)S(1)} all-to-all(bf16[8,608,128]{2,1,0:T(8,128)(2,1)} %get-tuple-element.28), channel_id=1, replica_groups=mesh['ka'=16,'ga'=8] {'ga'}, dimensions={0} | all-to-all | bytes 2490368 | tf_op jit(solution)/shard_map/all_to_all | solution.py:377
  29.4 7.8 %all-to-all-start.1 = ((bf16[32,48,128]{2,1,0:T(8,128)(2,1)}), bf16[32,48,128]{2,1,0:T(8,128)(2,1)S(1)}, u32[]{:S(2)}, u32[]{:S(2)}) async-start(bf16[32,48,128]{2,1,0:T(8,128)(2,1)} %get-tuple-element.31), calls=%async_computation.1 | async-start | bytes 786432 | tf_op jit(solution)/shard_map/all_to_all | solution.py:380
  37.2 0.7 slice_bitcast_fusion
  37.9 1.4 %collective-permute-start = (bf16[8,96,128]{2,1,0:T(8,128)(2,1)S(1)}, bf16[8,96,128]{2,1,0:T(8,128)(2,1)}, u32[]{:S(2)}, u32[]{:S(2)}) collective-permute-start(bf16[8,96,128]{2,1,0:T(8,128)(2,1)S(1)} %get-tuple-element.52), channel_id=1, source_target_pairs={{0,64},{8,72},{16,80},{24,88},{32,96},{40,104},{48,112},{56,120},{... | collective-permute-start | bytes 589832 | tf_op jit(solution)/shard_map/ppermute | solution.py:333
  39.3 2.7 %collective-permute-start.1 = (bf16[8,96,128]{2,1,0:T(8,128)(2,1)S(1)}, bf16[8,96,128]{2,1,0:T(8,128)(2,1)S(1)}, u32[]{:S(2)}, u32[]{:S(2)}) collective-permute-start(bf16[8,96,128]{2,1,0:T(8,128)(2,1)S(1)} %get-tuple-element.52), channel_id=1, source_target_pairs={{0,32},{8,40},{16,48},{24,56},{32,0},{40,8},{48,16},{56,24},{64,96... | collective-permute-start | bytes 589832 | tf_op jit(solution)/shard_map/ppermute | solution.py:337
  42.0 0.0 copy-done.8
  42.0 0.0 copy-done.4
  42.1 0.0 copy-done.5
  42.1 0.0 copy-start.6
  42.1 7.9 %shard_map.83 = bf16[16,8,32,128]{3,2,1,0:T(8,128)(2,1)} custom-call(s32[4096]{0:T(1024)S(1)} %fusion.1.place_ref, bf16[8,608,128]{2,1,0:T(8,128)(2,1)S(1)} %all_to_all.29.got_ref, bf16[128,128]{1,0:T(8,128)(2,1)S(1)} %copy-done.5, bf16[384,256]{1,0:T(8,128)(2,1)S(1)} %copy-done.4), custom_call_target="tpu_custom_call" | custom-call | tf_op jit(solution)/shard_map/pallas_call | solution.py:320
  49.9 0.0 copy-start.7
  50.0 0.0 collective-permute-done
  50.0 0.0 collective-permute-done.1.refs_3_
  50.0 0.0 all-to-all-done.1.refs_0_
  50.0 5.7 %all-to-all-start.2 = ((bf16[128,32,128]{2,1,0:T(8,128)(2,1)}), bf16[128,32,128]{2,1,0:T(8,128)(2,1)S(1)}, u32[]{:S(2)}, u32[]{:S(2)}) async-start(bf16[128,32,128]{2,1,0:T(8,128)(2,1)} %bitcast.4), calls=%async_computation.2 | async-start | bytes 2097152 | tf_op jit(solution)/shard_map/all_to_all | solution.py:397
  55.7 1.6 %collective-permute-start.7 = (bf16[8,96,128]{2,1,0:T(8,128)(2,1)S(1)}, bf16[8,96,128]{2,1,0:T(8,128)(2,1)S(1)}, u32[]{:S(2)}, u32[]{:S(2)}) collective-permute-start(bf16[8,96,128]{2,1,0:T(8,128)(2,1)S(1)} %collective-permute-done.1.refs_3_), channel_id=1, source_target_pairs={{0,64},{8,72},{16,80},{24,88},{32,96},{40,104},{48,112},{56,120},{... | collective-permute-start | bytes 589832 | tf_op jit(solution)/shard_map/ppermute | solution.py:333
  57.3 0.0 copy-done.7
  57.3 1.0 pad_maximum_fusion.refs_0_
  58.3 0.0 copy-start.9
  58.3 2.5 %collective-permute-start.3 = (bf16[2,8,96,128]{3,2,1,0:T(8,128)(2,1)S(1)}, bf16[2,8,96,128]{3,2,1,0:T(8,128)(2,1)}, u32[]{:S(2)}, u32[]{:S(2)}) collective-permute-start(bf16[2,8,96,128]{3,2,1,0:T(8,128)(2,1)S(1)} %pad_maximum_fusion.refs_0_), channel_id=1, source_target_pairs={{0,48},{8,56},{16,0},{24,8},{32,16},{40,24},{48,32},{56,40},{64,11... | collective-permute-start | bytes 1179656 | tf_op jit(solution)/shard_map/ppermute | solution.py:337
  60.8 0.0 collective-permute-start.2
  60.8 2.6 %collective-permute-start.6 = (bf16[32,48,128]{2,1,0:T(8,128)(2,1)S(1)}, bf16[32,48,128]{2,1,0:T(8,128)(2,1)S(1)}, u32[]{:S(2)}, u32[]{:S(2)}) collective-permute-start(bf16[32,48,128]{2,1,0:T(8,128)(2,1)S(1)} %all-to-all-done.1.refs_0_), channel_id=1, source_target_pairs={{0,6},{1,7},{2,0},{3,1},{4,2},{5,3},{6,4},{7,5},{8,14},{9,15},{10,... | collective-permute-start | bytes 1179656 | tf_op jit(solution)/shard_map/ppermute | solution.py:344
  63.4 0.0 collective-permute-start.4
  63.4 10.1 %all-to-all-done.2.got_ref = bf16[128,32,128]{2,1,0:T(8,128)(2,1)S(1)} async-done(((bf16[128,32,128]{2,1,0:T(8,128)(2,1)}), bf16[128,32,128]{2,1,0:T(8,128)(2,1)S(1)}, u32[]{:S(2)}, u32[]{:S(2)}) %all-to-all-start.2) | async-done | bytes 1048608 | tf_op jit(solution)/shard_map/all_to_all | solution.py:397
  73.5 0.0 collective-permute-done.7.refs_4_
  73.5 2.4 %collective-permute-start.5 = (bf16[32,48,128]{2,1,0:T(8,128)(2,1)S(1)}, bf16[32,48,128]{2,1,0:T(8,128)(2,1)S(1)}, u32[]{:S(2)}, u32[]{:S(2)}) collective-permute-start(bf16[32,48,128]{2,1,0:T(8,128)(2,1)S(1)} %all-to-all-done.1.refs_0_), channel_id=1, source_target_pairs={{0,4},{1,5},{2,6},{3,7},{4,0},{5,1},{6,2},{7,3},{8,12},{9,13},{10,... | collective-permute-start | bytes 1179656 | tf_op jit(solution)/shard_map/ppermute | solution.py:344
  75.9 0.0 copy-done.6
  75.9 7.5 %shard_map.84 = bf16[4096,128]{1,0:T(8,128)(2,1)} custom-call(s32[4096]{0:T(1024)S(1)} %fusion.1.place_ref, bf16[128,32,128]{2,1,0:T(8,128)(2,1)S(1)} %all-to-all-done.2.got_ref, bf16[128,128]{1,0:T(8,128)(2,1)S(1)} %copy-done.5, bf16[128,192]{1,0:T(8,128)(2,1)S(1)} %copy-done.6), custom_call_target="tpu_custom_call" | custom-call | tf_op jit(solution)/shard_map/pallas_call | solution.py:320
  83.5 0.0 collective-permute-done.3.refs_2_
  83.5 0.0 collective-permute-done.2.refs_1_
  83.5 0.0 collective-permute-done.6.refs_3_
  83.5 0.0 collective-permute-done.4.refs_1_
  83.5 4.0 %collective-permute-done.5.refs_2_ = bf16[32,48,128]{2,1,0:T(8,128)(2,1)S(1)} collective-permute-done((bf16[32,48,128]{2,1,0:T(8,128)(2,1)S(1)}, bf16[32,48,128]{2,1,0:T(8,128)(2,1)S(1)}, u32[]{:S(2)}, u32[]{:S(2)}) %collective-permute-start.5) | collective-permute-done | bytes 393248 | tf_op jit(solution)/shard_map/ppermute | solution.py:344
  87.5 5.6 %all-to-all-start.3 = ((bf16[16,256,128]{2,1,0:T(8,128)(2,1)}), bf16[16,256,128]{2,1,0:T(8,128)(2,1)}, u32[]{:S(2)}, u32[]{:S(2)}) async-start(bf16[16,256,128]{2,1,0:T(8,128)(2,1)} %bitcast.6), calls=%async_computation.3 | async-start | bytes 2097152 | tf_op jit(solution)/shard_map/all_to_all | solution.py:410
  93.1 0.2 collective-permute-start.8
  93.4 0.3 collective-permute-start.9
  93.7 0.3 collective-permute-start.10
  93.9 0.2 collective-permute-start.11
  94.2 0.3 collective-permute-start.12
  94.4 0.0 copy-done.9
  94.4 0.6 select_reduce_fusion.point_ref
  95.1 1.8 %shard_map.86 = (bf16[16,512,192]{2,1,0:T(8,128)(2,1)S(1)}, bf16[16,32,512]{2,1,0:T(8,128)(2,1)S(1)}) custom-call(s32[1]{0:T(128)} %bitcast.own_ref, bf16[32,48,128]{2,1,0:T(8,128)(2,1)S(1)} %all-to-all-done.1.refs_0_, bf16[32,48,128]{2,1,0:T(8,128)(2,1)S(1)} %collective-permute-done.4.refs_1_, bf16[32,48,128]{2,1,0:T(8,128)(2,1)S(1)} %collective-permute-done.5.refs_2_, ...), custom_call_target="tpu_custom_call" | custom-call | tf_op jit(solution)/shard_map/pallas_call | solution.py:320
  96.9 0.0 copy-start
  96.9 1.9 %copy-done = bf16[16,512,192]{2,1,0:T(8,128)(2,1)} copy-done((bf16[16,512,192]{2,1,0:T(8,128)(2,1)}, bf16[16,512,192]{2,1,0:T(8,128)(2,1)S(1)}, u32[]{:S(2)}) %copy-start) | copy-done | bytes 3145752
  98.9 0.0 copy-start.2
  98.9 0.8 copy-done.2
  99.7 0.0 collective-permute-done.8.refs_5_
  99.7 0.0 collective-permute-done.11.refs_8_
  99.7 0.0 collective-permute-done.12.refs_9_
  99.7 0.0 collective-permute-done.9.refs_6_
  99.7 0.0 collective-permute-done.10.refs_7_
  99.7 2.3 %shard_map.85 = (bf16[16,192,512]{2,1,0:T(8,128)(2,1)S(1)}, f32[16,16,512]{2,1,0:T(8,128)S(1)}) custom-call(s32[1]{0:T(128)} %bitcast.7.own_ref, bf16[2,8,96,128]{3,2,1,0:T(8,128)(2,1)S(1)} %pad_maximum_fusion.refs_0_, bf16[2,8,96,128]{3,2,1,0:T(8,128)(2,1)} %collective-permute-done.2.refs_1_, bf16[2,8,96,128]{3,2,1,0:T(8,128)(2,1)} %collective-permute-done.3.refs_2_, ...), custom_call_target="tpu_custom_call" | custom-call | tf_op jit(solution)/shard_map/pallas_call | solution.py:320
  102.0 0.0 copy-start.1
  102.0 1.7 %copy-done.1 = bf16[16,192,512]{2,1,0:T(8,128)(2,1)} copy-done((bf16[16,192,512]{2,1,0:T(8,128)(2,1)}, bf16[16,192,512]{2,1,0:T(8,128)(2,1)S(1)}, u32[]{:S(2)}) %copy-start.1) | copy-done | bytes 3145752
  103.7 0.8 copy-done.3
  104.5 4.6 %all-to-all-done.3.screen_ref = bf16[16,256,128]{2,1,0:T(8,128)(2,1)} async-done(((bf16[16,256,128]{2,1,0:T(8,128)(2,1)}), bf16[16,256,128]{2,1,0:T(8,128)(2,1)}, u32[]{:S(2)}, u32[]{:S(2)}) %all-to-all-start.3) | async-done | bytes 1048608 | tf_op jit(solution)/shard_map/all_to_all | solution.py:410
  109.1 11.6 %shard_map.87 = f32[16,8,16]{2,1,0:T(8,128)} custom-call(s32[2,16]{1,0:T(2,128)} %select_reduce_fusion.point_ref, bf16[16,256,128]{2,1,0:T(8,128)(2,1)} %all-to-all-done.3.screen_ref, bf16[16,192,512]{2,1,0:T(8,128)(2,1)} %copy-done.1, f32[16,16,512]{2,1,0:T(8,128)} %copy-done.3, bf16[16,512,192]{2,1,0:T(8,128)(2,1)} %copy-done, bf16[16,32,512]{2,1,0:T(8,128)(2,1)} %copy-done.2), custom_call_target="tpu_custom_call" | custom-call | tf_op jit(solution)/shard_map/pallas_call | solution.py:422
  120.7 14.7 %all_to_all.30 = f32[128,1,16]{2,1,0:T(1,128)S(1)} all-to-all(f32[128,1,16]{2,1,0:T(1,128)} %bitcast.14), channel_id=1, replica_groups=mesh['ka'=16,'ga'=8] {'ka','ga'}, dimensions={0} | all-to-all | bytes 16384 | tf_op jit(solution)/shard_map/all_to_all | solution.py:439
  135.4 0.2 reduce_sum.21
  135.6 0.6 reduce_sum.22
  (2 shorter events, 0.0 us)
Async XLA Ops:
  3.4 38.7 %copy-start.8 = (s32[4096]{0:T(1024)S(1)}, s32[4096]{0:T(1024)}, u32[]{:S(2)}) copy-start(s32[4096]{0:T(1024)} %param.12) | copy-start | bytes 49156
  3.4 38.7 %copy-start.4 = (bf16[384,256]{1,0:T(8,128)(2,1)S(1)}, bf16[384,256]{1,0:T(8,128)(2,1)}, u32[]{:S(2)}) copy-start(bf16[384,256]{1,0:T(8,128)(2,1)} %constant.49.clone.turned_ref) | copy-start | bytes 589828
  3.4 38.7 %copy-start.5 = (bf16[128,128]{1,0:T(8,128)(2,1)S(1)}, bf16[128,128]{1,0:T(8,128)(2,1)}, u32[]{:S(2)}) copy-start(bf16[128,128]{1,0:T(8,128)(2,1)} %constant.47.clone.exact_ref) | copy-start | bytes 98308
  29.4 20.6 %all-to-all-start.1 = ((bf16[32,48,128]{2,1,0:T(8,128)(2,1)}), bf16[32,48,128]{2,1,0:T(8,128)(2,1)S(1)}, u32[]{:S(2)}, u32[]{:S(2)}) async-start(bf16[32,48,128]{2,1,0:T(8,128)(2,1)} %get-tuple-element.31), calls=%async_computation.1 | async-start | bytes 786432 | tf_op jit(solution)/shard_map/all_to_all | solution.py:380
  37.9 12.1 %collective-permute-start = (bf16[8,96,128]{2,1,0:T(8,128)(2,1)S(1)}, bf16[8,96,128]{2,1,0:T(8,128)(2,1)}, u32[]{:S(2)}, u32[]{:S(2)}) collective-permute-start(bf16[8,96,128]{2,1,0:T(8,128)(2,1)S(1)} %get-tuple-element.52), channel_id=1, source_target_pairs={{0,64},{8,72},{16,80},{24,88},{32,96},{40,104},{48,112},{56,120},{... | collective-permute-start | bytes 589832 | tf_op jit(solution)/shard_map/ppermute | solution.py:333
  39.3 10.7 %collective-permute-start.1 = (bf16[8,96,128]{2,1,0:T(8,128)(2,1)S(1)}, bf16[8,96,128]{2,1,0:T(8,128)(2,1)S(1)}, u32[]{:S(2)}, u32[]{:S(2)}) collective-permute-start(bf16[8,96,128]{2,1,0:T(8,128)(2,1)S(1)} %get-tuple-element.52), channel_id=1, source_target_pairs={{0,32},{8,40},{16,48},{24,56},{32,0},{40,8},{48,16},{56,24},{64,96... | collective-permute-start | bytes 589832 | tf_op jit(solution)/shard_map/ppermute | solution.py:337
  42.1 33.9 %copy-start.6 = (bf16[128,192]{1,0:T(8,128)(2,1)S(1)}, bf16[128,192]{1,0:T(8,128)(2,1)}, u32[]{:S(2)}) copy-start(bf16[128,192]{1,0:T(8,128)(2,1)} %constant.48.clone.split_ref) | copy-start | bytes 147460
  49.9 7.4 %copy-start.7 = (bf16[1,8,96,128]{3,2,1,0:T(8,128)(2,1)S(1)}, bf16[1,8,96,128]{3,2,1,0:T(8,128)(2,1)}, u32[]{:S(2)}) copy-start(bf16[1,8,96,128]{3,2,1,0:T(8,128)(2,1)} %get-tuple-element.51) | copy-start | bytes 589828
  50.0 23.6 %all-to-all-start.2 = ((bf16[128,32,128]{2,1,0:T(8,128)(2,1)}), bf16[128,32,128]{2,1,0:T(8,128)(2,1)S(1)}, u32[]{:S(2)}, u32[]{:S(2)}) async-start(bf16[128,32,128]{2,1,0:T(8,128)(2,1)} %bitcast.4), calls=%async_computation.2 | async-start | bytes 2097152 | tf_op jit(solution)/shard_map/all_to_all | solution.py:397
  55.7 17.8 %collective-permute-start.7 = (bf16[8,96,128]{2,1,0:T(8,128)(2,1)S(1)}, bf16[8,96,128]{2,1,0:T(8,128)(2,1)S(1)}, u32[]{:S(2)}, u32[]{:S(2)}) collective-permute-start(bf16[8,96,128]{2,1,0:T(8,128)(2,1)S(1)} %collective-permute-done.1.refs_3_), channel_id=1, source_target_pairs={{0,64},{8,72},{16,80},{24,88},{32,96},{40,104},{48,112},{56,120},{... | collective-permute-start | bytes 589832 | tf_op jit(solution)/shard_map/ppermute | solution.py:333
  58.3 36.2 %copy-start.9 = (s32[2,16]{1,0:T(2,128)S(1)}, s32[2,16]{1,0:T(2,128)}, u32[]{:S(2)}) copy-start(s32[2,16]{1,0:T(2,128)} %param.11) | copy-start | bytes 388
  58.3 25.2 %collective-permute-start.3 = (bf16[2,8,96,128]{3,2,1,0:T(8,128)(2,1)S(1)}, bf16[2,8,96,128]{3,2,1,0:T(8,128)(2,1)}, u32[]{:S(2)}, u32[]{:S(2)}) collective-permute-start(bf16[2,8,96,128]{3,2,1,0:T(8,128)(2,1)S(1)} %pad_maximum_fusion.refs_0_), channel_id=1, source_target_pairs={{0,48},{8,56},{16,0},{24,8},{32,16},{40,24},{48,32},{56,40},{64,11... | collective-permute-start | bytes 1179656 | tf_op jit(solution)/shard_map/ppermute | solution.py:337
  60.8 22.7 %collective-permute-start.2 = (bf16[2,8,96,128]{3,2,1,0:T(8,128)(2,1)S(1)}, bf16[2,8,96,128]{3,2,1,0:T(8,128)(2,1)}, u32[]{:S(2)}, u32[]{:S(2)}) collective-permute-start(bf16[2,8,96,128]{3,2,1,0:T(8,128)(2,1)S(1)} %pad_maximum_fusion.refs_0_), channel_id=1, source_target_pairs={{0,16},{8,24},{16,32},{24,40},{32,48},{40,56},{48,0},{56,8},{64,80... | collective-permute-start | bytes 1179656 | tf_op jit(solution)/shard_map/ppermute | solution.py:337
  60.8 22.7 %collective-permute-start.6 = (bf16[32,48,128]{2,1,0:T(8,128)(2,1)S(1)}, bf16[32,48,128]{2,1,0:T(8,128)(2,1)S(1)}, u32[]{:S(2)}, u32[]{:S(2)}) collective-permute-start(bf16[32,48,128]{2,1,0:T(8,128)(2,1)S(1)} %all-to-all-done.1.refs_0_), channel_id=1, source_target_pairs={{0,6},{1,7},{2,0},{3,1},{4,2},{5,3},{6,4},{7,5},{8,14},{9,15},{10,... | collective-permute-start | bytes 1179656 | tf_op jit(solution)/shard_map/ppermute | solution.py:344
  63.4 20.1 %collective-permute-start.4 = (bf16[32,48,128]{2,1,0:T(8,128)(2,1)S(1)}, bf16[32,48,128]{2,1,0:T(8,128)(2,1)S(1)}, u32[]{:S(2)}, u32[]{:S(2)}) collective-permute-start(bf16[32,48,128]{2,1,0:T(8,128)(2,1)S(1)} %all-to-all-done.1.refs_0_), channel_id=1, source_target_pairs={{0,2},{1,3},{2,4},{3,5},{4,6},{5,7},{6,0},{7,1},{8,10},{9,11},{10,... | collective-permute-start | bytes 1179656 | tf_op jit(solution)/shard_map/ppermute | solution.py:344
  73.5 14.0 %collective-permute-start.5 = (bf16[32,48,128]{2,1,0:T(8,128)(2,1)S(1)}, bf16[32,48,128]{2,1,0:T(8,128)(2,1)S(1)}, u32[]{:S(2)}, u32[]{:S(2)}) collective-permute-start(bf16[32,48,128]{2,1,0:T(8,128)(2,1)S(1)} %all-to-all-done.1.refs_0_), channel_id=1, source_target_pairs={{0,4},{1,5},{2,6},{3,7},{4,0},{5,1},{6,2},{7,3},{8,12},{9,13},{10,... | collective-permute-start | bytes 1179656 | tf_op jit(solution)/shard_map/ppermute | solution.py:344
  87.5 21.6 %all-to-all-start.3 = ((bf16[16,256,128]{2,1,0:T(8,128)(2,1)}), bf16[16,256,128]{2,1,0:T(8,128)(2,1)}, u32[]{:S(2)}, u32[]{:S(2)}) async-start(bf16[16,256,128]{2,1,0:T(8,128)(2,1)} %bitcast.6), calls=%async_computation.3 | async-start | bytes 2097152 | tf_op jit(solution)/shard_map/all_to_all | solution.py:410
  93.1 6.5 %collective-permute-start.8 = (bf16[2,8,96,128]{3,2,1,0:T(8,128)(2,1)S(1)}, bf16[2,8,96,128]{3,2,1,0:T(8,128)(2,1)S(1)}, u32[]{:S(2)}, u32[]{:S(2)}) collective-permute-start(bf16[2,8,96,128]{3,2,1,0:T(8,128)(2,1)S(1)} %pad_maximum_fusion.refs_0_), channel_id=1, source_target_pairs={{0,8},{8,0},{16,24},{24,16},{32,40},{40,32},{48,56},{56,48},{64,72... | collective-permute-start | bytes 1179656 | tf_op jit(solution)/shard_map/ppermute | solution.py:349
  93.4 6.3 %collective-permute-start.9 = (bf16[2,8,96,128]{3,2,1,0:T(8,128)(2,1)}, bf16[2,8,96,128]{3,2,1,0:T(8,128)(2,1)S(1)}, u32[]{:S(2)}, u32[]{:S(2)}) collective-permute-start(bf16[2,8,96,128]{3,2,1,0:T(8,128)(2,1)} %collective-permute-done.2.refs_1_), channel_id=1, source_target_pairs={{0,8},{8,0},{16,24},{24,16},{32,40},{40,32},{48,56},{56,48},{64,72... | collective-permute-start | bytes 1179656 | tf_op jit(solution)/shard_map/ppermute | solution.py:349
  93.7 6.0 %collective-permute-start.10 = (bf16[2,8,96,128]{3,2,1,0:T(8,128)(2,1)}, bf16[2,8,96,128]{3,2,1,0:T(8,128)(2,1)S(1)}, u32[]{:S(2)}, u32[]{:S(2)}) collective-permute-start(bf16[2,8,96,128]{3,2,1,0:T(8,128)(2,1)} %collective-permute-done.3.refs_2_), channel_id=1, source_target_pairs={{0,8},{8,0},{16,24},{24,16},{32,40},{40,32},{48,56},{56,48},{64,72... | collective-permute-start | bytes 1179656 | tf_op jit(solution)/shard_map/ppermute | solution.py:349
  93.9 5.7 %collective-permute-start.11 = (bf16[8,96,128]{2,1,0:T(8,128)(2,1)S(1)}, bf16[8,96,128]{2,1,0:T(8,128)(2,1)}, u32[]{:S(2)}, u32[]{:S(2)}) collective-permute-start(bf16[8,96,128]{2,1,0:T(8,128)(2,1)S(1)} %collective-permute-done.1.refs_3_), channel_id=1, source_target_pairs={{0,8},{8,0},{16,24},{24,16},{32,40},{40,32},{48,56},{56,48},{64,72... | collective-permute-start | bytes 589832 | tf_op jit(solution)/shard_map/ppermute | solution.py:349
  94.2 5.5 %collective-permute-start.12 = (bf16[8,96,128]{2,1,0:T(8,128)(2,1)S(1)}, bf16[8,96,128]{2,1,0:T(8,128)(2,1)}, u32[]{:S(2)}, u32[]{:S(2)}) collective-permute-start(bf16[8,96,128]{2,1,0:T(8,128)(2,1)S(1)} %collective-permute-done.7.refs_4_), channel_id=1, source_target_pairs={{0,8},{8,0},{16,24},{24,16},{32,40},{40,32},{48,56},{56,48},{64,72... | collective-permute-start | bytes 589832 | tf_op jit(solution)/shard_map/ppermute | solution.py:349
  96.9 2.0 %copy-start = (bf16[16,512,192]{2,1,0:T(8,128)(2,1)}, bf16[16,512,192]{2,1,0:T(8,128)(2,1)S(1)}, u32[]{:S(2)}) copy-start(bf16[16,512,192]{2,1,0:T(8,128)(2,1)S(1)} %get-tuple-element.49.turned_ref) | copy-start | bytes 9437188
  98.9 0.8 copy-start.2
  102.0 1.7 %copy-start.1 = (bf16[16,192,512]{2,1,0:T(8,128)(2,1)}, bf16[16,192,512]{2,1,0:T(8,128)(2,1)S(1)}, u32[]{:S(2)}) copy-start(bf16[16,192,512]{2,1,0:T(8,128)(2,1)S(1)} %get-tuple-element.43.row_ref) | copy-start | bytes 9437188
  103.7 0.8 copy-start.3
